TPU v7x, 32 devices: a whole 2x2x4 slice. The times are simulated.
32 devices in a mesh: row: 8 (over z, y), col: 4 (over x, core).
Axes of the slice: x: 2, y: 2, z: 4, core: 2. Of those that a mesh axis runs over, the one named last changes fastest.
Arguments:
- panel_block: float32 [16384, 128], P('row', 'col'), may hold values from -6 to 6
- trailing: float32 [16384, 2048], P('row', 'col'), may hold values from -6 to 6
Outputs:
- updated: float32 [16384, 2048], P('row', 'col')
- reflectors: float32 [16384, 128], P('row', 'col')
- panel_factor: float32 [128, 128], replicated
All inputs are finite; a program needn't handle non-finite values.
Results may differ from a plain program's by a relative error of at most 0.0003.
Values sent between devices are 32-bit elements; how exact they have to be, the bound alone decides.
No kernel may reach another device: no remote copies, remote signals or barrier semaphores. Data moves between devices by JAX's collectives and lax.ppermute only.
A program may use at most 64 MiB of HBM per device.

v0:
```python
import jax
import jax.numpy as jnp
from jax import lax
from jax.sharding import PartitionSpec as P

HIGH = lax.Precision.HIGHEST


def partner_2(x, axis, bit):
    return lax.ppermute(x, axis, [(i, i ^ 1 << bit) for i in range(lax.axis_size(axis))])


def from_root(x, axis, root):
    mine = lax.axis_index(axis) == root
    return lax.psum(jnp.where(mine, x, jnp.zeros_like(x)), axis)


def decompose(matrix):
    extent = matrix.shape[0]
    positions = jnp.arange(extent)

    def advance(column, current):
        row_pick = lax.dynamic_index_in_dim(current, column, 0, keepdims=False)
        col_pick = lax.dynamic_index_in_dim(current, column, 1, keepdims=False)
        pivot_value = lax.dynamic_index_in_dim(row_pick, column, 0, keepdims=False)
        below_mask = positions > column
        factor_col = jnp.where(below_mask, col_pick / pivot_value, jnp.float32(0.0))
        current = (
            current
            - factor_col[:, None] * jnp.where(below_mask, row_pick, jnp.float32(0.0))[None, :]
        )
        place_mask = (positions == column)[None, :] & below_mask[:, None]
        return jnp.where(place_mask, factor_col[:, None], current)

    return lax.fori_loop(0, extent, advance, matrix)


def cross_of(matrix):
    return lax.dot_general(
        matrix, matrix, (((0,), (0,)), ((), ())), precision=HIGH, preferred_element_type=jnp.float32
    )


def upper_factor(gram_part):
    return jnp.linalg.cholesky(gram_part).T


def per_device(panel_block, trailing):
    panel_rows = lax.all_gather(panel_block, "col", axis=1, tiled=True)
    rows_here = panel_rows.shape[0]
    width = panel_rows.shape[1]
    local_gram = cross_of(panel_rows)
    factor = upper_factor(local_gram)
    levels = lax.axis_size("row").bit_length() - 1
    for level in range(levels):
        partner = partner_2(factor, "row", level)
        factor = upper_factor(cross_of(factor) + cross_of(partner))
    q_trans = jax.scipy.linalg.solve_triangular(factor.T, panel_rows.T, lower=True)
    leading = from_root(q_trans[:, :width], "row", 0).T
    sign_flip = jnp.where(jnp.diag(leading) >= 0, jnp.float32(-1.0), jnp.float32(1.0))
    packed_lu = decompose(leading - jnp.diag(sign_flip))
    lower_f = jnp.tril(packed_lu, -1) + jnp.eye(width, dtype=jnp.float32)
    upper_f = jnp.triu(packed_lu)
    reflect_t = jax.scipy.linalg.solve_triangular(upper_f.T, q_trans, lower=True)
    global_rows = lax.axis_index("row") * rows_here + jnp.arange(rows_here)
    padded_lower = jnp.zeros((width, rows_here), jnp.float32).at[:, :width].set(lower_f.T)
    reflect_t = jnp.where((global_rows < width)[None, :], padded_lower, reflect_t)
    coupling_t = jax.scipy.linalg.solve_triangular(
        lower_f, -(sign_flip[:, None] * upper_f.T), lower=True, unit_diagonal=True
    )
    local_products = lax.dot_general(
        trailing,
        reflect_t,
        (((0,), (1,)), ((), ())),
        precision=HIGH,
        preferred_element_type=jnp.float32,
    )
    products = lax.psum(local_products, "row")
    mixed = lax.dot_general(
        products,
        coupling_t,
        (((1,), (1,)), ((), ())),
        precision=HIGH,
        preferred_element_type=jnp.float32,
    )
    change = lax.dot_general(
        reflect_t,
        mixed,
        (((0,), (1,)), ((), ())),
        precision=HIGH,
        preferred_element_type=jnp.float32,
    )
    updated = trailing - change
    piece = width // lax.axis_size("col")
    reflect_part = lax.dynamic_slice_in_dim(reflect_t, lax.axis_index("col") * piece, piece, 0).T
    return (updated, reflect_part, sign_flip[:, None] * factor)


def solution(mesh):
    in_specs = (P("row", "col"), P("row", "col"))
    out_specs = (P("row", "col"), P("row", "col"), P())
    return jax.shard_map(
        per_device, mesh=mesh, in_specs=in_specs, out_specs=out_specs, check_vma=False
    )
```

profile of v0, /device:TPU:0, one launch (start us, length us, event | category | flops | bytes accessed | tf_op | source)
XLA Modules:
  0.0 488.9 jit_solution(15477685854106112589)
XLA Ops:
  8.7 20.3 %all-gather.2.cloned.1.call-done = f32[2048,128]{0,1:T(8,128)} async-done(((f32[2048,32]{0,1:T(8,128)}), f32[2048,128]{0,1:T(8,128)}) %all-gather.2.cloned.1.call-update) | async-done | bytes 1048592 | tf_op jit(solution)/shard_map/all_gather | solution.py:49
  29.0 2.6 fusion.56
  31.8 11.7 %cholesky.74 = f32[128,128]{1,0:T(8,128)S(1)} custom-call(f32[128,128]{1,0:T(8,128)S(1)} %fusion.17), custom_call_target="Cholesky" | custom-call | tf_op jit(solution)/shard_map/jit(cholesky)/cholesky | solution.py:45
  44.8 1.5 collective-permute-start
  47.3 1.9 collective-permute-done
  49.5 11.7 %cholesky.85 = f32[128,128]{1,0:T(8,128)S(1)} custom-call(f32[128,128]{1,0:T(8,128)S(1)} %fusion.16), custom_call_target="Cholesky" | custom-call | tf_op jit(solution)/shard_map/jit(cholesky)/cholesky | solution.py:45
  62.6 1.6 collective-permute-start.1
  65.0 1.9 collective-permute-done.1
  67.3 11.9 %cholesky.96 = f32[128,128]{1,0:T(8,128)S(1)} custom-call(f32[128,128]{1,0:T(8,128)S(1)} %fusion.15), custom_call_target="Cholesky" | custom-call | tf_op jit(solution)/shard_map/jit(cholesky)/cholesky | solution.py:45
  80.5 2.5 collective-permute-start.2
  83.9 1.8 collective-permute-done.2
  86.1 11.7 %cholesky.107 = f32[128,128]{1,0:T(8,128)S(1)} custom-call(f32[128,128]{1,0:T(8,128)S(1)} %fusion.14), custom_call_target="Cholesky" | custom-call | tf_op jit(solution)/shard_map/jit(cholesky)/cholesky | solution.py:45
  99.2 9.8 %custom-call.13 = f32[1,128,128]{1,2,0:T(8,128)S(1)} custom-call(f32[1,128,128]{2,1,0:T(8,128)S(1)} %select_bitcast_fusion), custom_call_target="InvertDiagBlocksLowerTriangular" | custom-call | tf_op jit(solution)/shard_map/jit(_solve_triangular)/triangular_solve | solution.py:58
  109.0 1.1 fusion.4
  110.8 69.2 %all-reduce.4.cloned.1.call-done = f32[128,128]{0,1:T(8,128)} async-done(((f32[128,128]{0,1:T(8,128)}), f32[128,128]{0,1:T(8,128)}) %all-reduce.4.cloned.1.call-update) | async-done | bytes 65552 | tf_op jit(solution)/shard_map/psum | solution.py:15
  180.0 1.9 gather_fusion
  182.8 193.4 %while.19 = (s32[]{:T(128)}, f32[128,128]{0,1:T(8,128)S(1)}, s32[]{:T(128)}, s32[]{:T(128)}, s32[]{:T(128)}) while((s32[]{:T(128)}, f32[128,128]{0,1:T(8,128)S(1)}, s32[]{:T(128)}, s32[]{:T(128)}, s32[]{:T(128)}) %tuple.61), condition=%wide.region_5.8_spmd.clone.clone, body=%wide.region_4.7_spmd.clone.clone.sunk | while | flops 66435 | bytes 268381 | solution.py:35
  377.1 9.8 %custom-call.9 = f32[1,128,128]{1,2,0:T(8,128)S(1)} custom-call(f32[1,128,128]{2,1,0:T(8,128)S(1)} %add_bitcast_fusion), custom_call_target="InvertDiagBlocksLowerTriangular" | custom-call | tf_op jit(solution)/shard_map/jit(_solve_triangular)/triangular_solve | solution.py:68
  387.3 9.8 %custom-call.14 = f32[1,128,128]{1,2,0:T(8,128)S(1)} custom-call(f32[1,128,128]{2,1,0:T(8,128)S(1)} %copy.41), custom_call_target="InvertDiagBlocksLowerTriangular" | custom-call | tf_op jit(solution)/shard_map/jit(_solve_triangular)/triangular_solve | solution.py:64
  397.1 1.1 convolution_select_fusion
  398.2 5.3 %convolution_bitcast_fusion = f32[512,128]{0,1:T(8,128)} fusion(f32[128,2048]{1,0:T(8,128)S(1)} %convolution_select_fusion, f32[2048,512]{1,0:T(8,128)} %param.10), kind=kOutput, calls=%fused_computation.11 | convolution fusion | flops 1610612736 | bytes 5505024 | tf_op jit(solution)/shard_map/dot_general | solution.py:71
  405.7 68.5 %all-reduce.6.cloned.1.call-done = f32[512,128]{0,1:T(8,128)} async-done(((f32[512,128]{0,1:T(8,128)}), f32[512,128]{0,1:T(8,128)}) %all-reduce.6.cloned.1.call-update) | async-done | bytes 262160 | tf_op jit(solution)/shard_map/psum | solution.py:78
  474.2 1.5 fusion.57
  475.8 6.6 %convolution_subtract_fusion = f32[2048,512]{1,0:T(8,128)} fusion(f32[2048,512]{1,0:T(8,128)} %param.10, f32[128,2048]{1,0:T(8,128)S(1)} %convolution_select_fusion, f32[512,128]{1,0:T(8,128)S(1)} %fusion.57), kind=kOutput, calls=%fused_computation.9 | convolution fusion | flops 1611661312 | bytes 9699328 | tf_op jit(solution)/shard_map/dot_general | solution.py:86
  (821 shorter events, 202.1 us)
Async XLA Ops:
  7.2 21.8 %all-gather.2.cloned.1.call-start = ((), (), s32[]{:S(2)}) async-start(), calls=%async_computation | async-start | bytes 1310720 | tf_op jit(solution)/shard_map/all_gather | solution.py:49
  7.9 172.1 %all-reduce.4.cloned.1.call-start = ((), (), s32[]{:S(2)}) async-start(), calls=%async_computation.1 | async-start | bytes 131072 | tf_op jit(solution)/shard_map/psum | solution.py:15
  29.0 80.0 %copy-start = (f32[2048,128]{0,1:T(8,128)S(1)}, f32[2048,128]{0,1:T(8,128)}, u32[]{:S(2)}) copy-start(f32[2048,128]{0,1:T(8,128)} %all-gather.2.cloned.1.call-done) | copy-start | bytes 3145732
  44.8 4.3 collective-permute-start
  62.6 4.3 collective-permute-start.1
  80.5 5.2 %collective-permute-start.2 = (f32[128,128]{0,1:T(8,128)S(1)}, f32[128,128]{0,1:T(8,128)S(1)}, u32[]{:S(2)}, u32[]{:S(2)}) collective-permute-start(f32[128,128]{0,1:T(8,128)S(1)} %fusion.28), channel_id=1, source_target_pairs={{0,16},{4,20},{8,24},{12,28},{16,0},{20,4},{24,8},{28,12},{1,17},{... | collective-permute-start | bytes 196616 | tf_op jit(solution)/shard_map/ppermute | solution.py:10
  110.7 363.5 %all-reduce.6.cloned.1.call-start = ((), (), s32[]{:S(2)}) async-start(), calls=%async_computation.2 | async-start | bytes 524288 | tf_op jit(solution)/shard_map/psum | solution.py:78
Sparse Core Ops, SparseCore 0:
  9.6 19.4 all-gather.1
  110.9 69.1 all-reduce.3
  403.7 70.4 all-reduce.5
where the time goes:
time: 490 us; the launch traced here: 489 us
  other arithmetic  185 us (38%)
  waiting for transfers between devices  164 us (33%)
  local copies, waits for them, and re-layouts  90.7 us (19%)
  matrix products  22 us (4%)
  between operations  14 us (3%)
  loops' own time  7.02 us (1%)
  starting transfers between devices  5.68 us (1%)
    broadcast_in_dim x128, other arithmetic, advance(): return jnp.where(place_mask, factor_col[:, None], current)  83.7 us
    dynamic_slice x128, local copies, waits for them, and re-layouts, advance(): pivot_value = lax.dynamic_index_in_dim(row_pick, column, 0, keepdims=False)  75.3 us
    psum x1, waiting for transfers between devices, from_root(): return lax.psum(jnp.where(mine, x, jnp.zeros_like(x)), axis)  69.2 us
    psum x1, waiting for transfers between devices, per_device(): products = lax.psum(local_products, 'row')  68.5 us
    another operation x12, other arithmetic, upper_factor(): return jnp.linalg.cholesky(gram_part).T  49.7 us
    all_gather x1, waiting for transfers between devices, per_device(): panel_rows = lax.all_gather(panel_block, 'col', axis=1, tiled=True)  20.3 us
    select_n x128, other arithmetic, advance(): return jnp.where(place_mask, factor_col[:, None], current)  13.6 us
    while x128, local copies, waits for them, and re-layouts  11.3 us
  transfers between devices with their start and end apart: 6, of which 6 were waited for; matrix products, arithmetic and copies ran while one was open for 1% of the time, Pallas kernels for 0%

commit v1 on v0

v1 whole, which is shorter than its diff:
```python
import jax
import jax.numpy as jnp
from jax import lax
from jax.experimental import pallas as pl
from jax.experimental.pallas import tpu as pltpu
from jax.sharding import PartitionSpec as P

SUB = 8


def factor_kernel(gram_ref, lead_t_ref, panel_factor_ref, weight_ref, inv_ref, pivot_ref, lead_ref, g, z, d, e, lead):
    n = gram_ref.shape[0]
    slabs = n // SUB
    sub = lax.broadcasted_iota(jnp.int32, (SUB, n), 0)
    lane = lax.broadcasted_iota(jnp.int32, (SUB, n), 1)

    def rows(s):
        return pl.ds(s * SUB, SUB)

    def spread(block, j):
        return jnp.broadcast_to(block[j : j + 1, :], block.shape)

    def column(block, k):
        return jnp.broadcast_to(block[:, k : k + 1], block.shape)

    g[...] = gram_ref[...]
    d[...] = lead_t_ref[...]
    lead[...] = lead_t_ref[...].T
    for s in range(slabs):
        unit = jnp.where(sub + s * SUB == lane, 1.0, 0.0).astype(jnp.float32)
        z[rows(s), :] = unit
        e[rows(s), :] = unit

    def reduce_slab(s, left, right):
        x, y = left[rows(s), :], right[rows(s), :]
        cols = [column(x, s * SUB + j) for j in range(SUB)]
        x_at, y_at, pivots = x, y, cols[0]
        for j in range(SUB):
            here = sub == j
            pivot = spread(cols[j], j)
            inv = 1.0 / pivot
            if j > 0:
                x_at, y_at = jnp.where(here, x, x_at), jnp.where(here, y, y_at)
            pivots = jnp.where(here, pivot, pivots)
            mult = cols[j]
            xj, yj = spread(x, j) * inv, spread(y, j) * inv
            for c in range(j + 1, SUB):
                cj = spread(cols[c], j) * inv
                cols[c] = jnp.where(here, cj, cols[c] - mult * cj)
            x = jnp.where(here, xj, x - mult * xj)
            y = jnp.where(here, yj, y - mult * yj)
        return x, y, x_at, y_at, pivots

    def eliminate(s, t, left, right, xs, ys):
        x, y = left[rows(t), :], right[rows(t), :]
        cols = [column(x, s * SUB + j) for j in range(SUB)]
        for j in range(SUB):
            x = x - cols[j] * xs[j]
            y = y - cols[j] * ys[j]
        left[rows(t), :] = x
        right[rows(t), :] = y

    def cholesky(s):
        x, y, x_at, y_at, pivots = reduce_slab(s, g, z)
        scale = lax.rsqrt(pivots)
        xs = [spread(x, j) for j in range(SUB)]
        ys = [spread(y, j) for j in range(SUB)]
        for t in range(s + 1, slabs):
            eliminate(s, t, g, z, xs, ys)
        r = jnp.where(lane >= sub + s * SUB, x_at * scale, 0.0)
        r_inv_t = y_at * scale
        diagonal = jnp.sum(lead[rows(s), :] * r_inv_t, axis=1, keepdims=True)
        sign = jnp.broadcast_to(jnp.where(diagonal >= 0, -1.0, 1.0).astype(jnp.float32), (SUB, n))
        signed = sign * r
        panel_factor_ref[rows(s), :] = signed
        weight_ref[rows(s), :] = sign * r_inv_t
        turned = jnp.concatenate([signed, jnp.zeros((n - SUB, n), jnp.float32)], axis=0).T
        for t in range(s, slabs):
            part = turned[t * SUB : (t + 1) * SUB, :]
            if s:
                part = pltpu.roll(part, s * SUB, 1)
            d[rows(t), :] = d[rows(t), :] - part

    def lower_upper(s):
        x, y, _, y_at, pivots = reduce_slab(s, d, e)
        pivot_ref[rows(s), :] = y_at / pivots
        d[rows(s), :] = x
        e[rows(s), :] = y
        xs = [spread(x, j) for j in range(SUB)]
        ys = [spread(y, j) for j in range(SUB)]
        for t in list(range(s + 1, slabs)) + list(range(s)):
            eliminate(s, t, d, e, xs, ys)

    for s in range(slabs):
        cholesky(s)
        if s:
            lower_upper(s - 1)
    lower_upper(slabs - 1)
    inv_ref[...] = e[...]
    lead_ref[...] = lead_t_ref[...] - panel_factor_ref[...].T


def factor(gram, lead_t):
    n = gram.shape[0]
    out = jax.ShapeDtypeStruct((n, n), jnp.float32)
    return pl.pallas_call(
        factor_kernel,
        out_shape=(out,) * 5,
        scratch_shapes=[pltpu.VMEM((n, n), jnp.float32)] * 5,
        name="factor",
    )(gram, lead_t)


def swap(x, axis, mask):
    return lax.ppermute(x, axis, [(i, i ^ mask) for i in range(lax.axis_size(axis))])


def bits_of(axis):
    return [1 << b for b in range(lax.axis_size(axis).bit_length() - 1)]


def total(x, axis):
    for bit in bits_of(axis):
        x = x + swap(x, axis, bit)
    return x


def from_first(x, axis):
    size, me = lax.axis_size(axis), lax.axis_index(axis)
    for bit in reversed(bits_of(axis)):
        got = lax.ppermute(x, axis, [(i, i + bit) for i in range(0, size, 2 * bit)])
        x = jnp.where(me & bit != 0, got, x)
    return x


def gram_kernel(masks, me_ref, *refs):
    pieces, panel_t, gram = refs[: len(masks)], refs[-2], refs[-1]
    width = pieces[0].shape[0]
    for mask, piece in zip(masks, pieces):
        at = pl.multiple_of((me_ref[0] ^ mask) * width, width)
        panel_t[pl.ds(at, width), :] = piece[...]
    whole = panel_t[...]
    gram[...] = lax.dot_general(
        whole,
        whole,
        (((1,), (1,)), ((), ())),
        precision=lax.Precision.HIGHEST,
        preferred_element_type=jnp.float32,
    )


def gathered(own):
    held = {0: own}
    for bit in reversed(bits_of("col")):
        held.update({mask | bit: swap(piece, "col", bit) for mask, piece in list(held.items())})
    masks = tuple(held)
    width, rows = own.shape
    n = width * len(masks)
    me = lax.axis_index("col").astype(jnp.int32).reshape(1)
    return pl.pallas_call(
        lambda *refs: gram_kernel(masks, *refs),
        out_shape=(
            jax.ShapeDtypeStruct((n, rows), jnp.float32),
            jax.ShapeDtypeStruct((n, n), jnp.float32),
        ),
        in_specs=[pl.BlockSpec(memory_space=pltpu.SMEM)]
        + [pl.BlockSpec(memory_space=pltpu.VMEM)] * len(masks),
        name="gram",
    )(me, *held.values())


def dot(a, b, over, precision):
    return lax.dot_general(
        a, b, (((over[0],), (over[1],)), ((), ())), precision=precision, preferred_element_type=jnp.float32
    )


HIGHEST, HIGH = lax.Precision.HIGHEST, lax.Precision.HIGH


def per_device(panel_block, trailing):
    own = panel_block.T
    panel_t, gram_here = gathered(own)
    n = panel_t.shape[0]
    gram = total(gram_here, "row")
    lead_t = from_first(panel_t[:, :n], "row")
    lead_trailing = from_first(trailing[:n], "row")
    products = total(dot(panel_t, trailing, (1, 0), HIGH), "row")
    panel_factor, weight, inv_t, pivot_t, replaced = factor(gram, lead_t)
    rest = lead_trailing - dot(weight, products, (1, 0), HIGHEST)
    mixed = dot(inv_t, rest, (0, 0), HIGHEST)
    first = lax.axis_index("row") == 0
    panel_t = panel_t.at[:, :n].set(jnp.where(first, replaced, panel_t[:, :n]))
    updated = trailing - dot(panel_t, mixed, (0, 0), HIGH)
    width = own.shape[0]
    pivot_part = lax.dynamic_slice_in_dim(pivot_t, lax.axis_index("col") * width, width, 0)
    reflectors = dot(pivot_part, panel_t, (1, 0), HIGH)
    return updated, reflectors.T, panel_factor


def solution(mesh):
    in_specs = (P("row", "col"), P("row", "col"))
    out_specs = (P("row", "col"), P("row", "col"), P())
    return jax.shard_map(per_device, mesh=mesh, in_specs=in_specs, out_specs=out_specs, check_vma=False)
```

time: 490 us -> 77.3 us (0.16)
  other arithmetic: 185 us -> 4.65 us
  waiting for transfers between devices: 164 us -> 20.2 us
  local copies, waits for them, and re-layouts: 90.7 us -> 2.77 us
  Pallas kernels: 0 us -> 15.3 us
  starting transfers between devices: 5.68 us -> 20.8 us
  between operations: 14 us -> 0.89 us
  matrix products: 22 us -> 12.1 us
  loops' own time: 7.02 us -> 0 us
    psum x2 -> x0, waiting for transfers between devices: 138 us -> none  [the longest x1 69.2 us: from_root(): return lax.psum(jnp.where(mine, x, jnp.zeros_like(x)), axis)]
    broadcast_in_dim x128 -> x0, other arithmetic: 83.7 us -> none  [advance(): return jnp.where(place_mask, factor_col[:, None], current)]
    another operation x20 -> x1, other arithmetic: 81.2 us -> 0.7 us  [the longest x12 49.7 us: upper_factor(): return jnp.linalg.cholesky(gram_part).T]
    dynamic_slice x128 -> x0, local copies, waits for them, and re-layouts: 75.3 us -> none  [advance(): pivot_value = lax.dynamic_index_in_dim(row_pick, column, 0, keepdims=False)]
    all_gather x1 -> x0, waiting for transfers between devices: 20.3 us -> none  [per_device(): panel_rows = lax.all_gather(panel_block, 'col', axis=1, tiled=True)]
    pallas_call x0 -> x2, Pallas kernels: none -> 15.3 us  [the longest x1 12.4 us: factor(): pl.pallas_call(factor_kernel, out_shape=(out,) * 5, scratch_shapes=[pltpu...]
    ppermute x3 -> x15, starting transfers between devices: 5.56 us -> 20.8 us  [the longest x6 11.4 us: from_first(): got = lax.ppermute(x, axis, [(i, i + bit) for i in range(0, size, 2 * bit)])]
    ppermute x3 -> x15, waiting for transfers between devices: 5.6 us -> 20.2 us  [the longest x9 20.2 us: swap(): lax.ppermute(x, axis, [(i, i ^ mask) for i in range(lax.axis_size(axis))])]
  transfers between devices with their start and end apart: 6 -> 15, of which waited for: 6 -> 4; matrix products, arithmetic and copies ran while one was open for 1% -> 18% of each run, Pallas kernels for 0% -> 20%
where the time goes in v1:
time: 77.3 us; the launch traced here: 76.7 us
  starting transfers between devices  20.8 us (27%)
  waiting for transfers between devices  20.2 us (26%)
  Pallas kernels  15.3 us (20%)
  matrix products  12.1 us (16%)
  other arithmetic  4.65 us (6%)
  local copies, waits for them, and re-layouts  2.77 us (4%)
  between operations  0.89 us (1%)
    ppermute x9, waiting for transfers between devices, swap(): lax.ppermute(x, axis, [(i, i ^ mask) for i in range(lax.axis_size(axis))])  20.2 us
    pallas_call x1, Pallas kernels, factor(): pl.pallas_call(factor_kernel, out_shape=(out,) * 5, scratch_shapes=[pltpu...  12.4 us
    dot_general x5, matrix products, dot(): lax.dot_general(a, b, (((over[0],), (over[1],)), ((), ())), precision=pre...  12.1 us
    ppermute x6, starting transfers between devices, from_first(): got = lax.ppermute(x, axis, [(i, i + bit) for i in range(0, size, 2 * bit)])  11.4 us
    ppermute x9, starting transfers between devices, swap(): lax.ppermute(x, axis, [(i, i ^ mask) for i in range(lax.axis_size(axis))])  9.41 us
    pallas_call x1, Pallas kernels, gathered(): pl.pallas_call(lambda *refs: gram_kernel(masks, *refs), out_shape=(jax.Sh...  2.91 us
    select_n x5, other arithmetic, from_first(): x = jnp.where(me & bit != 0, got, x)  1.69 us
  transfers between devices with their start and end apart: 15, of which 4 were waited for; matrix products, arithmetic and copies ran while one was open for 18% of the time, Pallas kernels for 20%

profile of v1, /device:TPU:0, one launch (start us, length us, event | category | flops | bytes accessed | tf_op | source)
XLA Modules:
  0.0 76.7 jit_solution(15607480693534237627)
XLA Ops:
  0.6 3.0 %collective-permute-start = (f32[32,2048]{1,0:T(8,128)}, f32[32,2048]{1,0:T(8,128)S(1)}, u32[]{:S(2)}, u32[]{:S(2)}) collective-permute-start(f32[32,2048]{1,0:T(8,128)} %bitcast.9), channel_id=1, source_target_pairs={{0,2},{1,3},{2,0},{3,1},{4,6},{5,7},{6,4},{7,5},{8,10},{9,11},{10,... | collective-permute-start | bytes 786440 | tf_op jit(solution)/shard_map/ppermute | solution.py:115
  3.6 6.5 %collective-permute-done.refs_2_ = f32[32,2048]{1,0:T(8,128)S(1)} collective-permute-done((f32[32,2048]{1,0:T(8,128)}, f32[32,2048]{1,0:T(8,128)S(1)}, u32[]{:S(2)}, u32[]{:S(2)}) %collective-permute-start) | collective-permute-done | bytes 262176 | tf_op jit(solution)/shard_map/ppermute | solution.py:115
  10.2 1.1 %slice.25 = f32[128,512]{1,0:T(8,128)S(1)} slice(f32[2048,512]{1,0:T(8,128)} %param.5), slice={[0:128], [0:512]} | slice | bytes 524288 | tf_op jit(solution)/shard_map/slice | solution.py:187
  11.2 4.8 %collective-permute-start.9 = (f32[128,512]{1,0:T(8,128)S(1)}, f32[128,512]{1,0:T(8,128)S(1)}, u32[]{:S(2)}, u32[]{:S(2)}) collective-permute-start(f32[128,512]{1,0:T(8,128)S(1)} %slice.25), channel_id=1, source_target_pairs={{0,16},{1,17},{2,18},{3,19}} | collective-permute-start | bytes 786440 | tf_op jit(solution)/shard_map/ppermute | solution.py:131
  16.8 2.9 %gram.1 = (f32[128,2048]{1,0:T(8,128)}, f32[128,128]{1,0:T(8,128)}) custom-call(s32[1]{0:T(128)} %bitcast.refs_0_, f32[32,2048]{1,0:T(8,128)} %bitcast.11, f32[32,2048]{1,0:T(8,128)} %copy-done.2, f32[32,2048]{1,0:T(8,128)} %copy-done.3, f32[32,2048]{1,0:T(8,128)} %copy-done.4), custom_call_target="tpu_custom_call" | custom-call | tf_op jit(solution)/shard_map/gram/pallas_call | solution.py:160
  20.7 1.3 %collective-permute-start.6 = (f32[128,128]{1,0:T(8,128)S(1)}, f32[128,128]{1,0:T(8,128)S(1)}, u32[]{:S(2)}, u32[]{:S(2)}) collective-permute-start(f32[128,128]{1,0:T(8,128)S(1)} %slice.24), channel_id=1, source_target_pairs={{0,16},{1,17},{2,18},{3,19}} | collective-permute-start | bytes 196616 | tf_op jit(solution)/shard_map/ppermute | solution.py:131
  21.9 3.8 %fusion.10 = f32[128,512]{1,0:T(8,128)S(1)} fusion(f32[128,2048]{1,0:T(8,128)} %get-tuple-element.22, f32[2048,512]{1,0:T(8,128)} %param.5), kind=kOutput, calls=%fused_computation.18 | convolution fusion | flops 805306368 | bytes 5505024 | tf_op jit(solution)/shard_map/dot_general | solution.py:173
  25.8 2.0 %collective-permute-start.12 = (f32[128,512]{1,0:T(8,128)S(1)}, f32[128,512]{1,0:T(8,128)S(1)}, u32[]{:S(2)}, u32[]{:S(2)}) collective-permute-start(f32[128,512]{1,0:T(8,128)S(1)} %fusion.10), channel_id=1, source_target_pairs={{0,4},{4,0},{8,12},{12,8},{16,20},{20,16},{24,28},{28,24},{1,5},{5... | collective-permute-start | bytes 786440 | tf_op jit(solution)/shard_map/ppermute | solution.py:115
  27.9 1.3 %collective-permute-start.7 = (f32[128,128]{1,0:T(8,128)S(1)}, f32[128,128]{1,0:T(8,128)S(1)}, u32[]{:S(2)}, u32[]{:S(2)}) collective-permute-start(f32[128,128]{1,0:T(8,128)S(1)} %broadcast_select_fusion.2), channel_id=1, source_target_pairs={{0,8},{16,24},{1,9},{17,25},{2,10},{18,26},{3,11},{19,27}} | collective-permute-start | bytes 196616 | tf_op jit(solution)/shard_map/ppermute | solution.py:131
  29.2 1.0 %broadcast_select_fusion = f32[128,512]{1,0:T(8,128)S(1)} fusion(f32[128,512]{1,0:T(8,128)S(1)} %collective-permute-done.9, pred[]{:T(512)S(6)} %ne.14, f32[2048,512]{1,0:T(8,128)} %param.5), kind=kLoop, calls=%fused_computation.6 | loop fusion | flops 65536 | bytes 786433 | tf_op jit(solution)/shard_map/jit(_where)/select_n | solution.py:132
  30.2 1.3 %collective-permute-start.10 = (f32[128,512]{1,0:T(8,128)S(1)}, f32[128,512]{1,0:T(8,128)S(1)}, u32[]{:S(2)}, u32[]{:S(2)}) collective-permute-start(f32[128,512]{1,0:T(8,128)S(1)} %broadcast_select_fusion), channel_id=1, source_target_pairs={{0,8},{16,24},{1,9},{17,25},{2,10},{18,26},{3,11},{19,27}} | collective-permute-start | bytes 786440 | tf_op jit(solution)/shard_map/ppermute | solution.py:131
  32.3 1.3 %collective-permute-start.8 = (f32[128,128]{1,0:T(8,128)S(1)}, f32[128,128]{1,0:T(8,128)S(1)}, u32[]{:S(2)}, u32[]{:S(2)}) collective-permute-start(f32[128,128]{1,0:T(8,128)S(1)} %broadcast_select_fusion.3), channel_id=1, source_target_pairs={{0,4},{8,12},{16,20},{24,28},{1,5},{9,13},{17,21},{25,29},{2,6},{1... | collective-permute-start | bytes 196616 | tf_op jit(solution)/shard_map/ppermute | solution.py:131
  33.6 5.3 %collective-permute-done.4 = f32[128,128]{1,0:T(8,128)S(1)} collective-permute-done((f32[128,128]{1,0:T(8,128)S(1)}, f32[128,128]{1,0:T(8,128)S(1)}, u32[]{:S(2)}, u32[]{:S(2)}) %collective-permute-start.4) | collective-permute-done | bytes 65568 | tf_op jit(solution)/shard_map/ppermute | solution.py:115
  39.0 2.5 %collective-permute-start.13 = (f32[128,512]{1,0:T(8,128)S(1)}, f32[128,512]{1,0:T(8,128)S(1)}, u32[]{:S(2)}, u32[]{:S(2)}) collective-permute-start(f32[128,512]{1,0:T(8,128)S(1)} %add.26), channel_id=1, source_target_pairs={{0,8},{4,12},{8,0},{12,4},{16,24},{20,28},{24,16},{28,20},{1,9},{5... | collective-permute-start | bytes 786440 | tf_op jit(solution)/shard_map/ppermute | solution.py:115
  41.6 1.5 %collective-permute-start.11 = (f32[128,512]{1,0:T(8,128)S(1)}, f32[128,512]{1,0:T(8,128)S(1)}, u32[]{:S(2)}, u32[]{:S(2)}) collective-permute-start(f32[128,512]{1,0:T(8,128)S(1)} %broadcast_select_fusion.1), channel_id=1, source_target_pairs={{0,4},{8,12},{16,20},{24,28},{1,5},{9,13},{17,21},{25,29},{2,6},{1... | collective-permute-start | bytes 786440 | tf_op jit(solution)/shard_map/ppermute | solution.py:131
  43.1 1.3 %collective-permute-done.5 = f32[128,128]{1,0:T(8,128)S(1)} collective-permute-done((f32[128,128]{1,0:T(8,128)S(1)}, f32[128,128]{1,0:T(8,128)S(1)}, u32[]{:S(2)}, u32[]{:S(2)}) %collective-permute-start.5) | collective-permute-done | bytes 65568 | tf_op jit(solution)/shard_map/ppermute | solution.py:115
  45.7 12.4 %factor.1 = (f32[128,128]{1,0:T(8,128)}, f32[128,128]{1,0:T(8,128)}, f32[128,128]{1,0:T(8,128)}, f32[128,128]{1,0:T(8,128)}, f32[128,128]{1,0:T(8,128)}) custom-call(f32[128,128]{1,0:T(8,128)} %add.25.gram_ref, f32[128,128]{1,0:T(8,128)} %broadcast_select_fusion.4.lead_t_ref), custom_call_target="tpu_custom_call" | custom-call | tf_op jit(solution)/shard_map/factor/pallas_call | solution.py:106
  58.2 1.6 %collective-permute-start.14 = (f32[128,512]{1,0:T(8,128)S(1)}, f32[128,512]{1,0:T(8,128)S(1)}, u32[]{:S(2)}, u32[]{:S(2)}) collective-permute-start(f32[128,512]{1,0:T(8,128)S(1)} %add.27), channel_id=1, source_target_pairs={{0,16},{4,20},{8,24},{12,28},{16,0},{20,4},{24,8},{28,12},{1,17},{... | collective-permute-start | bytes 786440 | tf_op jit(solution)/shard_map/ppermute | solution.py:115
  59.8 1.5 %fusion.6 = f32[128,2048]{1,0:T(8,128)S(1)} fusion(f32[128,2048]{1,0:T(8,128)S(1)} %copy-done.1, f32[128,128]{1,0:T(8,128)} %get-tuple-element.24, pred[]{:T(512)S(6)} %eq.3, pred[]{:T(512)} %compare_reduce_fusion), kind=kLoop, calls=%fused_computation.10 | loop fusion | flops 32768 | bytes 196610 | tf_op jit(solution)/shard_map/scatter | solution.py:193
  61.3 1.8 %fusion.7 = f32[2048,32]{0,1:T(8,128)} fusion(f32[128,2048]{1,0:T(8,128)S(1)} %fusion.6, f32[128,128]{1,0:T(8,128)} %get-tuple-element.27, s32[]{:T(128)S(6)} %select_n.63), kind=kOutput, calls=%fused_computation.14 | convolution fusion | flops 50331648 | bytes 1327108 | tf_op jit(solution)/shard_map/dot_general | solution.py:173
  63.1 7.0 %collective-permute-done.14 = f32[128,512]{1,0:T(8,128)S(1)} collective-permute-done((f32[128,512]{1,0:T(8,128)S(1)}, f32[128,512]{1,0:T(8,128)S(1)}, u32[]{:S(2)}, u32[]{:S(2)}) %collective-permute-start.14) | collective-permute-done | bytes 262176 | tf_op jit(solution)/shard_map/ppermute | solution.py:115
  70.2 1.2 %fusion.2 = f32[128,512]{1,0:T(8,128)S(1)} fusion(f32[128,128]{1,0:T(8,128)} %get-tuple-element.26, f32[128,512]{1,0:T(8,128)S(1)} %add.27, f32[128,512]{1,0:T(8,128)S(1)} %collective-permute-done.14), kind=kOutput, calls=%fused_computation.3 | convolution fusion | flops 100728832 | bytes 851968 | tf_op jit(solution)/shard_map/dot_general | solution.py:173
  71.4 1.3 %fusion = f32[128,512]{1,0:T(8,128)S(1)} fusion(f32[128,128]{1,0:T(8,128)} %get-tuple-element.25, f32[128,512]{1,0:T(8,128)S(1)} %fusion.2, f32[128,512]{1,0:T(8,128)S(1)} %collective-permute-done.11, f32[128,512]{1,0:T(8,128)S(1)} %broadcast_select_fusion.1, pred[]{:T(512)S(6)} %ne.12), kind=kOutput, calls=%fused_computation.1 | convolution fusion | flops 100794368 | bytes 1114113 | tf_op jit(solution)/shard_map/dot_general | solution.py:173
  72.7 4.0 %convolution_subtract_fusion = f32[2048,512]{1,0:T(8,128)} fusion(f32[2048,512]{1,0:T(8,128)S(1)} %copy-done, f32[128,2048]{1,0:T(8,128)S(1)} %fusion.6, f32[128,512]{1,0:T(8,128)S(1)} %fusion), kind=kOutput, calls=%fused_computation | convolution fusion | flops 806354944 | bytes 9699328 | tf_op jit(solution)/shard_map/dot_general | solution.py:173
  (39 shorter events, 4.1 us)
Async XLA Ops:
  0.6 9.5 %collective-permute-start = (f32[32,2048]{1,0:T(8,128)}, f32[32,2048]{1,0:T(8,128)S(1)}, u32[]{:S(2)}, u32[]{:S(2)}) collective-permute-start(f32[32,2048]{1,0:T(8,128)} %bitcast.9), channel_id=1, source_target_pairs={{0,2},{1,3},{2,0},{3,1},{4,6},{5,7},{6,4},{7,5},{8,10},{9,11},{10,... | collective-permute-start | bytes 786440 | tf_op jit(solution)/shard_map/ppermute | solution.py:115
  3.6 12.4 %collective-permute-start.1 = (f32[32,2048]{1,0:T(8,128)}, f32[32,2048]{1,0:T(8,128)S(1)}, u32[]{:S(2)}, u32[]{:S(2)}) collective-permute-start(f32[32,2048]{1,0:T(8,128)} %bitcast.10), channel_id=1, source_target_pairs={{0,1},{1,0},{2,3},{3,2},{4,5},{5,4},{6,7},{7,6},{8,9},{9,8},{10,11... | collective-permute-start | bytes 786440 | tf_op jit(solution)/shard_map/ppermute | solution.py:115
  10.2 5.9 %copy-start.2 = (f32[32,2048]{1,0:T(8,128)}, f32[32,2048]{1,0:T(8,128)S(1)}, u32[]{:S(2)}) copy-start(f32[32,2048]{1,0:T(8,128)S(1)} %collective-permute-done.refs_2_) | copy-start | bytes 786436
  10.2 5.9 %collective-permute-start.2 = (f32[32,2048]{1,0:T(8,128)S(1)}, f32[32,2048]{1,0:T(8,128)S(1)}, u32[]{:S(2)}, u32[]{:S(2)}) collective-permute-start(f32[32,2048]{1,0:T(8,128)S(1)} %collective-permute-done.refs_2_), channel_id=1, source_target_pairs={{0,1},{1,0},{2,3},{3,2},{4,5},{5,4},{6,7},{7,6},{8,9},{9,8},{10,11... | collective-permute-start | bytes 786440 | tf_op jit(solution)/shard_map/ppermute | solution.py:115
  11.2 18.0 %collective-permute-start.9 = (f32[128,512]{1,0:T(8,128)S(1)}, f32[128,512]{1,0:T(8,128)S(1)}, u32[]{:S(2)}, u32[]{:S(2)}) collective-permute-start(f32[128,512]{1,0:T(8,128)S(1)} %slice.25), channel_id=1, source_target_pairs={{0,16},{1,17},{2,18},{3,19}} | collective-permute-start | bytes 786440 | tf_op jit(solution)/shard_map/ppermute | solution.py:131
  16.0 0.7 copy-start.3
  16.0 0.8 %copy-start.4 = (f32[32,2048]{1,0:T(8,128)}, f32[32,2048]{1,0:T(8,128)S(1)}, u32[]{:S(2)}) copy-start(f32[32,2048]{1,0:T(8,128)S(1)} %collective-permute-done.2.refs_4_) | copy-start | bytes 786436
  19.7 6.0 %copy-start.5 = (f32[128,128]{1,0:T(8,128)S(1)}, f32[128,128]{1,0:T(8,128)}, u32[]{:S(2)}) copy-start(f32[128,128]{1,0:T(8,128)} %get-tuple-element.23) | copy-start | bytes 196612
  19.7 8.1 %copy-start.1 = (f32[128,2048]{1,0:T(8,128)S(1)}, f32[128,2048]{1,0:T(8,128)}, u32[]{:S(2)}) copy-start(f32[128,2048]{1,0:T(8,128)} %get-tuple-element.22) | copy-start | bytes 3145732
  20.7 7.2 %collective-permute-start.6 = (f32[128,128]{1,0:T(8,128)S(1)}, f32[128,128]{1,0:T(8,128)S(1)}, u32[]{:S(2)}, u32[]{:S(2)}) collective-permute-start(f32[128,128]{1,0:T(8,128)S(1)} %slice.24), channel_id=1, source_target_pairs={{0,16},{1,17},{2,18},{3,19}} | collective-permute-start | bytes 196616 | tf_op jit(solution)/shard_map/ppermute | solution.py:131
  25.8 6.4 %collective-permute-start.3 = (f32[128,128]{1,0:T(8,128)S(1)}, f32[128,128]{1,0:T(8,128)S(1)}, u32[]{:S(2)}, u32[]{:S(2)}) collective-permute-start(f32[128,128]{1,0:T(8,128)S(1)} %copy-done.5), channel_id=1, source_target_pairs={{0,4},{4,0},{8,12},{12,8},{16,20},{20,16},{24,28},{28,24},{1,5},{5... | collective-permute-start | bytes 196616 | tf_op jit(solution)/shard_map/ppermute | solution.py:115
  25.8 13.1 %collective-permute-start.12 = (f32[128,512]{1,0:T(8,128)S(1)}, f32[128,512]{1,0:T(8,128)S(1)}, u32[]{:S(2)}, u32[]{:S(2)}) collective-permute-start(f32[128,512]{1,0:T(8,128)S(1)} %fusion.10), channel_id=1, source_target_pairs={{0,4},{4,0},{8,12},{12,8},{16,20},{20,16},{24,28},{28,24},{1,5},{5... | collective-permute-start | bytes 786440 | tf_op jit(solution)/shard_map/ppermute | solution.py:115
  27.9 4.4 %collective-permute-start.7 = (f32[128,128]{1,0:T(8,128)S(1)}, f32[128,128]{1,0:T(8,128)S(1)}, u32[]{:S(2)}, u32[]{:S(2)}) collective-permute-start(f32[128,128]{1,0:T(8,128)S(1)} %broadcast_select_fusion.2), channel_id=1, source_target_pairs={{0,8},{16,24},{1,9},{17,25},{2,10},{18,26},{3,11},{19,27}} | collective-permute-start | bytes 196616 | tf_op jit(solution)/shard_map/ppermute | solution.py:131
  30.2 11.4 %collective-permute-start.10 = (f32[128,512]{1,0:T(8,128)S(1)}, f32[128,512]{1,0:T(8,128)S(1)}, u32[]{:S(2)}, u32[]{:S(2)}) collective-permute-start(f32[128,512]{1,0:T(8,128)S(1)} %broadcast_select_fusion), channel_id=1, source_target_pairs={{0,8},{16,24},{1,9},{17,25},{2,10},{18,26},{3,11},{19,27}} | collective-permute-start | bytes 786440 | tf_op jit(solution)/shard_map/ppermute | solution.py:131
  32.2 6.7 %collective-permute-start.4 = (f32[128,128]{1,0:T(8,128)S(1)}, f32[128,128]{1,0:T(8,128)S(1)}, u32[]{:S(2)}, u32[]{:S(2)}) collective-permute-start(f32[128,128]{1,0:T(8,128)S(1)} %add.23), channel_id=1, source_target_pairs={{0,8},{4,12},{8,0},{12,4},{16,24},{20,28},{24,16},{28,20},{1,9},{5... | collective-permute-start | bytes 196616 | tf_op jit(solution)/shard_map/ppermute | solution.py:115
  32.3 12.8 %collective-permute-start.8 = (f32[128,128]{1,0:T(8,128)S(1)}, f32[128,128]{1,0:T(8,128)S(1)}, u32[]{:S(2)}, u32[]{:S(2)}) collective-permute-start(f32[128,128]{1,0:T(8,128)S(1)} %broadcast_select_fusion.3), channel_id=1, source_target_pairs={{0,4},{8,12},{16,20},{24,28},{1,5},{9,13},{17,21},{25,29},{2,6},{1... | collective-permute-start | bytes 196616 | tf_op jit(solution)/shard_map/ppermute | solution.py:131
  38.9 5.6 %collective-permute-start.5 = (f32[128,128]{1,0:T(8,128)S(1)}, f32[128,128]{1,0:T(8,128)S(1)}, u32[]{:S(2)}, u32[]{:S(2)}) collective-permute-start(f32[128,128]{1,0:T(8,128)S(1)} %add.24), channel_id=1, source_target_pairs={{0,16},{4,20},{8,24},{12,28},{16,0},{20,4},{24,8},{28,12},{1,17},{... | collective-permute-start | bytes 196616 | tf_op jit(solution)/shard_map/ppermute | solution.py:115
  39.0 19.1 %collective-permute-start.13 = (f32[128,512]{1,0:T(8,128)S(1)}, f32[128,512]{1,0:T(8,128)S(1)}, u32[]{:S(2)}, u32[]{:S(2)}) collective-permute-start(f32[128,512]{1,0:T(8,128)S(1)} %add.26), channel_id=1, source_target_pairs={{0,8},{4,12},{8,0},{12,4},{16,24},{20,28},{24,16},{28,20},{1,9},{5... | collective-permute-start | bytes 786440 | tf_op jit(solution)/shard_map/ppermute | solution.py:115
  41.6 29.8 %collective-permute-start.11 = (f32[128,512]{1,0:T(8,128)S(1)}, f32[128,512]{1,0:T(8,128)S(1)}, u32[]{:S(2)}, u32[]{:S(2)}) collective-permute-start(f32[128,512]{1,0:T(8,128)S(1)} %broadcast_select_fusion.1), channel_id=1, source_target_pairs={{0,4},{8,12},{16,20},{24,28},{1,5},{9,13},{17,21},{25,29},{2,6},{1... | collective-permute-start | bytes 786440 | tf_op jit(solution)/shard_map/ppermute | solution.py:131
  58.1 14.6 %copy-start = (f32[2048,512]{1,0:T(8,128)S(1)}, f32[2048,512]{1,0:T(8,128)}, u32[]{:S(2)}) copy-start(f32[2048,512]{1,0:T(8,128)} %param.5) | copy-start | bytes 12582916
  58.2 12.0 %collective-permute-start.14 = (f32[128,512]{1,0:T(8,128)S(1)}, f32[128,512]{1,0:T(8,128)S(1)}, u32[]{:S(2)}, u32[]{:S(2)}) collective-permute-start(f32[128,512]{1,0:T(8,128)S(1)} %add.27), channel_id=1, source_target_pairs={{0,16},{4,20},{8,24},{12,28},{16,0},{20,4},{24,8},{28,12},{1,17},{... | collective-permute-start | bytes 786440 | tf_op jit(solution)/shard_map/ppermute | solution.py:115

commit v2 on v0

v2 whole, which is shorter than its diff:
```python
import jax
import jax.numpy as jnp
from jax import lax
from jax.experimental import pallas as pl
from jax.experimental.pallas import tpu as pltpu
from jax.sharding import PartitionSpec as P

SUB = 16
GROUP = 2
LAG = 2
HIGHEST, HIGH = lax.Precision.HIGHEST, lax.Precision.HIGH
MOST = 60 << 20
MOST = 50 << 20
FREE = pl.CostEstimate(flops=1, bytes_accessed=1, transcendentals=0)
SCALAR = pl.BlockSpec(memory_space=pltpu.SMEM)
WHOLE = pl.BlockSpec(memory_space=pltpu.VMEM)


def dot(a, b, over, precision=HIGHEST):
    return lax.dot_general(
        a, b, (((over[0],), (over[1],)), ((), ())), precision=precision, preferred_element_type=jnp.float32
    )


def interleave(streams):
    steps = [((i + 0.5) / len(stream), k, step) for k, stream in enumerate(streams) for i, step in enumerate(stream)]
    for _, _, step in sorted(steps, key=lambda item: item[:2]):
        step()


def factor_kernel(even_ref, mine_ref, theirs_ref, panel_factor_ref, weight_ref, inv_ref, pivot_ref, replaced_ref, g, d, lower, upper, lead_ref):
    n = mine_ref.shape[0]
    slabs = n // SUB
    sub = lax.broadcasted_iota(jnp.int32, (SUB, n), 0)
    lane = lax.broadcasted_iota(jnp.int32, (SUB, n), 1)
    one = jnp.float32(1.0)
    state = {}

    def rows(s):
        return pl.ds(s * SUB, SUB)

    def spread(block, j):
        return jnp.broadcast_to(block[j : j + 1, :], block.shape)

    def columns(block, s):
        return [jnp.broadcast_to(block[:, k : k + 1], block.shape) for k in range(s * SUB, (s + 1) * SUB)]

    def within(first, last):
        return (lane >= first * SUB) & (lane < last * SUB)

    def group(s):
        first = s // GROUP * GROUP
        return range(first, first + GROUP)

    def reduce_steps(name, s, ref):
        me = state[name, s] = {}
        split = name == "g"

        def begin():
            block = ref[rows(s), :]
            unit = jnp.where(sub + s * SUB == lane, one, 0.0)
            me["cols"] = columns(block, s)
            if split:
                me["arrays"] = [block, jnp.where(lane < s * SUB, block, unit)]
                me["at"] = list(me["arrays"])
            else:
                me["arrays"] = [jnp.where(within(s, s + 1), unit, block)]
                me["upper"] = unit

        def step(j):
            here = sub == j
            cols = me["cols"]
            inv = 1.0 / spread(cols[j], j)
            me["inv"] = inv if j == 0 else jnp.where(here, inv, me["inv"])
            if j and split:
                me["at"] = [jnp.where(here, a, b) for a, b in zip(me["arrays"], me["at"])]
            mult = jnp.where(here, 0.0, cols[j]) * inv
            for c in range(j + 1, SUB):
                cols[c] = cols[c] - mult * spread(cols[c], j)
            me["arrays"] = [a - mult * spread(a, j) for a in me["arrays"]]
            if j and not split:
                me["upper"] = me["upper"] - jnp.where(sub < j, mult, 0.0) * spread(me["upper"], j)

        def end():
            scaled = [a * me["inv"] for a in me["arrays"]]
            whole = jnp.where(lane < (s + 1) * SUB, scaled[1], scaled[0]) if split else scaled[0]
            me["rows"] = [spread(whole, j) for j in range(SUB)]
            ref[rows(s), :] = whole
            if not split:
                full = me["upper"] * me["inv"]
                me["upper_rows"] = [spread(full, j) for j in range(SUB)]
                upper[rows(s), :] = full

        return [begin] + [lambda j=j: step(j) for j in range(SUB)] + [end]

    def eliminate(name, s, t, ref):
        def run():
            block = ref[rows(t), :]
            cols = columns(block, s)
            block = jnp.where(within(s, s + 1), 0.0, block)
            for col, row in zip(cols, state[name, s]["rows"]):
                block = block - col * row
            ref[rows(t), :] = block
            if name == "d" and t < s:
                block = upper[rows(t), :]
                for col, row in zip(cols, state[name, s]["upper_rows"]):
                    block = block - col * row
                upper[rows(t), :] = block

        return run

    def times(a, b):
        return jnp.dot(a, b, precision=lax.Precision.HIGHEST, preferred_element_type=jnp.float32)

    def others(name, s, ref):
        first, last = group(s)[0], group(s)[-1] + 1

        def run():
            whole = ref[...]
            mask = within(first, last)
            if name == "g":
                targets = list(range(last, slabs))
                left = jnp.concatenate([jnp.where(mask, whole[t * SUB : (t + 1) * SUB], 0.0) for t in targets], axis=0)
                change = times(left, whole)
            else:
                targets = list(range(slabs))
                left = jnp.concatenate(
                    [
                        jnp.where(mask, lower[rows(t), :] if t in group(s) else whole[t * SUB : (t + 1) * SUB], 0.0)
                        for t in targets
                    ],
                    axis=0,
                )
                change = times(left, whole)
                below = times(left[first * SUB :], upper[...])
                for i, t in enumerate(range(first, slabs)):
                    part = below[i * SUB : (i + 1) * SUB]
                    lower[rows(t), :] = jnp.where(mask, part, jnp.where(lane < first * SUB, lower[rows(t), :], 0.0))
            for i, t in enumerate(targets):
                if t not in group(s):
                    block = jnp.where(mask, 0.0, whole[t * SUB : (t + 1) * SUB])
                    ref[rows(t), :] = block - change[i * SUB : (i + 1) * SUB]

        return run

    started = set()

    def start_group(s):
        for t in group(s):
            lower[rows(t), :] = jnp.where(lane < s * SUB, lower[rows(t), :], d[rows(t), :]) if s else d[rows(t), :]
            started.add(t)

    def cholesky_out(s):
        me = state["g", s]

        def first():
            scale = jnp.sqrt(me["inv"])
            x_at, y_at = me["at"]
            me["r"] = jnp.where(lane >= sub + s * SUB, x_at * scale, 0.0)
            me["r_inv_t"] = y_at * scale
            diagonal = jnp.sum(lead_ref[rows(s), :] * me["r_inv_t"], axis=1, keepdims=True)
            me["sign"] = jnp.broadcast_to(jnp.where(diagonal >= 0, -one, one), (SUB, n))

        def second():
            signed = me["sign"] * me["r"]
            panel_factor_ref[rows(s), :] = signed
            weight_ref[rows(s), :] = me["sign"] * me["r_inv_t"]
            replaced_ref[rows(s), :] = lead_ref[rows(s), :] - signed
            d[rows(s), :] = d[rows(s), :] - signed
            if s in started:
                lower[rows(s), :] = lower[rows(s), :] - signed

        return [first, second]

    even = even_ref[0] == 0
    g[...] = jnp.where(even, mine_ref[...], theirs_ref[...])
    lead_ref[...] = jnp.where(even, theirs_ref[...], mine_ref[...])
    d[...] = lead_ref[...]
    lower[...] = jnp.zeros((n, n), jnp.float32)
    upper[...] = jnp.zeros((n, n), jnp.float32)
    for k in range(slabs + LAG):
        streams, after = [], []
        if 0 <= k - 1 < slabs:
            streams.append(cholesky_out(k - 1))
        for name, s, ref in (("g", k, g), ("d", k - LAG, d)):
            if not 0 <= s < slabs:
                continue
            if name == "d" and s % GROUP == 0:
                start_group(s)
            if s % GROUP:
                streams.append([eliminate(name, s - 1, t, ref) for t in group(s) if t not in (s - 1, s)])
            chain = reduce_steps(name, s, ref)
            if (s + 1) % GROUP:
                chain.append(eliminate(name, s, s + 1, ref))
            else:
                chain += [eliminate(name, s, t, ref) for t in group(s) if t != s]
                if name == "d" or s + 1 < slabs:
                    after.append(others(name, s, ref))
            streams.append(chain)
        interleave([s for s in streams if s])
        for step in after:
            step()
    inv_ref[...] = d[...]
    pivot_ref[...] = times(d[...], lower[...])


def factor(odd, mine, theirs):
    n = mine.shape[0]
    out = jax.ShapeDtypeStruct((n, n), jnp.float32)
    return pl.pallas_call(
        factor_kernel,
        out_shape=(out,) * 5,
        in_specs=[SCALAR, WHOLE, WHOLE],
        scratch_shapes=[pltpu.VMEM((n, n), jnp.float32)] * 5,
        compiler_params=pltpu.CompilerParams(vmem_limit_bytes=4 << 20),
        cost_estimate=FREE,
        name="factor",
    )(odd, mine, theirs)


def swap(x, axis, mask):
    return lax.ppermute(x, axis, [(i, i ^ mask) for i in range(lax.axis_size(axis))])


def bits_of(axis):
    return [1 << b for b in range(lax.axis_size(axis).bit_length() - 1)]


def halves(x):
    high = x.astype(jnp.bfloat16)
    return high, (x - high.astype(jnp.float32)).astype(jnp.bfloat16)


def anywhere():
    return pl.BlockSpec(memory_space=pl.ANY)


def fetch(trailing, held, got, steps=4):
    tall = trailing.shape[0] // steps
    copies = [
        pltpu.make_async_copy(trailing.at[pl.ds(i * tall, tall)], held.at[pl.ds(i * tall, tall)], got.at[i])
        for i in range(steps)
    ]
    for copy in copies:
        copy.start()
    return copies


def product(pieces, held, copies):
    left = jnp.concatenate([piece[...] for piece in pieces], axis=0)
    high, low = halves(left)
    both = jnp.concatenate([high, low], axis=0)
    m, tall = left.shape[0], held.shape[0] // len(copies)
    sums = jnp.zeros((m, held.shape[1]), jnp.float32)
    for i, copy in enumerate(copies):
        copy.wait()
        right_high, right_low = halves(held[i * tall : (i + 1) * tall, :])
        part = slice(i * tall, (i + 1) * tall)
        one = jnp.dot(both[:, part], right_high, preferred_element_type=jnp.float32)
        two = jnp.dot(high[:, part], right_low, preferred_element_type=jnp.float32)
        sums = sums + (one[:m] + one[m:] + two)
    return sums


def near_kernel(*refs):
    *pieces, trailing, out, held, got = refs
    out[...] = product(pieces, held, fetch(trailing, held, got))


def near_products(pieces, trailing):
    m, cols = sum(p.shape[0] for p in pieces), trailing.shape[1]
    return pl.pallas_call(
        near_kernel,
        out_shape=jax.ShapeDtypeStruct((m, cols), jnp.float32),
        in_specs=[WHOLE] * len(pieces) + [anywhere()],
        scratch_shapes=[pltpu.VMEM(trailing.shape, jnp.float32), pltpu.SemaphoreType.DMA((4,))],
        compiler_params=pltpu.CompilerParams(vmem_limit_bytes=MOST),
        cost_estimate=FREE,
        name="products",
    )(*pieces, trailing)


def gram_kernel(masks, near, where_ref, *refs):
    pieces, others = refs[: len(masks)], refs[len(masks) :]
    near_sums, trailing, panel_t, mine, keep, give, sums, held, got = others
    copies = fetch(trailing, held, got)
    col, row = where_ref[0], where_ref[1]
    width = pieces[0].shape[0]
    n = width * len(masks)

    def at(mask):
        return pl.ds(pl.multiple_of((col ^ mask) * width, width), width)

    for mask, piece in zip(masks, pieces):
        panel_t[at(mask), :] = piece[...]

    @pl.when(col & 1 == 0)
    def _():
        whole = panel_t[...]
        mine[...] = dot(whole, whole, (1, 1))

    @pl.when(col & 1 == 1)
    def _():
        mine[...] = jnp.where(row == 0, panel_t[:, :n].T, 0.0)

    far = [(mask, piece) for mask, piece in zip(masks, pieces) if mask not in near]
    late = product([piece for _, piece in far], held, copies)
    for i, mask in enumerate(near):
        sums[at(mask), :] = near_sums[i * width : (i + 1) * width, :]
    for i, (mask, _) in enumerate(far):
        sums[at(mask), :] = late[i * width : (i + 1) * width, :]
    half = sums.shape[1] // 2
    first = row & 1 == 0
    keep[...] = jnp.where(first, sums[:, :half], sums[:, half:])
    give[...] = jnp.where(first, sums[:, half:], sums[:, :half])


def gram(where, held, near, near_sums, trailing):
    width, rows = held[0].shape
    n, cols = width * len(held), trailing.shape[1]
    part = jax.ShapeDtypeStruct((n, cols // 2), jnp.float32)
    return pl.pallas_call(
        lambda *refs: gram_kernel(tuple(held), near, *refs),
        out_shape=(
            jax.ShapeDtypeStruct((n, rows), jnp.float32),
            jax.ShapeDtypeStruct((n, n), jnp.float32),
            part,
            part,
        ),
        in_specs=[SCALAR] + [WHOLE] * (len(held) + 1) + [anywhere()],
        scratch_shapes=[
            pltpu.VMEM((n, cols), jnp.float32),
            pltpu.VMEM(trailing.shape, jnp.float32),
            pltpu.SemaphoreType.DMA((4,)),
        ],
        compiler_params=pltpu.CompilerParams(vmem_limit_bytes=MOST),
        cost_estimate=FREE,
        name="gram",
    )(where, *held.values(), near_sums, trailing)


def split_kernel(panel_t, left):
    n, rows = panel_t.shape
    for i in range(0, rows, n):
        high, low = halves(panel_t[:, i : i + n].T)
        left[i : i + n, :n] = high
        left[i : i + n, n:] = low


def split_rows(panel_t):
    n, rows = panel_t.shape
    return pl.pallas_call(
        split_kernel,
        out_shape=jax.ShapeDtypeStruct((rows, 2 * n), jnp.bfloat16),
        in_specs=[WHOLE],
        compiler_params=pltpu.CompilerParams(vmem_limit_bytes=8 << 20),
        cost_estimate=FREE,
        name="split_rows",
    )(panel_t)


def update_kernel(second, where_ref, left_ref, mixed, trailing, *refs):
    if second:
        _, updated, high_ref, low_ref, result, sent = refs
    else:
        pivot, replaced, updated, reflectors, new_left, high_ref, low_ref, result, sent = refs
    row = where_ref[1]
    n, half = mixed.shape
    steps, tall = result.shape[0], result.shape[1]
    mine = row & 1 if not second else 1 - (row & 1)
    columns = pl.ds(pl.multiple_of(mine * half, half), half)
    high, low = halves(mixed[...])
    high_ref[:n], high_ref[n:] = high, high
    low_ref[:n], low_ref[n:] = low, low

    def going(i):
        return pltpu.make_async_copy(result.at[i], updated.at[pl.ds(i * tall, tall), columns], sent.at[i])

    def rows_of(i):
        left = left_ref[i * tall : (i + 1) * tall, :]
        if i == 0 and not second:
            top = jnp.concatenate(halves(replaced[...]), axis=1)
            left = jnp.concatenate([jnp.where(row == 0, top, left[:n]), left[n:]], axis=0)
            new_left[...] = left[:n]
        return left

    def times(left, high, low):
        return jnp.dot(left, high, preferred_element_type=jnp.float32) + jnp.dot(
            left, low, preferred_element_type=jnp.float32
        )

    for i in range(steps):
        result[i] = trailing[i * tall : (i + 1) * tall, columns] - times(rows_of(i), high_ref[...], low_ref[...])
        going(i).start()
    if not second:
        width = reflectors.shape[0]
        own = pivot[...]
        own = pltpu.roll(own, (n - where_ref[0] * width) % n, 1)
        a, b = halves(own)
        a, b = jnp.concatenate([a, a], axis=0), jnp.concatenate([b, b], axis=0)
        for i in range(steps):
            left = left_ref[i * tall : (i + 1) * tall, :]
            if i == 0:
                left = jnp.concatenate([new_left[...], left[n:]], axis=0)
            reflectors[:, i * tall : (i + 1) * tall] = times(left, a, b).T[:width]
    for i in range(steps):
        going(i).wait()


def update(where, left, mixed, trailing, pivot, replaced, width):
    n, half = mixed.shape
    rows, cols = trailing.shape
    steps = 4
    return pl.pallas_call(
        lambda *refs: update_kernel(False, *refs),
        out_shape=(
            jax.ShapeDtypeStruct((rows, cols), jnp.float32),
            jax.ShapeDtypeStruct((width, rows), jnp.float32),
            jax.ShapeDtypeStruct((n, 2 * n), jnp.bfloat16),
        ),
        in_specs=[SCALAR] + [WHOLE] * 5,
        out_specs=(anywhere(), WHOLE, WHOLE),
        scratch_shapes=[pltpu.VMEM((2 * n, half), jnp.bfloat16)] * 2
        + [pltpu.VMEM((steps, rows // steps, half), jnp.float32)]
        + [pltpu.SemaphoreType.DMA((steps,))],
        compiler_params=pltpu.CompilerParams(vmem_limit_bytes=8 << 20),
        cost_estimate=FREE,
        name="update",
    )(where, left, mixed, trailing, pivot, replaced)


def update_rest(where, left, new_left, mixed, trailing, updated):
    n, half = mixed.shape
    rows, cols = trailing.shape
    steps = 4

    def kernel(where_ref, left_ref, new_left_ref, mixed_ref, trailing_ref, updated_ref, *refs):
        out, scratch, high, low, result, sent = refs
        scratch[...] = left_ref[...]
        scratch[:n, :] = new_left_ref[...]
        update_kernel(True, where_ref, scratch, mixed_ref, trailing_ref, updated_ref, out, high, low, result, sent)

    return pl.pallas_call(
        kernel,
        out_shape=jax.ShapeDtypeStruct((rows, cols), jnp.float32),
        in_specs=[SCALAR] + [WHOLE] * 4 + [anywhere()],
        out_specs=anywhere(),
        scratch_shapes=[pltpu.VMEM((rows, 2 * n), jnp.bfloat16)]
        + [pltpu.VMEM((2 * n, half), jnp.bfloat16)] * 2
        + [pltpu.VMEM((steps, rows // steps, half), jnp.float32)]
        + [pltpu.SemaphoreType.DMA((steps,))],
        input_output_aliases={5: 0},
        compiler_params=pltpu.CompilerParams(vmem_limit_bytes=8 << 20),
        cost_estimate=FREE,
        name="update_rest",
    )(where, left, new_left, mixed, trailing, updated)


def mix(mine, theirs, lead, weight, inv):
    def kernel(mine, theirs, lead, weight, inv, mixed):
        rest = lead[...] - dot(weight[...], mine[...] + theirs[...], (1, 0))
        mixed[...] = dot(inv[...], rest, (1, 0))

    return pl.pallas_call(
        kernel,
        out_shape=jax.ShapeDtypeStruct(mine.shape, jnp.float32),
        in_specs=[WHOLE] * 5,
        compiler_params=pltpu.CompilerParams(vmem_limit_bytes=3 << 20),
        cost_estimate=FREE,
        name="mix",
    )(mine, theirs, lead, weight, inv)


def after(x, *others):
    return lax.optimization_barrier((x, *others))[0]


def per_device(panel_block, trailing):
    own = panel_block.T
    col, row = lax.axis_index("col"), lax.axis_index("row")
    where = jnp.stack([col, row]).astype(jnp.int32)
    held = {0: own}
    for bit in reversed(bits_of("col")):
        held.update({mask | bit: swap(piece, "col", bit) for mask, piece in list(held.items())})
    n = own.shape[0] * len(held)
    bits = bits_of("row")
    order = sorted(held)
    near, far = order[: len(order) // 2], order[len(order) // 2 :]

    odd = row & bits[0] != 0
    half = trailing.shape[1] // 2
    left_half, right_half = trailing[:n, :half], trailing[:n, half:]
    lead_got = swap(jnp.where(odd, left_half, right_half), "row", bits[0])
    lead = jnp.where(odd, lead_got, left_half)
    lead_got = swap(lead, "row", bits[-1])
    near_sums = near_products([held[m] for m in near], trailing)
    held[far[0]], near_sums, lead = lax.optimization_barrier((held[far[0]], near_sums, lead))
    for m in far[1:]:
        held[m] = swap(held[far[0]], "col", m ^ far[0])
    panel_t, mine, keep, give = gram(where, held, near, near_sums, trailing)
    left = split_rows(panel_t)
    got = swap(give, "row", bits[0])
    for bit in bits[1:-1]:
        mine = mine + swap(mine, "row", bit)
    lead_got, got, mine = lax.optimization_barrier((lead_got, got, mine))
    lead = jnp.where(row & bits[-1] != 0, lead_got, lead)
    for bit in reversed(bits[1:-1]):
        lead = jnp.where(row & bit != 0, swap(lead, "row", bit), lead)
    mine = mine + swap(mine, "row", bits[-1])
    sums, lead, _ = lax.optimization_barrier((keep + got, lead, mine))
    mine, left = lax.optimization_barrier((mine + swap(mine, "row", bits[0]), left))
    for bit in bits[1:-1]:
        sums = sums + swap(sums, "row", bit)
    theirs = swap(mine, "col", 1)
    last = swap(sums, "row", bits[-1])
    theirs, sums = lax.optimization_barrier((theirs, sums))
    panel_factor, weight, inv, pivot, replaced = factor(col.astype(jnp.int32).reshape(1) & 1, mine, theirs)
    mixed = mix(sums, last, lead, weight, inv)
    other = swap(mixed, "row", bits[0])
    updated, reflectors, top = update(where, left, mixed, trailing, pivot, replaced, own.shape[0])
    updated = update_rest(where, left, top, other, trailing, updated)
    return updated, reflectors.T, panel_factor


def solution(mesh):
    in_specs = (P("row", "col"), P("row", "col"))
    out_specs = (P("row", "col"), P("row", "col"), P())
    return jax.shard_map(per_device, mesh=mesh, in_specs=in_specs, out_specs=out_specs, check_vma=False)
```

time: 490 us -> 55.9 us (0.11)
  other arithmetic: 185 us -> 2.13 us
  waiting for transfers between devices: 164 us -> 15.1 us
  local copies, waits for them, and re-layouts: 90.7 us -> 0.96 us
  matrix products: 22 us -> 0 us
  Pallas kernels: 0 us -> 18.3 us
  between operations: 14 us -> 0.79 us
  starting transfers between devices: 5.68 us -> 18.4 us
  loops' own time: 7.02 us -> 0 us
    psum x2 -> x0, waiting for transfers between devices: 138 us -> none  [the longest x1 69.2 us: from_root(): return lax.psum(jnp.where(mine, x, jnp.zeros_like(x)), axis)]
    broadcast_in_dim x128 -> x0, other arithmetic: 83.7 us -> none  [advance(): return jnp.where(place_mask, factor_col[:, None], current)]
    another operation x20 -> x1, other arithmetic: 81.2 us -> 0.07 us  [per_device(): where = jnp.stack([col, row]).astype(jnp.int32)]
    dynamic_slice x128 -> x0, local copies, waits for them, and re-layouts: 75.3 us -> none  [advance(): pivot_value = lax.dynamic_index_in_dim(row_pick, column, 0, keepdims=False)]
    all_gather x1 -> x0, waiting for transfers between devices: 20.3 us -> none  [per_device(): panel_rows = lax.all_gather(panel_block, 'col', axis=1, tiled=True)]
    dot_general x10 -> x0, matrix products: 19.6 us -> none  [the longest x1 6.63 us: per_device(): lax.dot_general(reflect_t, mixed, (((0,), (1,)), ((), ())), precision=HIG...]
    pallas_call x0 -> x7, Pallas kernels: none -> 18.3 us  [the longest x1 6.13 us: factor(): pl.pallas_call(factor_kernel, out_shape=(out,) * 5, in_specs=[SCALAR, WHO...]
    ppermute x3 -> x14, starting transfers between devices: 5.56 us -> 18.4 us  [swap(): lax.ppermute(x, axis, [(i, i ^ mask) for i in range(lax.axis_size(axis))])]
  transfers between devices with their start and end apart: 6 -> 14, of which waited for: 6 -> 8; matrix products, arithmetic and copies ran while one was open for 1% -> 2% of each run, Pallas kernels for 0% -> 27%
where the time goes in v2:
time: 55.9 us; the launch traced here: 55.7 us
  starting transfers between devices  18.4 us (33%)
  Pallas kernels  18.3 us (33%)
  waiting for transfers between devices  15.1 us (27%)
  other arithmetic  2.13 us (4%)
  local copies, waits for them, and re-layouts  0.96 us (2%)
  between operations  0.79 us (1%)
    ppermute x14, starting transfers between devices, swap(): lax.ppermute(x, axis, [(i, i ^ mask) for i in range(lax.axis_size(axis))])  18.4 us
    ppermute x14, waiting for transfers between devices, swap(): lax.ppermute(x, axis, [(i, i ^ mask) for i in range(lax.axis_size(axis))])  15.1 us
    pallas_call x1, Pallas kernels, factor(): pl.pallas_call(factor_kernel, out_shape=(out,) * 5, in_specs=[SCALAR, WHO...  6.13 us
    pallas_call x1, Pallas kernels, update(): pl.pallas_call(lambda *refs: update_kernel(False, *refs), out_shape=(jax....  3.24 us
    pallas_call x1, Pallas kernels, gram(): pl.pallas_call(lambda *refs: gram_kernel(tuple(held), near, *refs), out_s...  3.08 us
    pallas_call x1, Pallas kernels, near_products(): pl.pallas_call(near_kernel, out_shape=jax.ShapeDtypeStruct((m, cols), jnp...  2.51 us
    pallas_call x1, Pallas kernels, update_rest(): pl.pallas_call(kernel, out_shape=jax.ShapeDtypeStruct((rows, cols), jnp.f...  2.35 us
  transfers between devices with their start and end apart: 14, of which 8 were waited for; matrix products, arithmetic and copies ran while one was open for 2% of the time, Pallas kernels for 27%

profile of v2, /device:TPU:0, one launch (start us, length us, event | category | flops | bytes accessed | tf_op | source)
XLA Modules:
  0.0 55.7 jit_solution(14849686440567202322)
XLA Ops:
  0.6 1.0 %slice_select_fusion = f32[128,256]{1,0:T(8,128)S(1)} fusion(f32[2048,512]{1,0:T(8,128)} %trailing_ref.1, pred[]{:T(512)S(6)} %ne.9), kind=kLoop, calls=%fused_computation | loop fusion | flops 32768 | bytes 393217 | tf_op jit(solution)/shard_map/jit(_where)/select_n | solution.py:493
  1.7 3.0 %collective-permute-start = (f32[128,256]{1,0:T(8,128)S(1)}, f32[128,256]{1,0:T(8,128)S(1)}, u32[]{:S(2)}, u32[]{:S(2)}) collective-permute-start(f32[128,256]{1,0:T(8,128)S(1)} %slice_select_fusion), channel_id=1, source_target_pairs={{0,4},{4,0},{8,12},{12,8},{16,20},{20,16},{24,28},{28,24},{1,5},{5... | collective-permute-start | bytes 393224 | tf_op jit(solution)/shard_map/ppermute | solution.py:222
  4.7 1.5 %collective-permute-start.2 = (f32[32,2048]{1,0:T(8,128)}, f32[32,2048]{1,0:T(8,128)S(1)}, u32[]{:S(2)}, u32[]{:S(2)}) collective-permute-start(f32[32,2048]{1,0:T(8,128)} %bitcast.5), channel_id=1, source_target_pairs={{0,2},{1,3},{2,0},{3,1},{4,6},{5,7},{6,4},{7,5},{8,10},{9,11},{10,... | collective-permute-start | bytes 786440 | tf_op jit(solution)/shard_map/ppermute | solution.py:222
  6.2 2.0 %collective-permute-done = f32[128,256]{1,0:T(8,128)S(1)} collective-permute-done((f32[128,256]{1,0:T(8,128)S(1)}, f32[128,256]{1,0:T(8,128)S(1)}, u32[]{:S(2)}, u32[]{:S(2)}) %collective-permute-start) | collective-permute-done | bytes 131104 | tf_op jit(solution)/shard_map/ppermute | solution.py:222
  8.2 0.9 %slice_select_fusion.1 = f32[128,256]{1,0:T(8,128)S(1)} fusion(f32[128,256]{1,0:T(8,128)S(1)} %collective-permute-done, f32[2048,512]{1,0:T(8,128)} %trailing_ref.1, pred[]{:T(512)S(6)} %ne.9), kind=kLoop, calls=%fused_computation.1 | loop fusion | flops 32768 | bytes 393217 | tf_op jit(solution)/shard_map/jit(_where)/select_n | solution.py:494
  9.2 0.9 %copy-done.1 = f32[2048,32]{0,1:T(8,128)S(1)} copy-done((f32[2048,32]{0,1:T(8,128)S(1)}, f32[2048,32]{0,1:T(8,128)}, u32[]{:S(2)}) %copy-start.1) | copy-done | bytes 262168
  10.1 2.5 %products.1.refs_5_ = f32[64,512]{1,0:T(8,128)S(1)} custom-call(f32[32,2048]{1,0:T(8,128)S(1)} %bitcast.6, f32[32,2048]{1,0:T(8,128)S(1)} %collective-permute-done.3.refs_1_.refs_3_, f32[2048,512]{1,0:T(8,128)} %trailing_ref.1), custom_call_target="tpu_custom_call" | custom-call | flops 1 | bytes 1 | tf_op jit(solution)/shard_map/products/pallas_call | solution.py:272
  12.6 1.0 %collective-permute-done.2.refs_2_ = f32[32,2048]{1,0:T(8,128)S(1)} collective-permute-done((f32[32,2048]{1,0:T(8,128)}, f32[32,2048]{1,0:T(8,128)S(1)}, u32[]{:S(2)}, u32[]{:S(2)}) %collective-permute-start.2) | collective-permute-done | bytes 262176 | tf_op jit(solution)/shard_map/ppermute | solution.py:222
  13.7 2.6 %collective-permute-start.1 = (f32[128,256]{1,0:T(8,128)S(1)}, f32[128,256]{1,0:T(8,128)S(1)}, u32[]{:S(2)}, u32[]{:S(2)}) collective-permute-start(f32[128,256]{1,0:T(8,128)S(1)} %slice_select_fusion.1), channel_id=1, source_target_pairs={{0,16},{4,20},{8,24},{12,28},{16,0},{20,4},{24,8},{28,12},{1,17},{... | collective-permute-start | bytes 393224 | tf_op jit(solution)/shard_map/ppermute | solution.py:222
  16.3 3.1 %gram.1 = (f32[128,2048]{1,0:T(8,128)S(1)}, f32[128,128]{1,0:T(8,128)S(1)}, f32[128,256]{1,0:T(8,128)S(1)}, f32[128,256]{1,0:T(8,128)S(1)}) custom-call(s32[2]{0:T(128)S(1)} %pad_add_fusion.refs_0_.where_ref, f32[32,2048]{1,0:T(8,128)S(1)} %bitcast.7, f32[32,2048]{1,0:T(8,128)S(1)} %collective-permute-done.2.refs_2_, ...), custom_call_target="tpu_custom_call" | custom-call | flops 1 | bytes 1 | tf_op jit(solution)/shard_map/gram/pallas_call | solution.py:322
  19.4 0.9 %collective-permute-start.5 = (f32[128,256]{1,0:T(8,128)S(1)}, f32[128,256]{1,0:T(8,128)S(1)}, u32[]{:S(2)}, u32[]{:S(2)}) collective-permute-start(f32[128,256]{1,0:T(8,128)S(1)} %get-tuple-element.29), channel_id=1, source_target_pairs={{0,4},{4,0},{8,12},{12,8},{16,20},{20,16},{24,28},{28,24},{1,5},{5... | collective-permute-start | bytes 393224 | tf_op jit(solution)/shard_map/ppermute | solution.py:222
  20.3 1.6 %collective-permute-start.6 = (f32[128,128]{1,0:T(8,128)S(1)}, f32[128,128]{1,0:T(8,128)S(1)}, u32[]{:S(2)}, u32[]{:S(2)}) collective-permute-start(f32[128,128]{1,0:T(8,128)S(1)} %get-tuple-element.30), channel_id=1, source_target_pairs={{0,8},{4,12},{8,0},{12,4},{16,24},{20,28},{24,16},{28,20},{1,9},{5... | collective-permute-start | bytes 196616 | tf_op jit(solution)/shard_map/ppermute | solution.py:222
  21.8 2.9 %collective-permute-done.6 = f32[128,128]{1,0:T(8,128)S(1)} collective-permute-done((f32[128,128]{1,0:T(8,128)S(1)}, f32[128,128]{1,0:T(8,128)S(1)}, u32[]{:S(2)}, u32[]{:S(2)}) %collective-permute-start.6) | collective-permute-done | bytes 65568 | tf_op jit(solution)/shard_map/ppermute | solution.py:222
  25.1 1.6 %collective-permute-start.10 = (f32[128,256]{1,0:T(8,128)S(1)}, f32[128,256]{1,0:T(8,128)S(1)}, u32[]{:S(2)}, u32[]{:S(2)}) collective-permute-start(f32[128,256]{1,0:T(8,128)S(1)} %broadcast_select_fusion), channel_id=1, source_target_pairs={{0,8},{4,12},{8,0},{12,4},{16,24},{20,28},{24,16},{28,20},{1,9},{5... | collective-permute-start | bytes 393224 | tf_op jit(solution)/shard_map/ppermute | solution.py:222
  26.8 2.2 %collective-permute-start.7 = (f32[128,128]{1,0:T(8,128)S(1)}, f32[128,128]{1,0:T(8,128)S(1)}, u32[]{:S(2)}, u32[]{:S(2)}) collective-permute-start(f32[128,128]{1,0:T(8,128)S(1)} %add.15), channel_id=1, source_target_pairs={{0,16},{4,20},{8,24},{12,28},{16,0},{20,4},{24,8},{28,12},{1,17},{... | collective-permute-start | bytes 196616 | tf_op jit(solution)/shard_map/ppermute | solution.py:222
  28.9 3.5 %collective-permute-done.7 = f32[128,128]{1,0:T(8,128)S(1)} collective-permute-done((f32[128,128]{1,0:T(8,128)S(1)}, f32[128,128]{1,0:T(8,128)S(1)}, u32[]{:S(2)}, u32[]{:S(2)}) %collective-permute-start.7) | collective-permute-done | bytes 65568 | tf_op jit(solution)/shard_map/ppermute | solution.py:222
  32.5 1.6 %collective-permute-start.11 = (f32[128,256]{1,0:T(8,128)S(1)}, f32[128,256]{1,0:T(8,128)S(1)}, u32[]{:S(2)}, u32[]{:S(2)}) collective-permute-start(f32[128,256]{1,0:T(8,128)S(1)} %add.18), channel_id=1, source_target_pairs={{0,8},{4,12},{8,0},{12,4},{16,24},{20,28},{24,16},{28,20},{1,9},{5... | collective-permute-start | bytes 393224 | tf_op jit(solution)/shard_map/ppermute | solution.py:222
  34.9 2.6 %collective-permute-done.11 = f32[128,256]{1,0:T(8,128)S(1)} collective-permute-done((f32[128,256]{1,0:T(8,128)S(1)}, f32[128,256]{1,0:T(8,128)S(1)}, u32[]{:S(2)}, u32[]{:S(2)}) %collective-permute-start.11) | collective-permute-done | bytes 131104 | tf_op jit(solution)/shard_map/ppermute | solution.py:222
  37.5 1.7 %collective-permute-start.12 = (f32[128,256]{1,0:T(8,128)S(1)}, f32[128,256]{1,0:T(8,128)S(1)}, u32[]{:S(2)}, u32[]{:S(2)}) collective-permute-start(f32[128,256]{1,0:T(8,128)S(1)} %add.19.mine), channel_id=1, source_target_pairs={{0,16},{4,20},{8,24},{12,28},{16,0},{20,4},{24,8},{28,12},{1,17},{... | collective-permute-start | bytes 393224 | tf_op jit(solution)/shard_map/ppermute | solution.py:222
  39.7 1.2 %collective-permute-done.9.theirs_ref = f32[128,128]{1,0:T(8,128)S(1)} collective-permute-done((f32[128,128]{1,0:T(8,128)S(1)}, f32[128,128]{1,0:T(8,128)S(1)}, u32[]{:S(2)}, u32[]{:S(2)}) %collective-permute-start.9) | collective-permute-done | bytes 65568 | tf_op jit(solution)/shard_map/ppermute | solution.py:222
  41.0 6.1 %factor.1 = (f32[128,128]{1,0:T(8,128)}, f32[128,128]{1,0:T(8,128)S(1)}, f32[128,128]{1,0:T(8,128)S(1)}, f32[128,128]{1,0:T(8,128)S(1)}, f32[128,128]{1,0:T(8,128)S(1)}) custom-call(s32[1]{0:T(128)S(6)} %and.17.even_ref, f32[128,128]{1,0:T(8,128)S(1)} %add.17.mine_ref, f32[128,128]{1,0:T(8,128)S(1)} %collective-permute-done.9.theirs_ref), custom_call_target="tpu_custom_call" | custom-call | flops 1 | bytes 1 | tf_op jit(solution)/shard_map/factor/pallas_call | solution.py:210
  48.6 3.2 %update.1 = (f32[2048,512]{1,0:T(8,128)}, f32[32,2048]{1,0:T(8,128)}, bf16[128,256]{1,0:T(8,128)(2,1)S(1)}) custom-call(s32[2]{0:T(128)S(1)} %pad_add_fusion.refs_0_.where_ref, bf16[2048,256]{1,0:T(8,128)(2,1)S(1)} %split_rows.1.refs_1_.left_ref, f32[128,256]{1,0:T(8,128)S(1)} %mix.1.refs_2_, f32[2048,512]{1,0:T(8,128)S(1)} %copy-done, ...), custom_call_target="tpu_custom_call" | custom-call | flops 1 | bytes 1 | tf_op jit(solution)/shard_map/update/pallas_call | solution.py:414
  51.9 1.5 %collective-permute-done.13.mixed_ref = f32[128,256]{1,0:T(8,128)S(1)} collective-permute-done((f32[128,256]{1,0:T(8,128)S(1)}, f32[128,256]{1,0:T(8,128)S(1)}, u32[]{:S(2)}, u32[]{:S(2)}) %collective-permute-start.13) | collective-permute-done | bytes 131104 | tf_op jit(solution)/shard_map/ppermute | solution.py:222
  53.4 2.4 %update_rest.1 = f32[2048,512]{1,0:T(8,128)} custom-call(s32[2]{0:T(128)S(1)} %pad_add_fusion.refs_0_.where_ref, bf16[2048,256]{1,0:T(8,128)(2,1)S(1)} %split_rows.1.refs_1_.left_ref, bf16[128,256]{1,0:T(8,128)(2,1)S(1)} %get-tuple-element.47.new_left_ref, f32[128,256]{1,0:T(8,128)S(1)} %collective-permute-done.13.mixed_ref, ...), custom_call_target="tpu_custom_call", output_to_operand_aliasing={{}: (5, {})} | custom-call | flops 1 | bytes 1 | tf_op jit(solution)/shard_map/update_rest/pallas_call | solution.py:443
  (27 shorter events, 3.2 us)
Async XLA Ops:
  0.6 15.7 %copy-start.2 = (f32[2048,32]{0,1:T(8,128)S(1)}, f32[2048,32]{0,1:T(8,128)}, u32[]{:S(2)}) copy-start(f32[2048,32]{0,1:T(8,128)} %param.2) | copy-start | bytes 786436
  1.7 6.5 %collective-permute-start = (f32[128,256]{1,0:T(8,128)S(1)}, f32[128,256]{1,0:T(8,128)S(1)}, u32[]{:S(2)}, u32[]{:S(2)}) collective-permute-start(f32[128,256]{1,0:T(8,128)S(1)} %slice_select_fusion), channel_id=1, source_target_pairs={{0,4},{4,0},{8,12},{12,8},{16,20},{20,16},{24,28},{28,24},{1,5},{5... | collective-permute-start | bytes 393224 | tf_op jit(solution)/shard_map/ppermute | solution.py:222
  4.7 4.4 %collective-permute-start.3 = (f32[32,2048]{1,0:T(8,128)}, f32[32,2048]{1,0:T(8,128)S(1)}, u32[]{:S(2)}, u32[]{:S(2)}) collective-permute-start(f32[32,2048]{1,0:T(8,128)} %bitcast.4), channel_id=1, source_target_pairs={{0,1},{1,0},{2,3},{3,2},{4,5},{5,4},{6,7},{7,6},{8,9},{9,8},{10,11... | collective-permute-start | bytes 786440 | tf_op jit(solution)/shard_map/ppermute | solution.py:222
  4.7 8.9 %collective-permute-start.2 = (f32[32,2048]{1,0:T(8,128)}, f32[32,2048]{1,0:T(8,128)S(1)}, u32[]{:S(2)}, u32[]{:S(2)}) collective-permute-start(f32[32,2048]{1,0:T(8,128)} %bitcast.5), channel_id=1, source_target_pairs={{0,2},{1,3},{2,0},{3,1},{4,6},{5,7},{6,4},{7,5},{8,10},{9,11},{10,... | collective-permute-start | bytes 786440 | tf_op jit(solution)/shard_map/ppermute | solution.py:222
  9.1 1.0 %copy-start.1 = (f32[2048,32]{0,1:T(8,128)S(1)}, f32[2048,32]{0,1:T(8,128)}, u32[]{:S(2)}) copy-start(f32[2048,32]{0,1:T(8,128)} %param.2) | copy-start | bytes 786436
  13.6 2.7 %collective-permute-start.4 = (f32[32,2048]{1,0:T(8,128)S(1)}, f32[32,2048]{1,0:T(8,128)S(1)}, u32[]{:S(2)}, u32[]{:S(2)}) collective-permute-start(f32[32,2048]{1,0:T(8,128)S(1)} %collective-permute-done.2.refs_2_), channel_id=1, source_target_pairs={{0,1},{1,0},{2,3},{3,2},{4,5},{5,4},{6,7},{7,6},{8,9},{9,8},{10,11... | collective-permute-start | bytes 786440 | tf_op jit(solution)/shard_map/ppermute | solution.py:222
  13.7 11.0 %collective-permute-start.1 = (f32[128,256]{1,0:T(8,128)S(1)}, f32[128,256]{1,0:T(8,128)S(1)}, u32[]{:S(2)}, u32[]{:S(2)}) collective-permute-start(f32[128,256]{1,0:T(8,128)S(1)} %slice_select_fusion.1), channel_id=1, source_target_pairs={{0,16},{4,20},{8,24},{12,28},{16,0},{20,4},{24,8},{28,12},{1,17},{... | collective-permute-start | bytes 393224 | tf_op jit(solution)/shard_map/ppermute | solution.py:222
  19.4 5.7 %collective-permute-start.5 = (f32[128,256]{1,0:T(8,128)S(1)}, f32[128,256]{1,0:T(8,128)S(1)}, u32[]{:S(2)}, u32[]{:S(2)}) collective-permute-start(f32[128,256]{1,0:T(8,128)S(1)} %get-tuple-element.29), channel_id=1, source_target_pairs={{0,4},{4,0},{8,12},{12,8},{16,20},{20,16},{24,28},{28,24},{1,5},{5... | collective-permute-start | bytes 393224 | tf_op jit(solution)/shard_map/ppermute | solution.py:222
  20.3 4.5 %collective-permute-start.6 = (f32[128,128]{1,0:T(8,128)S(1)}, f32[128,128]{1,0:T(8,128)S(1)}, u32[]{:S(2)}, u32[]{:S(2)}) collective-permute-start(f32[128,128]{1,0:T(8,128)S(1)} %get-tuple-element.30), channel_id=1, source_target_pairs={{0,8},{4,12},{8,0},{12,4},{16,24},{20,28},{24,16},{28,20},{1,9},{5... | collective-permute-start | bytes 196616 | tf_op jit(solution)/shard_map/ppermute | solution.py:222
  25.1 7.3 %collective-permute-start.10 = (f32[128,256]{1,0:T(8,128)S(1)}, f32[128,256]{1,0:T(8,128)S(1)}, u32[]{:S(2)}, u32[]{:S(2)}) collective-permute-start(f32[128,256]{1,0:T(8,128)S(1)} %broadcast_select_fusion), channel_id=1, source_target_pairs={{0,8},{4,12},{8,0},{12,4},{16,24},{20,28},{24,16},{28,20},{1,9},{5... | collective-permute-start | bytes 393224 | tf_op jit(solution)/shard_map/ppermute | solution.py:222
  26.8 5.7 %collective-permute-start.7 = (f32[128,128]{1,0:T(8,128)S(1)}, f32[128,128]{1,0:T(8,128)S(1)}, u32[]{:S(2)}, u32[]{:S(2)}) collective-permute-start(f32[128,128]{1,0:T(8,128)S(1)} %add.15), channel_id=1, source_target_pairs={{0,16},{4,20},{8,24},{12,28},{16,0},{20,4},{24,8},{28,12},{1,17},{... | collective-permute-start | bytes 196616 | tf_op jit(solution)/shard_map/ppermute | solution.py:222
  28.9 19.7 %copy-start = (f32[2048,512]{1,0:T(8,128)S(1)}, f32[2048,512]{1,0:T(8,128)}, u32[]{:S(2)}) copy-start(f32[2048,512]{1,0:T(8,128)} %trailing_ref.1) | copy-start | bytes 12582916
  32.5 5.0 %collective-permute-start.11 = (f32[128,256]{1,0:T(8,128)S(1)}, f32[128,256]{1,0:T(8,128)S(1)}, u32[]{:S(2)}, u32[]{:S(2)}) collective-permute-start(f32[128,256]{1,0:T(8,128)S(1)} %add.18), channel_id=1, source_target_pairs={{0,8},{4,12},{8,0},{12,4},{16,24},{20,28},{24,16},{28,20},{1,9},{5... | collective-permute-start | bytes 393224 | tf_op jit(solution)/shard_map/ppermute | solution.py:222
  34.1 5.5 %collective-permute-start.8 = (f32[128,128]{1,0:T(8,128)S(1)}, f32[128,128]{1,0:T(8,128)S(1)}, u32[]{:S(2)}, u32[]{:S(2)}) collective-permute-start(f32[128,128]{1,0:T(8,128)S(1)} %add.16), channel_id=1, source_target_pairs={{0,4},{4,0},{8,12},{12,8},{16,20},{20,16},{24,28},{28,24},{1,5},{5... | collective-permute-start | bytes 196616 | tf_op jit(solution)/shard_map/ppermute | solution.py:222
  37.5 9.5 %collective-permute-start.12 = (f32[128,256]{1,0:T(8,128)S(1)}, f32[128,256]{1,0:T(8,128)S(1)}, u32[]{:S(2)}, u32[]{:S(2)}) collective-permute-start(f32[128,256]{1,0:T(8,128)S(1)} %add.19.mine), channel_id=1, source_target_pairs={{0,16},{4,20},{8,24},{12,28},{16,0},{20,4},{24,8},{28,12},{1,17},{... | collective-permute-start | bytes 393224 | tf_op jit(solution)/shard_map/ppermute | solution.py:222
  39.6 1.3 %collective-permute-start.9 = (f32[128,128]{1,0:T(8,128)S(1)}, f32[128,128]{1,0:T(8,128)S(1)}, u32[]{:S(2)}, u32[]{:S(2)}) collective-permute-start(f32[128,128]{1,0:T(8,128)S(1)} %add.17.mine_ref), channel_id=1, source_target_pairs={{0,1},{1,0},{2,3},{3,2},{4,5},{5,4},{6,7},{7,6},{8,9},{9,8},{10,11... | collective-permute-start | bytes 196616 | tf_op jit(solution)/shard_map/ppermute | solution.py:222
  47.8 5.6 %collective-permute-start.13 = (f32[128,256]{1,0:T(8,128)S(1)}, f32[128,256]{1,0:T(8,128)S(1)}, u32[]{:S(2)}, u32[]{:S(2)}) collective-permute-start(f32[128,256]{1,0:T(8,128)S(1)} %mix.1.refs_2_), channel_id=1, source_target_pairs={{0,4},{4,0},{8,12},{12,8},{16,20},{20,16},{24,28},{28,24},{1,5},{5... | collective-permute-start | bytes 393224 | tf_op jit(solution)/shard_map/ppermute | solution.py:222

commit v3 on v2

--- a/solution.py
+++ b/solution.py
@@ -204,18 +204,31 @@
     pivot_ref[...] = times(d[...], lower[...])
 
 
-def factor(odd, mine, theirs):
+def fetching_factor_kernel(odd, mine, theirs, trailing, *refs):
+    *outs, held = refs[:6]
+    *scratch, got = refs[6:]
+    copy = pltpu.make_async_copy(trailing, held, got.at[0])
+    copy.start()
+
+    @pl.when(odd[0] >= 0)
+    def _():
+        factor_kernel(odd, mine, theirs, *outs, *scratch)
+
+    copy.wait()
+
+
+def factor(odd, mine, theirs, trailing):
     n = mine.shape[0]
     out = jax.ShapeDtypeStruct((n, n), jnp.float32)
     return pl.pallas_call(
-        factor_kernel,
-        out_shape=(out,) * 5,
-        in_specs=[SCALAR, WHOLE, WHOLE],
-        scratch_shapes=[pltpu.VMEM((n, n), jnp.float32)] * 5,
-        compiler_params=pltpu.CompilerParams(vmem_limit_bytes=4 << 20),
-        cost_estimate=FREE,
+        fetching_factor_kernel,
+        out_shape=(out,) * 5 + (jax.ShapeDtypeStruct(trailing.shape, jnp.float32),),
+        in_specs=[SCALAR, WHOLE, WHOLE, anywhere()],
+        scratch_shapes=[pltpu.VMEM((n, n), jnp.float32)] * 5 + [pltpu.SemaphoreType.DMA((1,))],
+        compiler_params=pltpu.CompilerParams(vmem_limit_bytes=47 << 20),
+        cost_estimate=pl.CostEstimate(flops=0, bytes_accessed=22_000_000, transcendentals=0),
         name="factor",
-    )(odd, mine, theirs)
+    )(odd, mine, theirs, trailing)
 
 
 def swap(x, axis, mask):
@@ -235,7 +248,7 @@
     return pl.BlockSpec(memory_space=pl.ANY)
 
 
-def fetch(trailing, held, got, steps=4):
+def fetch(trailing, held, got, steps=8):
     tall = trailing.shape[0] // steps
     copies = [
         pltpu.make_async_copy(trailing.at[pl.ds(i * tall, tall)], held.at[pl.ds(i * tall, tall)], got.at[i])
@@ -262,198 +275,174 @@
     return sums
 
 
-def near_kernel(*refs):
-    *pieces, trailing, out, held, got = refs
-    out[...] = product(pieces, held, fetch(trailing, held, got))
-
-
-def near_products(pieces, trailing):
-    m, cols = sum(p.shape[0] for p in pieces), trailing.shape[1]
-    return pl.pallas_call(
-        near_kernel,
-        out_shape=jax.ShapeDtypeStruct((m, cols), jnp.float32),
-        in_specs=[WHOLE] * len(pieces) + [anywhere()],
-        scratch_shapes=[pltpu.VMEM(trailing.shape, jnp.float32), pltpu.SemaphoreType.DMA((4,))],
-        compiler_params=pltpu.CompilerParams(vmem_limit_bytes=MOST),
-        cost_estimate=FREE,
-        name="products",
-    )(*pieces, trailing)
-
-
-def gram_kernel(masks, near, where_ref, *refs):
-    pieces, others = refs[: len(masks)], refs[len(masks) :]
-    near_sums, trailing, panel_t, mine, keep, give, sums, held, got = others
-    copies = fetch(trailing, held, got)
+def gram_kernel(masks, where_ref, *refs):
+    pieces, panel_t, mine = refs[: len(masks)], refs[-2], refs[-1]
     col, row = where_ref[0], where_ref[1]
     width = pieces[0].shape[0]
     n = width * len(masks)
-
-    def at(mask):
-        return pl.ds(pl.multiple_of((col ^ mask) * width, width), width)
-
     for mask, piece in zip(masks, pieces):
-        panel_t[at(mask), :] = piece[...]
+        panel_t[pl.ds(pl.multiple_of((col ^ mask) * width, width), width), :] = piece[...]
 
     @pl.when(col & 1 == 0)
     def _():
         whole = panel_t[...]
-        mine[...] = dot(whole, whole, (1, 1))
+        high = whole.astype(jnp.bfloat16)
+        rest = whole - high.astype(jnp.float32)
+        middle = rest.astype(jnp.bfloat16)
+        low = (rest - middle.astype(jnp.float32)).astype(jnp.bfloat16)
+        parts = lax.dot_general(
+            jnp.concatenate([high, middle, low], axis=0),
+            jnp.concatenate([high, middle], axis=0),
+            (((1,), (1,)), ((), ())),
+            preferred_element_type=jnp.float32,
+        )
+        small = parts[n : 2 * n, n:] + (parts[2 * n :, :n] + parts[2 * n :, :n].T)
+        mine[...] = parts[:n, :n] + ((parts[n : 2 * n, :n] + parts[:n, n:]) + small)
 
     @pl.when(col & 1 == 1)
     def _():
         mine[...] = jnp.where(row == 0, panel_t[:, :n].T, 0.0)
 
-    far = [(mask, piece) for mask, piece in zip(masks, pieces) if mask not in near]
-    late = product([piece for _, piece in far], held, copies)
-    for i, mask in enumerate(near):
-        sums[at(mask), :] = near_sums[i * width : (i + 1) * width, :]
-    for i, (mask, _) in enumerate(far):
-        sums[at(mask), :] = late[i * width : (i + 1) * width, :]
-    half = sums.shape[1] // 2
-    first = row & 1 == 0
-    keep[...] = jnp.where(first, sums[:, :half], sums[:, half:])
-    give[...] = jnp.where(first, sums[:, half:], sums[:, :half])
-
-
-def gram(where, held, near, near_sums, trailing):
+
+def gram(where, held):
     width, rows = held[0].shape
-    n, cols = width * len(held), trailing.shape[1]
+    n = width * len(held)
+    return pl.pallas_call(
+        lambda *refs: gram_kernel(tuple(held), *refs),
+        out_shape=(jax.ShapeDtypeStruct((n, rows), jnp.float32), jax.ShapeDtypeStruct((n, n), jnp.float32)),
+        in_specs=[SCALAR] + [WHOLE] * len(held),
+        compiler_params=pltpu.CompilerParams(vmem_limit_bytes=8 << 20),
+        cost_estimate=FREE,
+        name="gram",
+    )(where, *held.values())
+
+
+def copy_kernel(x, out):
+    out[...] = x[...]
+
+
+def nearby(x):
+    return pl.pallas_call(
+        copy_kernel,
+        out_shape=jax.ShapeDtypeStruct(x.shape, x.dtype),
+        in_specs=[WHOLE],
+        compiler_params=pltpu.CompilerParams(vmem_limit_bytes=1 << 20),
+        cost_estimate=FREE,
+        name="nearby",
+    )(x)
+
+
+def products_kernel(where_ref, panel_t, trailing, keep, give, left, held, got):
+    copies = fetch(trailing, held, got)
+    n, rows = panel_t.shape
+
+    @pl.when(where_ref[1] >= 0)
+    def _():
+        for i in range(0, rows, n):
+            left[i : i + n, :n], left[i : i + n, n:] = halves(panel_t[:, i : i + n].T)
+        sums = product([panel_t], held, copies)
+        half = sums.shape[1] // 2
+        first = where_ref[1] & 1 == 0
+        keep[...] = jnp.where(first, sums[:, :half], sums[:, half:])
+        give[...] = jnp.where(first, sums[:, half:], sums[:, :half])
+
+
+def products_of(where, panel_t, trailing):
+    (n, rows), cols = panel_t.shape, trailing.shape[1]
     part = jax.ShapeDtypeStruct((n, cols // 2), jnp.float32)
     return pl.pallas_call(
-        lambda *refs: gram_kernel(tuple(held), near, *refs),
-        out_shape=(
-            jax.ShapeDtypeStruct((n, rows), jnp.float32),
-            jax.ShapeDtypeStruct((n, n), jnp.float32),
-            part,
-            part,
-        ),
-        in_specs=[SCALAR] + [WHOLE] * (len(held) + 1) + [anywhere()],
-        scratch_shapes=[
-            pltpu.VMEM((n, cols), jnp.float32),
-            pltpu.VMEM(trailing.shape, jnp.float32),
-            pltpu.SemaphoreType.DMA((4,)),
-        ],
+        products_kernel,
+        out_shape=(part, part, jax.ShapeDtypeStruct((rows, 2 * n), jnp.bfloat16)),
+        in_specs=[SCALAR, WHOLE, anywhere()],
+        scratch_shapes=[pltpu.VMEM(trailing.shape, jnp.float32), pltpu.SemaphoreType.DMA((8,))],
         compiler_params=pltpu.CompilerParams(vmem_limit_bytes=MOST),
-        cost_estimate=FREE,
-        name="gram",
-    )(where, *held.values(), near_sums, trailing)
-
-
-def split_kernel(panel_t, left):
-    n, rows = panel_t.shape
-    for i in range(0, rows, n):
-        high, low = halves(panel_t[:, i : i + n].T)
-        left[i : i + n, :n] = high
-        left[i : i + n, n:] = low
-
-
-def split_rows(panel_t):
-    n, rows = panel_t.shape
-    return pl.pallas_call(
-        split_kernel,
-        out_shape=jax.ShapeDtypeStruct((rows, 2 * n), jnp.bfloat16),
-        in_specs=[WHOLE],
-        compiler_params=pltpu.CompilerParams(vmem_limit_bytes=8 << 20),
-        cost_estimate=FREE,
-        name="split_rows",
-    )(panel_t)
+        cost_estimate=pl.CostEstimate(flops=0, bytes_accessed=11_000_000, transcendentals=0),
+        name="products",
+    )(where, panel_t, trailing)
 
 
 def update_kernel(second, where_ref, left_ref, mixed, trailing, *refs):
     if second:
-        _, updated, high_ref, low_ref, result, sent = refs
+        top_ref, _, updated, high_ref, low_ref, result, sent = refs
     else:
-        pivot, replaced, updated, reflectors, new_left, high_ref, low_ref, result, sent = refs
+        pivot, replaced, updated, reflectors, top_ref, high_ref, low_ref, result, sent = refs
     row = where_ref[1]
     n, half = mixed.shape
     steps, tall = result.shape[0], result.shape[1]
-    mine = row & 1 if not second else 1 - (row & 1)
+    mine = 1 - (row & 1) if second else row & 1
     columns = pl.ds(pl.multiple_of(mine * half, half), half)
+
+    def going(i):
+        return pltpu.make_async_copy(result.at[i], updated.at[pl.ds(i * tall, tall), columns], sent.at[i])
+
+    if not second:
+        top_ref[...] = jnp.where(row == 0, jnp.concatenate(halves(replaced[...]), axis=1), left_ref[:n, :])
     high, low = halves(mixed[...])
     high_ref[:n], high_ref[n:] = high, high
     low_ref[:n], low_ref[n:] = low, low
 
-    def going(i):
-        return pltpu.make_async_copy(result.at[i], updated.at[pl.ds(i * tall, tall), columns], sent.at[i])
-
     def rows_of(i):
         left = left_ref[i * tall : (i + 1) * tall, :]
-        if i == 0 and not second:
-            top = jnp.concatenate(halves(replaced[...]), axis=1)
-            left = jnp.concatenate([jnp.where(row == 0, top, left[:n]), left[n:]], axis=0)
-            new_left[...] = left[:n]
-        return left
+        return jnp.concatenate([top_ref[...], left[n:]], axis=0) if i == 0 else left
 
     def times(left, high, low):
         return jnp.dot(left, high, preferred_element_type=jnp.float32) + jnp.dot(
             left, low, preferred_element_type=jnp.float32
         )
 
-    for i in range(steps):
-        result[i] = trailing[i * tall : (i + 1) * tall, columns] - times(rows_of(i), high_ref[...], low_ref[...])
-        going(i).start()
+    for first in range(0, steps, 2):
+        @pl.when(row >= 0)
+        def _():
+            for i in range(first, first + 2):
+                change = times(rows_of(i), high_ref[...], low_ref[...])
+                result[i] = trailing[i * tall : (i + 1) * tall, columns] - change
+                going(i).start()
+
     if not second:
         width = reflectors.shape[0]
-        own = pivot[...]
-        own = pltpu.roll(own, (n - where_ref[0] * width) % n, 1)
+        own = pltpu.roll(pivot[...], (n - where_ref[0] * width) % n, 1)
         a, b = halves(own)
         a, b = jnp.concatenate([a, a], axis=0), jnp.concatenate([b, b], axis=0)
         for i in range(steps):
-            left = left_ref[i * tall : (i + 1) * tall, :]
-            if i == 0:
-                left = jnp.concatenate([new_left[...], left[n:]], axis=0)
-            reflectors[:, i * tall : (i + 1) * tall] = times(left, a, b).T[:width]
+            reflectors[:, i * tall : (i + 1) * tall] = times(rows_of(i), a, b).T[:width]
     for i in range(steps):
         going(i).wait()
 
 
-def update(where, left, mixed, trailing, pivot, replaced, width):
+def update_call(second, inputs, outs, specs, mixed, trailing, name, aliases):
     n, half = mixed.shape
-    rows, cols = trailing.shape
-    steps = 4
+    rows, _ = trailing.shape
+    steps = 8
     return pl.pallas_call(
-        lambda *refs: update_kernel(False, *refs),
-        out_shape=(
-            jax.ShapeDtypeStruct((rows, cols), jnp.float32),
-            jax.ShapeDtypeStruct((width, rows), jnp.float32),
-            jax.ShapeDtypeStruct((n, 2 * n), jnp.bfloat16),
-        ),
-        in_specs=[SCALAR] + [WHOLE] * 5,
-        out_specs=(anywhere(), WHOLE, WHOLE),
+        lambda *refs: update_kernel(second, *refs),
+        out_shape=outs,
+        in_specs=[SCALAR, WHOLE, WHOLE, WHOLE] + specs,
+        out_specs=(anywhere(),) + (WHOLE,) * (len(outs) - 1),
         scratch_shapes=[pltpu.VMEM((2 * n, half), jnp.bfloat16)] * 2
         + [pltpu.VMEM((steps, rows // steps, half), jnp.float32)]
         + [pltpu.SemaphoreType.DMA((steps,))],
+        input_output_aliases=aliases,
         compiler_params=pltpu.CompilerParams(vmem_limit_bytes=8 << 20),
         cost_estimate=FREE,
-        name="update",
-    )(where, left, mixed, trailing, pivot, replaced)
-
-
-def update_rest(where, left, new_left, mixed, trailing, updated):
-    n, half = mixed.shape
-    rows, cols = trailing.shape
-    steps = 4
-
-    def kernel(where_ref, left_ref, new_left_ref, mixed_ref, trailing_ref, updated_ref, *refs):
-        out, scratch, high, low, result, sent = refs
-        scratch[...] = left_ref[...]
-        scratch[:n, :] = new_left_ref[...]
-        update_kernel(True, where_ref, scratch, mixed_ref, trailing_ref, updated_ref, out, high, low, result, sent)
-
-    return pl.pallas_call(
-        kernel,
-        out_shape=jax.ShapeDtypeStruct((rows, cols), jnp.float32),
-        in_specs=[SCALAR] + [WHOLE] * 4 + [anywhere()],
-        out_specs=anywhere(),
-        scratch_shapes=[pltpu.VMEM((rows, 2 * n), jnp.bfloat16)]
-        + [pltpu.VMEM((2 * n, half), jnp.bfloat16)] * 2
-        + [pltpu.VMEM((steps, rows // steps, half), jnp.float32)]
-        + [pltpu.SemaphoreType.DMA((steps,))],
-        input_output_aliases={5: 0},
-        compiler_params=pltpu.CompilerParams(vmem_limit_bytes=8 << 20),
-        cost_estimate=FREE,
-        name="update_rest",
-    )(where, left, new_left, mixed, trailing, updated)
+        name=name,
+    )(*inputs)
+
+
+def update(where, left, mixed, trailing, pivot, replaced, width):
+    n, rows = mixed.shape[0], trailing.shape[0]
+    outs = (
+        jax.ShapeDtypeStruct(trailing.shape, jnp.float32),
+        jax.ShapeDtypeStruct((width, rows), jnp.float32),
+        jax.ShapeDtypeStruct((n, 2 * n), jnp.bfloat16),
+    )
+    inputs = (where, left, mixed, trailing, pivot, replaced)
+    return update_call(False, inputs, outs, [WHOLE, WHOLE], mixed, trailing, "update", {})
+
+
+def update_rest(where, left, top, mixed, trailing, updated):
+    outs = (jax.ShapeDtypeStruct(trailing.shape, jnp.float32),)
+    inputs = (where, left, mixed, trailing, top, updated)
+    return update_call(True, inputs, outs, [WHOLE, anywhere()], mixed, trailing, "update_rest", {5: 0})[0]
 
 
 def mix(mine, theirs, lead, weight, inv):
@@ -481,44 +470,43 @@
     where = jnp.stack([col, row]).astype(jnp.int32)
     held = {0: own}
     for bit in reversed(bits_of("col")):
-        held.update({mask | bit: swap(piece, "col", bit) for mask, piece in list(held.items())})
+        if bit == 1:
+            far = max(held)
+            own, held[1] = lax.optimization_barrier((own, swap(own, "col", 1)))
+            held[0], held[far] = lax.optimization_barrier((nearby(own), held[far]))
+        held.update({m | bit: swap(piece, "col", bit) for m, piece in list(held.items()) if m | bit not in held})
     n = own.shape[0] * len(held)
     bits = bits_of("row")
-    order = sorted(held)
-    near, far = order[: len(order) // 2], order[len(order) // 2 :]
-
-    odd = row & bits[0] != 0
-    half = trailing.shape[1] // 2
-    left_half, right_half = trailing[:n, :half], trailing[:n, half:]
-    lead_got = swap(jnp.where(odd, left_half, right_half), "row", bits[0])
-    lead = jnp.where(odd, lead_got, left_half)
+    odd, half = row & bits[0] != 0, trailing.shape[1] // 2
+
+    lead, _ = lax.optimization_barrier((trailing[:n], held[1]))
+    keep, give = lax.optimization_barrier(
+        (lead[:, :half], jnp.where(odd, lead[:, :half], lead[:, half:]))
+    )
+    lead = jnp.where(odd, swap(give, "row", bits[0]), keep)
     lead_got = swap(lead, "row", bits[-1])
-    near_sums = near_products([held[m] for m in near], trailing)
-    held[far[0]], near_sums, lead = lax.optimization_barrier((held[far[0]], near_sums, lead))
-    for m in far[1:]:
-        held[m] = swap(held[far[0]], "col", m ^ far[0])
-    panel_t, mine, keep, give = gram(where, held, near, near_sums, trailing)
-    left = split_rows(panel_t)
+    panel_t, mine = gram(where, held)
+    keep, give, left = products_of(where, panel_t, trailing)
     got = swap(give, "row", bits[0])
     for bit in bits[1:-1]:
-        mine = mine + swap(mine, "row", bit)
-    lead_got, got, mine = lax.optimization_barrier((lead_got, got, mine))
+        mine = mine + lax.optimization_barrier((swap(mine, "row", bit), keep))[0]
+    lead_got, mine = lax.optimization_barrier((lead_got, mine))
     lead = jnp.where(row & bits[-1] != 0, lead_got, lead)
+    mine = mine + swap(mine, "row", bits[-1])
+    sums, lead, _ = lax.optimization_barrier((keep + got, lead, mine))
     for bit in reversed(bits[1:-1]):
         lead = jnp.where(row & bit != 0, swap(lead, "row", bit), lead)
-    mine = mine + swap(mine, "row", bits[-1])
-    sums, lead, _ = lax.optimization_barrier((keep + got, lead, mine))
-    mine, left = lax.optimization_barrier((mine + swap(mine, "row", bits[0]), left))
+    mine = mine + swap(mine, "row", bits[0])
     for bit in bits[1:-1]:
         sums = sums + swap(sums, "row", bit)
     theirs = swap(mine, "col", 1)
     last = swap(sums, "row", bits[-1])
     theirs, sums = lax.optimization_barrier((theirs, sums))
-    panel_factor, weight, inv, pivot, replaced = factor(col.astype(jnp.int32).reshape(1) & 1, mine, theirs)
+    panel_factor, weight, inv, pivot, replaced, kept = factor(col.astype(jnp.int32).reshape(1) & 1, mine, theirs, trailing)
     mixed = mix(sums, last, lead, weight, inv)
     other = swap(mixed, "row", bits[0])
-    updated, reflectors, top = update(where, left, mixed, trailing, pivot, replaced, own.shape[0])
-    updated = update_rest(where, left, top, other, trailing, updated)
+    updated, reflectors, top = update(where, left, mixed, kept, pivot, replaced, own.shape[0])
+    updated = update_rest(where, left, top, other, kept, updated)
     return updated, reflectors.T, panel_factor
 
 

time: 55.9 us -> 50.3 us (0.90)
  waiting for transfers between devices: 15.1 us -> 11.1 us
  other arithmetic: 2.13 us -> 0.22 us
  Pallas kernels: 18.3 us -> 16.6 us
  starting transfers between devices: 18.4 us -> 19.5 us
  local copies, waits for them, and re-layouts: 0.96 us -> 1.92 us
    ppermute x14, waiting for transfers between devices: 15.1 us -> 11.1 us  [swap(): lax.ppermute(x, axis, [(i, i ^ mask) for i in range(lax.axis_size(axis))])]
    select_n x2, other arithmetic: 1.95 us -> 0.04 us  [the longest x1 0.02 us: per_device(): jnp.where(odd, lead[:, :half], lead[:, half:])]
    pallas_call x6, Pallas kernels: 17.7 us -> 16 us  [the longest x1 6.36 us: factor(): pl.pallas_call(fetching_factor_kernel, out_shape=(out,) * 5 + (jax.ShapeD...]
    ppermute x14, starting transfers between devices: 18.4 us -> 19.5 us  [swap(): lax.ppermute(x, axis, [(i, i ^ mask) for i in range(lax.axis_size(axis))])]
    slice x0 -> x1, local copies, waits for them, and re-layouts: none -> 0.97 us  [per_device(): lead, _ = lax.optimization_barrier((trailing[:n], held[1]))]
  transfers between devices with their start and end apart: 14 -> 14, of which waited for: 8 -> 6; matrix products, arithmetic and copies ran while one was open for 2% -> 2% of each run, Pallas kernels for 27% -> 27%
where the time goes in v3:
time: 50.3 us; the launch traced here: 50.2 us
  starting transfers between devices  19.5 us (39%)
  Pallas kernels  16.6 us (33%)
  waiting for transfers between devices  11.1 us (22%)
  local copies, waits for them, and re-layouts  1.92 us (4%)
  between operations  0.78 us (2%)
    ppermute x14, starting transfers between devices, swap(): lax.ppermute(x, axis, [(i, i ^ mask) for i in range(lax.axis_size(axis))])  19.5 us
    ppermute x14, waiting for transfers between devices, swap(): lax.ppermute(x, axis, [(i, i ^ mask) for i in range(lax.axis_size(axis))])  11.1 us
    pallas_call x1, Pallas kernels, factor(): pl.pallas_call(fetching_factor_kernel, out_shape=(out,) * 5 + (jax.ShapeD...  6.36 us
    pallas_call x2, Pallas kernels, update_call(): pl.pallas_call(lambda *refs: update_kernel(second, *refs), out_shape=outs...  5.26 us
    pallas_call x1, Pallas kernels, products_of(): pl.pallas_call(products_kernel, out_shape=(part, part, jax.ShapeDtypeStru...  3.03 us
    pallas_call x1, Pallas kernels, gram(): pl.pallas_call(lambda *refs: gram_kernel(tuple(held), *refs), out_shape=(...  1.3 us
  transfers between devices with their start and end apart: 14, of which 6 were waited for; matrix products, arithmetic and copies ran while one was open for 2% of the time, Pallas kernels for 27%

profile of v3, /device:TPU:0, one launch (start us, length us, event | category | flops | bytes accessed | tf_op | source)
XLA Modules:
  0.0 50.2 jit_solution(7926224234293812846)
XLA Ops:
  1.1 2.6 %collective-permute-start.1 = (f32[32,2048]{1,0:T(8,128)}, f32[32,2048]{1,0:T(8,128)S(1)}, u32[]{:S(2)}, u32[]{:S(2)}) collective-permute-start(f32[32,2048]{1,0:T(8,128)} %bitcast.5), channel_id=1, source_target_pairs={{0,2},{1,3},{2,0},{3,1},{4,6},{5,7},{6,4},{7,5},{8,10},{9,11},{10,... | collective-permute-start | bytes 786440 | tf_op jit(solution)/shard_map/ppermute | solution.py:235
  3.7 1.0 %slice.10 = f32[128,512]{1,0:T(8,128)S(1)} slice(f32[2048,512]{1,0:T(8,128)} %trailing.3), slice={[0:128], [0:512]} | slice | bytes 524288 | tf_op jit(solution)/shard_map/slice | solution.py:482
  4.7 1.6 %collective-permute-start.3 = (f32[128,256]{1,0:T(8,128)S(1)}, f32[128,256]{1,0:T(8,128)S(1)}, u32[]{:S(2)}, u32[]{:S(2)}) collective-permute-start(f32[128,256]{1,0:T(8,128)S(1)} %get-tuple-element.38), channel_id=1, source_target_pairs={{0,4},{4,0},{8,12},{12,8},{16,20},{20,16},{24,28},{28,24},{1,5},{5... | collective-permute-start | bytes 393224 | tf_op jit(solution)/shard_map/ppermute | solution.py:235
  6.3 0.9 %copy-done = f32[2048,32]{0,1:T(8,128)S(1)} copy-done((f32[2048,32]{0,1:T(8,128)S(1)}, f32[2048,32]{0,1:T(8,128)}, u32[]{:S(2)}) %copy-start) | copy-done | bytes 262168
  7.3 3.5 %collective-permute-done.1.refs_2_ = f32[32,2048]{1,0:T(8,128)S(1)} collective-permute-done((f32[32,2048]{1,0:T(8,128)}, f32[32,2048]{1,0:T(8,128)S(1)}, u32[]{:S(2)}, u32[]{:S(2)}) %collective-permute-start.1) | collective-permute-done | bytes 262176 | tf_op jit(solution)/shard_map/ppermute | solution.py:235
  10.8 2.9 %collective-permute-start.4 = (f32[128,256]{1,0:T(8,128)S(1)}, f32[128,256]{1,0:T(8,128)S(1)}, u32[]{:S(2)}, u32[]{:S(2)}) collective-permute-start(f32[128,256]{1,0:T(8,128)S(1)} %broadcast_select_fusion.2), channel_id=1, source_target_pairs={{0,16},{4,20},{8,24},{12,28},{16,0},{20,4},{24,8},{28,12},{1,17},{... | collective-permute-start | bytes 393224 | tf_op jit(solution)/shard_map/ppermute | solution.py:235
  13.8 1.3 %gram.1 = (f32[128,2048]{1,0:T(8,128)S(1)}, f32[128,128]{1,0:T(8,128)S(1)}) custom-call(s32[2]{0:T(128)S(1)} %pad_add_fusion.refs_0_.where_ref, f32[32,2048]{1,0:T(8,128)S(1)} %nearby.1.refs_1_, f32[32,2048]{1,0:T(8,128)S(1)} %collective-permute-done.1.refs_2_, f32[32,2048]{1,0:T(8,128)S(1)} %collective-permute-done.refs_3_, ...), custom_call_target="tpu_custom_call" | custom-call | flops 1 | bytes 1 | tf_op jit(solution)/shard_map/gram/pallas_call | solution.py:310
  15.2 1.6 %collective-permute-start.5 = (f32[128,128]{1,0:T(8,128)S(1)}, f32[128,128]{1,0:T(8,128)S(1)}, u32[]{:S(2)}, u32[]{:S(2)}) collective-permute-start(f32[128,128]{1,0:T(8,128)S(1)} %get-tuple-element.40), channel_id=1, source_target_pairs={{0,8},{4,12},{8,0},{12,4},{16,24},{20,28},{24,16},{28,20},{1,9},{5... | collective-permute-start | bytes 196616 | tf_op jit(solution)/shard_map/ppermute | solution.py:235
  16.8 3.0 %products.1 = (f32[128,256]{1,0:T(8,128)S(1)}, f32[128,256]{1,0:T(8,128)S(1)}, bf16[2048,256]{1,0:T(8,128)(2,1)S(1)}) custom-call(s32[2]{0:T(128)S(1)} %pad_add_fusion.refs_0_.where_ref, f32[128,2048]{1,0:T(8,128)S(1)} %get-tuple-element.35.panel_t, f32[2048,512]{1,0:T(8,128)} %trailing.3), custom_call_target="tpu_custom_call" | custom-call | bytes 11000000 | tf_op jit(solution)/shard_map/products/pallas_call | solution.py:353
  19.8 1.6 %collective-permute-start.9 = (f32[128,256]{1,0:T(8,128)S(1)}, f32[128,256]{1,0:T(8,128)S(1)}, u32[]{:S(2)}, u32[]{:S(2)}) collective-permute-start(f32[128,256]{1,0:T(8,128)S(1)} %get-tuple-element.44), channel_id=1, source_target_pairs={{0,4},{4,0},{8,12},{12,8},{16,20},{20,16},{24,28},{28,24},{1,5},{5... | collective-permute-start | bytes 393224 | tf_op jit(solution)/shard_map/ppermute | solution.py:235
  21.5 1.4 %collective-permute-start.6 = (f32[128,128]{1,0:T(8,128)S(1)}, f32[128,128]{1,0:T(8,128)S(1)}, u32[]{:S(2)}, u32[]{:S(2)}) collective-permute-start(f32[128,128]{1,0:T(8,128)S(1)} %add.15), channel_id=1, source_target_pairs={{0,16},{4,20},{8,24},{12,28},{16,0},{20,4},{24,8},{28,12},{1,17},{... | collective-permute-start | bytes 196616 | tf_op jit(solution)/shard_map/ppermute | solution.py:235
  22.9 4.5 %collective-permute-done.6 = f32[128,128]{1,0:T(8,128)S(1)} collective-permute-done((f32[128,128]{1,0:T(8,128)S(1)}, f32[128,128]{1,0:T(8,128)S(1)}, u32[]{:S(2)}, u32[]{:S(2)}) %collective-permute-start.6) | collective-permute-done | bytes 65568 | tf_op jit(solution)/shard_map/ppermute | solution.py:235
  27.7 1.4 %collective-permute-start.7 = (f32[128,128]{1,0:T(8,128)S(1)}, f32[128,128]{1,0:T(8,128)S(1)}, u32[]{:S(2)}, u32[]{:S(2)}) collective-permute-start(f32[128,128]{1,0:T(8,128)S(1)} %add.16), channel_id=1, source_target_pairs={{0,4},{4,0},{8,12},{12,8},{16,20},{20,16},{24,28},{28,24},{1,5},{5... | collective-permute-start | bytes 196616 | tf_op jit(solution)/shard_map/ppermute | solution.py:235
  29.1 1.9 %collective-permute-start.12 = (f32[128,256]{1,0:T(8,128)S(1)}, f32[128,256]{1,0:T(8,128)S(1)}, u32[]{:S(2)}, u32[]{:S(2)}) collective-permute-start(f32[128,256]{1,0:T(8,128)S(1)} %broadcast_select_fusion.1), channel_id=1, source_target_pairs={{0,8},{4,12},{8,0},{12,4},{16,24},{20,28},{24,16},{28,20},{1,9},{5... | collective-permute-start | bytes 393224 | tf_op jit(solution)/shard_map/ppermute | solution.py:235
  31.0 0.9 %collective-permute-done.7 = f32[128,128]{1,0:T(8,128)S(1)} collective-permute-done((f32[128,128]{1,0:T(8,128)S(1)}, f32[128,128]{1,0:T(8,128)S(1)}, u32[]{:S(2)}, u32[]{:S(2)}) %collective-permute-start.7) | collective-permute-done | bytes 65568 | tf_op jit(solution)/shard_map/ppermute | solution.py:235
  32.1 1.0 %collective-permute-done.10 = f32[128,256]{1,0:T(8,128)S(1)} collective-permute-done((f32[128,256]{1,0:T(8,128)S(1)}, f32[128,256]{1,0:T(8,128)S(1)}, u32[]{:S(2)}, u32[]{:S(2)}) %collective-permute-start.10) | collective-permute-done | bytes 131104 | tf_op jit(solution)/shard_map/ppermute | solution.py:235
  33.1 2.1 %collective-permute-start.11 = (f32[128,256]{1,0:T(8,128)S(1)}, f32[128,256]{1,0:T(8,128)S(1)}, u32[]{:S(2)}, u32[]{:S(2)}) collective-permute-start(f32[128,256]{1,0:T(8,128)S(1)} %add.19.mine), channel_id=1, source_target_pairs={{0,16},{4,20},{8,24},{12,28},{16,0},{20,4},{24,8},{28,12},{1,17},{... | collective-permute-start | bytes 393224 | tf_op jit(solution)/shard_map/ppermute | solution.py:235
  35.2 6.4 %factor.1 = (f32[128,128]{1,0:T(8,128)}, f32[128,128]{1,0:T(8,128)S(1)}, f32[128,128]{1,0:T(8,128)S(1)}, f32[128,128]{1,0:T(8,128)S(1)}, f32[128,128]{1,0:T(8,128)S(1)}, /*index=5*/f32[2048,512]{1,0:T(8,128)S(1)}) custom-call(s32[1]{0:T(128)S(6)} %and.17.odd, f32[128,128]{1,0:T(8,128)S(1)} %add.17.mine, f32[128,128]{1,0:T(8,128)S(1)} %collective-permute-done.8.theirs, ...), custom_call_target="tpu_custom_call" | custom-call | bytes 22000000 | tf_op jit(solution)/shard_map/factor/pallas_call | solution.py:223
  41.6 0.5 %collective-permute-done.11.theirs = f32[128,256]{1,0:T(8,128)S(1)} collective-permute-done((f32[128,256]{1,0:T(8,128)S(1)}, f32[128,256]{1,0:T(8,128)S(1)}, u32[]{:S(2)}, u32[]{:S(2)}) %collective-permute-start.11) | collective-permute-done | bytes 131104 | tf_op jit(solution)/shard_map/ppermute | solution.py:235
  42.1 0.7 %mix.1.refs_2_ = f32[128,256]{1,0:T(8,128)S(1)} custom-call(f32[128,256]{1,0:T(8,128)S(1)} %add.19.mine, f32[128,256]{1,0:T(8,128)S(1)} %collective-permute-done.11.theirs, f32[128,256]{1,0:T(8,128)S(1)} %broadcast_select_fusion.lead, f32[128,128]{1,0:T(8,128)S(1)} %get-tuple-element.50.weight, f32[128,128]{1,0:T(8,128)S(1)} %get-tuple-element.51.inv), custom_call_target="tpu_custom_call" | custom-call | flops 1 | bytes 1 | tf_op jit(solution)/shard_map/mix/pallas_call | solution.py:453
  42.8 1.6 %collective-permute-start.13 = (f32[128,256]{1,0:T(8,128)S(1)}, f32[128,256]{1,0:T(8,128)S(1)}, u32[]{:S(2)}, u32[]{:S(2)}) collective-permute-start(f32[128,256]{1,0:T(8,128)S(1)} %mix.1.refs_2_), channel_id=1, source_target_pairs={{0,4},{4,0},{8,12},{12,8},{16,20},{20,16},{24,28},{28,24},{1,5},{5... | collective-permute-start | bytes 393224 | tf_op jit(solution)/shard_map/ppermute | solution.py:235
  44.3 3.0 %update.1 = (f32[2048,512]{1,0:T(8,128)}, f32[32,2048]{1,0:T(8,128)}, bf16[128,256]{1,0:T(8,128)(2,1)S(1)}) custom-call(s32[2]{0:T(128)S(1)} %pad_add_fusion.refs_0_.where_ref, bf16[2048,256]{1,0:T(8,128)(2,1)S(1)} %get-tuple-element.36.refs_1_, f32[128,256]{1,0:T(8,128)S(1)} %mix.1.refs_2_, f32[2048,512]{1,0:T(8,128)S(1)} %get-tuple-element.52.refs_3_, ...), custom_call_target="tpu_custom_call" | custom-call | flops 1 | bytes 1 | tf_op jit(solution)/shard_map/update/pallas_call | solution.py:416
  47.4 0.5 %collective-permute-done.13.refs_2_ = f32[128,256]{1,0:T(8,128)S(1)} collective-permute-done((f32[128,256]{1,0:T(8,128)S(1)}, f32[128,256]{1,0:T(8,128)S(1)}, u32[]{:S(2)}, u32[]{:S(2)}) %collective-permute-start.13) | collective-permute-done | bytes 131104 | tf_op jit(solution)/shard_map/ppermute | solution.py:235
  47.9 2.3 %update_rest.1 = f32[2048,512]{1,0:T(8,128)} custom-call(s32[2]{0:T(128)S(1)} %pad_add_fusion.refs_0_.where_ref, bf16[2048,256]{1,0:T(8,128)(2,1)S(1)} %get-tuple-element.36.refs_1_, f32[128,256]{1,0:T(8,128)S(1)} %collective-permute-done.13.refs_2_, f32[2048,512]{1,0:T(8,128)S(1)} %get-tuple-element.52.refs_3_, ...), custom_call_target="tpu_custom_call", output_to_operand_aliasing={{}: (5, {})} | custom-call | flops 1 | bytes 1 | tf_op jit(solution)/shard_map/update_rest/pallas_call | solution.py:416
  (24 shorter events, 1.1 us)
Async XLA Ops:
  0.6 4.1 %collective-permute-start = (f32[32,2048]{1,0:T(8,128)}, f32[32,2048]{1,0:T(8,128)S(1)}, u32[]{:S(2)}, u32[]{:S(2)}) collective-permute-start(f32[32,2048]{1,0:T(8,128)} %bitcast.4), channel_id=1, source_target_pairs={{0,1},{1,0},{2,3},{3,2},{4,5},{5,4},{6,7},{7,6},{8,9},{9,8},{10,11... | collective-permute-start | bytes 786440 | tf_op jit(solution)/shard_map/ppermute | solution.py:235
  1.1 9.7 %collective-permute-start.1 = (f32[32,2048]{1,0:T(8,128)}, f32[32,2048]{1,0:T(8,128)S(1)}, u32[]{:S(2)}, u32[]{:S(2)}) collective-permute-start(f32[32,2048]{1,0:T(8,128)} %bitcast.5), channel_id=1, source_target_pairs={{0,2},{1,3},{2,0},{3,1},{4,6},{5,7},{6,4},{7,5},{8,10},{9,11},{10,... | collective-permute-start | bytes 786440 | tf_op jit(solution)/shard_map/ppermute | solution.py:235
  4.7 6.1 %collective-permute-start.3 = (f32[128,256]{1,0:T(8,128)S(1)}, f32[128,256]{1,0:T(8,128)S(1)}, u32[]{:S(2)}, u32[]{:S(2)}) collective-permute-start(f32[128,256]{1,0:T(8,128)S(1)} %get-tuple-element.38), channel_id=1, source_target_pairs={{0,4},{4,0},{8,12},{12,8},{16,20},{20,16},{24,28},{28,24},{1,5},{5... | collective-permute-start | bytes 393224 | tf_op jit(solution)/shard_map/ppermute | solution.py:235
  6.3 0.9 %copy-start = (f32[2048,32]{0,1:T(8,128)S(1)}, f32[2048,32]{0,1:T(8,128)}, u32[]{:S(2)}) copy-start(f32[2048,32]{0,1:T(8,128)} %param.2) | copy-start | bytes 786436
  10.8 3.0 %collective-permute-start.2 = (f32[32,2048]{1,0:T(8,128)S(1)}, f32[32,2048]{1,0:T(8,128)S(1)}, u32[]{:S(2)}, u32[]{:S(2)}) collective-permute-start(f32[32,2048]{1,0:T(8,128)S(1)} %collective-permute-done.1.refs_2_), channel_id=1, source_target_pairs={{0,1},{1,0},{2,3},{3,2},{4,5},{5,4},{6,7},{7,6},{8,9},{9,8},{10,11... | collective-permute-start | bytes 786440 | tf_op jit(solution)/shard_map/ppermute | solution.py:235
  10.8 10.6 %collective-permute-start.4 = (f32[128,256]{1,0:T(8,128)S(1)}, f32[128,256]{1,0:T(8,128)S(1)}, u32[]{:S(2)}, u32[]{:S(2)}) collective-permute-start(f32[128,256]{1,0:T(8,128)S(1)} %broadcast_select_fusion.2), channel_id=1, source_target_pairs={{0,16},{4,20},{8,24},{12,28},{16,0},{20,4},{24,8},{28,12},{1,17},{... | collective-permute-start | bytes 393224 | tf_op jit(solution)/shard_map/ppermute | solution.py:235
  15.2 6.3 %collective-permute-start.5 = (f32[128,128]{1,0:T(8,128)S(1)}, f32[128,128]{1,0:T(8,128)S(1)}, u32[]{:S(2)}, u32[]{:S(2)}) collective-permute-start(f32[128,128]{1,0:T(8,128)S(1)} %get-tuple-element.40), channel_id=1, source_target_pairs={{0,8},{4,12},{8,0},{12,4},{16,24},{20,28},{24,16},{28,20},{1,9},{5... | collective-permute-start | bytes 196616 | tf_op jit(solution)/shard_map/ppermute | solution.py:235
  19.8 7.6 %collective-permute-start.9 = (f32[128,256]{1,0:T(8,128)S(1)}, f32[128,256]{1,0:T(8,128)S(1)}, u32[]{:S(2)}, u32[]{:S(2)}) collective-permute-start(f32[128,256]{1,0:T(8,128)S(1)} %get-tuple-element.44), channel_id=1, source_target_pairs={{0,4},{4,0},{8,12},{12,8},{16,20},{20,16},{24,28},{28,24},{1,5},{5... | collective-permute-start | bytes 393224 | tf_op jit(solution)/shard_map/ppermute | solution.py:235
  21.5 5.9 %collective-permute-start.6 = (f32[128,128]{1,0:T(8,128)S(1)}, f32[128,128]{1,0:T(8,128)S(1)}, u32[]{:S(2)}, u32[]{:S(2)}) collective-permute-start(f32[128,128]{1,0:T(8,128)S(1)} %add.15), channel_id=1, source_target_pairs={{0,16},{4,20},{8,24},{12,28},{16,0},{20,4},{24,8},{28,12},{1,17},{... | collective-permute-start | bytes 196616 | tf_op jit(solution)/shard_map/ppermute | solution.py:235
  27.4 5.6 %collective-permute-start.10 = (f32[128,256]{1,0:T(8,128)S(1)}, f32[128,256]{1,0:T(8,128)S(1)}, u32[]{:S(2)}, u32[]{:S(2)}) collective-permute-start(f32[128,256]{1,0:T(8,128)S(1)} %add.18), channel_id=1, source_target_pairs={{0,8},{4,12},{8,0},{12,4},{16,24},{20,28},{24,16},{28,20},{1,9},{5... | collective-permute-start | bytes 393224 | tf_op jit(solution)/shard_map/ppermute | solution.py:235
  27.7 4.3 %collective-permute-start.7 = (f32[128,128]{1,0:T(8,128)S(1)}, f32[128,128]{1,0:T(8,128)S(1)}, u32[]{:S(2)}, u32[]{:S(2)}) collective-permute-start(f32[128,128]{1,0:T(8,128)S(1)} %add.16), channel_id=1, source_target_pairs={{0,4},{4,0},{8,12},{12,8},{16,20},{20,16},{24,28},{28,24},{1,5},{5... | collective-permute-start | bytes 196616 | tf_op jit(solution)/shard_map/ppermute | solution.py:235
  29.1 12.4 %collective-permute-start.12 = (f32[128,256]{1,0:T(8,128)S(1)}, f32[128,256]{1,0:T(8,128)S(1)}, u32[]{:S(2)}, u32[]{:S(2)}) collective-permute-start(f32[128,256]{1,0:T(8,128)S(1)} %broadcast_select_fusion.1), channel_id=1, source_target_pairs={{0,8},{4,12},{8,0},{12,4},{16,24},{20,28},{24,16},{28,20},{1,9},{5... | collective-permute-start | bytes 393224 | tf_op jit(solution)/shard_map/ppermute | solution.py:235
  32.0 3.2 %collective-permute-start.8 = (f32[128,128]{1,0:T(8,128)S(1)}, f32[128,128]{1,0:T(8,128)S(1)}, u32[]{:S(2)}, u32[]{:S(2)}) collective-permute-start(f32[128,128]{1,0:T(8,128)S(1)} %add.17.mine), channel_id=1, source_target_pairs={{0,1},{1,0},{2,3},{3,2},{4,5},{5,4},{6,7},{7,6},{8,9},{9,8},{10,11... | collective-permute-start | bytes 196616 | tf_op jit(solution)/shard_map/ppermute | solution.py:235
  33.1 9.0 %collective-permute-start.11 = (f32[128,256]{1,0:T(8,128)S(1)}, f32[128,256]{1,0:T(8,128)S(1)}, u32[]{:S(2)}, u32[]{:S(2)}) collective-permute-start(f32[128,256]{1,0:T(8,128)S(1)} %add.19.mine), channel_id=1, source_target_pairs={{0,16},{4,20},{8,24},{12,28},{16,0},{20,4},{24,8},{28,12},{1,17},{... | collective-permute-start | bytes 393224 | tf_op jit(solution)/shard_map/ppermute | solution.py:235
  42.8 5.1 %collective-permute-start.13 = (f32[128,256]{1,0:T(8,128)S(1)}, f32[128,256]{1,0:T(8,128)S(1)}, u32[]{:S(2)}, u32[]{:S(2)}) collective-permute-start(f32[128,256]{1,0:T(8,128)S(1)} %mix.1.refs_2_), channel_id=1, source_target_pairs={{0,4},{4,0},{8,12},{12,8},{16,20},{20,16},{24,28},{28,24},{1,5},{5... | collective-permute-start | bytes 393224 | tf_op jit(solution)/shard_map/ppermute | solution.py:235

commit v4 on v3

--- a/solution.py
+++ b/solution.py
@@ -11,6 +11,7 @@
 HIGHEST, HIGH = lax.Precision.HIGHEST, lax.Precision.HIGH
 MOST = 60 << 20
 MOST = 50 << 20
+PIECES = 1
 FREE = pl.CostEstimate(flops=1, bytes_accessed=1, transcendentals=0)
 SCALAR = pl.BlockSpec(memory_space=pltpu.SMEM)
 WHOLE = pl.BlockSpec(memory_space=pltpu.VMEM)
@@ -28,7 +29,9 @@
         step()
 
 
-def factor_kernel(even_ref, mine_ref, theirs_ref, panel_factor_ref, weight_ref, inv_ref, pivot_ref, replaced_ref, g, d, lower, upper, lead_ref):
+def factor_kernel(
+    even_ref, mine_ref, theirs_ref, panel_factor_ref, inv_ref, pivot_ref, replaced_ref, g, d, lower, upper, lead_ref, weight_ref
+):
     n = mine_ref.shape[0]
     slabs = n // SUB
     sub = lax.broadcasted_iota(jnp.int32, (SUB, n), 0)
@@ -200,13 +203,14 @@
         interleave([s for s in streams if s])
         for step in after:
             step()
-    inv_ref[...] = d[...]
+    inv_ref[:, :n] = d[...]
+    inv_ref[:, n:] = -times(d[...], weight_ref[...])
     pivot_ref[...] = times(d[...], lower[...])
 
 
 def fetching_factor_kernel(odd, mine, theirs, trailing, *refs):
-    *outs, held = refs[:6]
-    *scratch, got = refs[6:]
+    *outs, held = refs[:5]
+    *scratch, got = refs[5:]
     copy = pltpu.make_async_copy(trailing, held, got.at[0])
     copy.start()
 
@@ -222,9 +226,15 @@
     out = jax.ShapeDtypeStruct((n, n), jnp.float32)
     return pl.pallas_call(
         fetching_factor_kernel,
-        out_shape=(out,) * 5 + (jax.ShapeDtypeStruct(trailing.shape, jnp.float32),),
+        out_shape=(
+            out,
+            jax.ShapeDtypeStruct((n, 2 * n), jnp.float32),
+            out,
+            out,
+            jax.ShapeDtypeStruct(trailing.shape, jnp.float32),
+        ),
         in_specs=[SCALAR, WHOLE, WHOLE, anywhere()],
-        scratch_shapes=[pltpu.VMEM((n, n), jnp.float32)] * 5 + [pltpu.SemaphoreType.DMA((1,))],
+        scratch_shapes=[pltpu.VMEM((n, n), jnp.float32)] * 6 + [pltpu.SemaphoreType.DMA((1,))],
         compiler_params=pltpu.CompilerParams(vmem_limit_bytes=47 << 20),
         cost_estimate=pl.CostEstimate(flops=0, bytes_accessed=22_000_000, transcendentals=0),
         name="factor",
@@ -361,23 +371,25 @@
     )(where, panel_t, trailing)
 
 
-def update_kernel(second, where_ref, left_ref, mixed, trailing, *refs):
+def update_kernel(pieces, second, where_ref, left_ref, trailing, *refs):
+    mixed, refs = refs[: len(pieces)], refs[len(pieces) :]
     if second:
         top_ref, _, updated, high_ref, low_ref, result, sent = refs
     else:
         pivot, replaced, updated, reflectors, top_ref, high_ref, low_ref, result, sent = refs
     row = where_ref[1]
-    n, half = mixed.shape
+    n, width = mixed[0].shape
     steps, tall = result.shape[0], result.shape[1]
     mine = 1 - (row & 1) if second else row & 1
-    columns = pl.ds(pl.multiple_of(mine * half, half), half)
+    first_piece = pl.multiple_of(mine * (PIECES * width) + pieces[0] * width, width)
+    columns = pl.ds(first_piece, len(pieces) * width)
 
     def going(i):
         return pltpu.make_async_copy(result.at[i], updated.at[pl.ds(i * tall, tall), columns], sent.at[i])
 
     if not second:
         top_ref[...] = jnp.where(row == 0, jnp.concatenate(halves(replaced[...]), axis=1), left_ref[:n, :])
-    high, low = halves(mixed[...])
+    high, low = halves(jnp.concatenate([piece[...] for piece in mixed], axis=1))
     high_ref[:n], high_ref[n:] = high, high
     low_ref[:n], low_ref[n:] = low, low
 
@@ -409,55 +421,63 @@
         going(i).wait()
 
 
-def update_call(second, inputs, outs, specs, mixed, trailing, name, aliases):
-    n, half = mixed.shape
-    rows, _ = trailing.shape
-    steps = 8
+def update_call(pieces, second, where, left, trailing, mixed, inputs, outs, specs, name, aliases):
+    n, width = mixed[0].shape
+    width *= len(pieces)
+    rows, steps = trailing.shape[0], 8
     return pl.pallas_call(
-        lambda *refs: update_kernel(second, *refs),
+        lambda *refs: update_kernel(pieces, second, *refs),
         out_shape=outs,
-        in_specs=[SCALAR, WHOLE, WHOLE, WHOLE] + specs,
+        in_specs=[SCALAR, WHOLE, WHOLE] + [WHOLE] * len(pieces) + specs,
         out_specs=(anywhere(),) + (WHOLE,) * (len(outs) - 1),
-        scratch_shapes=[pltpu.VMEM((2 * n, half), jnp.bfloat16)] * 2
-        + [pltpu.VMEM((steps, rows // steps, half), jnp.float32)]
+        scratch_shapes=[pltpu.VMEM((2 * n, width), jnp.bfloat16)] * 2
+        + [pltpu.VMEM((steps, rows // steps, width), jnp.float32)]
         + [pltpu.SemaphoreType.DMA((steps,))],
         input_output_aliases=aliases,
         compiler_params=pltpu.CompilerParams(vmem_limit_bytes=8 << 20),
         cost_estimate=FREE,
         name=name,
-    )(*inputs)
+    )(where, left, trailing, *mixed, *inputs)
 
 
 def update(where, left, mixed, trailing, pivot, replaced, width):
-    n, rows = mixed.shape[0], trailing.shape[0]
+    n, rows = mixed[0].shape[0], trailing.shape[0]
     outs = (
         jax.ShapeDtypeStruct(trailing.shape, jnp.float32),
         jax.ShapeDtypeStruct((width, rows), jnp.float32),
         jax.ShapeDtypeStruct((n, 2 * n), jnp.bfloat16),
     )
-    inputs = (where, left, mixed, trailing, pivot, replaced)
-    return update_call(False, inputs, outs, [WHOLE, WHOLE], mixed, trailing, "update", {})
-
-
-def update_rest(where, left, top, mixed, trailing, updated):
+    pieces = tuple(range(PIECES))
+    return update_call(
+        pieces, False, where, left, trailing, mixed, (pivot, replaced), outs, [WHOLE, WHOLE], "update", {}
+    )
+
+
+def update_rest(piece, where, left, top, mixed, trailing, updated):
     outs = (jax.ShapeDtypeStruct(trailing.shape, jnp.float32),)
-    inputs = (where, left, mixed, trailing, top, updated)
-    return update_call(True, inputs, outs, [WHOLE, anywhere()], mixed, trailing, "update_rest", {5: 0})[0]
-
-
-def mix(mine, theirs, lead, weight, inv):
-    def kernel(mine, theirs, lead, weight, inv, mixed):
-        rest = lead[...] - dot(weight[...], mine[...] + theirs[...], (1, 0))
-        mixed[...] = dot(inv[...], rest, (1, 0))
-
+    inputs = (top, updated)
+    return update_call(
+        (piece,), True, where, left, trailing, (mixed,), inputs, outs, [WHOLE, anywhere()], "update_rest", {5: 0}
+    )[0]
+
+
+def mix(mine, theirs, lead, inv):
+    def kernel(mine, theirs, lead, inv, *outs):
+        right = jnp.concatenate([lead[...], mine[...] + theirs[...]], axis=0)
+        mixed = dot(inv[...], right, (1, 0))
+        width = outs[0].shape[1]
+        for i, out in enumerate(outs):
+            out[...] = mixed[:, i * width : (i + 1) * width]
+
+    n, half = mine.shape
     return pl.pallas_call(
         kernel,
-        out_shape=jax.ShapeDtypeStruct(mine.shape, jnp.float32),
-        in_specs=[WHOLE] * 5,
+        out_shape=(jax.ShapeDtypeStruct((n, half // PIECES), jnp.float32),) * PIECES,
+        in_specs=[WHOLE] * 4,
         compiler_params=pltpu.CompilerParams(vmem_limit_bytes=3 << 20),
         cost_estimate=FREE,
         name="mix",
-    )(mine, theirs, lead, weight, inv)
+    )(mine, theirs, lead, inv)
 
 
 def after(x, *others):
@@ -484,29 +504,32 @@
         (lead[:, :half], jnp.where(odd, lead[:, :half], lead[:, half:]))
     )
     lead = jnp.where(odd, swap(give, "row", bits[0]), keep)
-    lead_got = swap(lead, "row", bits[-1])
+    for bit in bits[1:-1]:
+        lead = jnp.where(row & bit != 0, swap(lead, "row", bit), lead)
     panel_t, mine = gram(where, held)
     keep, give, left = products_of(where, panel_t, trailing)
     got = swap(give, "row", bits[0])
     for bit in bits[1:-1]:
         mine = mine + lax.optimization_barrier((swap(mine, "row", bit), keep))[0]
-    lead_got, mine = lax.optimization_barrier((lead_got, mine))
-    lead = jnp.where(row & bits[-1] != 0, lead_got, lead)
-    mine = mine + swap(mine, "row", bits[-1])
-    sums, lead, _ = lax.optimization_barrier((keep + got, lead, mine))
-    for bit in reversed(bits[1:-1]):
-        lead = jnp.where(row & bit != 0, swap(lead, "row", bit), lead)
+    lead, mine = lax.optimization_barrier((lead, mine))
+    got_z = swap(mine, "row", bits[-1])
+    mine = mine + got_z
+    sums, lead, mine = lax.optimization_barrier((keep + got, lead, mine))
+    lead_got = swap(lead, "row", bits[-1])
     mine = mine + swap(mine, "row", bits[0])
     for bit in bits[1:-1]:
         sums = sums + swap(sums, "row", bit)
     theirs = swap(mine, "col", 1)
     last = swap(sums, "row", bits[-1])
     theirs, sums = lax.optimization_barrier((theirs, sums))
-    panel_factor, weight, inv, pivot, replaced, kept = factor(col.astype(jnp.int32).reshape(1) & 1, mine, theirs, trailing)
-    mixed = mix(sums, last, lead, weight, inv)
-    other = swap(mixed, "row", bits[0])
+    lead = jnp.where(row & bits[-1] != 0, lead_got, lead)
+    odd_col = col.astype(jnp.int32).reshape(1) & 1
+    panel_factor, inv, pivot, replaced, kept = factor(odd_col, mine, theirs, trailing)
+    mixed = mix(sums, last, lead, inv)
+    others = [swap(piece, "row", bits[0]) for piece in mixed]
     updated, reflectors, top = update(where, left, mixed, kept, pivot, replaced, own.shape[0])
-    updated = update_rest(where, left, top, other, kept, updated)
+    for i, other in enumerate(others):
+        updated = update_rest(i, where, left, top, other, kept, updated)
     return updated, reflectors.T, panel_factor
 
 

time: 50.3 us -> 48.2 us (0.958)
  starting transfers between devices: 19.5 us -> 16.8 us
  waiting for transfers between devices: 11.1 us -> 12 us
    ppermute x14, starting transfers between devices: 19.5 us -> 16.8 us  [swap(): lax.ppermute(x, axis, [(i, i ^ mask) for i in range(lax.axis_size(axis))])]
    ppermute x14, waiting for transfers between devices: 11.1 us -> 12 us  [swap(): lax.ppermute(x, axis, [(i, i ^ mask) for i in range(lax.axis_size(axis))])]
  transfers between devices with their start and end apart: 14 -> 14, of which waited for: 6 -> 6; matrix products, arithmetic and copies ran while one was open for 2% -> 2% of each run, Pallas kernels for 27% -> 29%
where the time goes in v4:
time: 48.2 us; the launch traced here: 48 us
  starting transfers between devices  16.8 us (35%)
  Pallas kernels  16.2 us (34%)
  waiting for transfers between devices  12 us (25%)
  local copies, waits for them, and re-layouts  1.92 us (4%)
  between operations  0.79 us (2%)
    ppermute x14, starting transfers between devices, swap(): lax.ppermute(x, axis, [(i, i ^ mask) for i in range(lax.axis_size(axis))])  16.8 us
    ppermute x14, waiting for transfers between devices, swap(): lax.ppermute(x, axis, [(i, i ^ mask) for i in range(lax.axis_size(axis))])  12 us
    pallas_call x1, Pallas kernels, factor(): pl.pallas_call(fetching_factor_kernel, out_shape=(out, jax.ShapeDtypeStru...  6.34 us
    pallas_call x2, Pallas kernels, update_call(): pl.pallas_call(lambda *refs: update_kernel(pieces, second, *refs), out_sh...  5.26 us
    pallas_call x1, Pallas kernels, products_of(): pl.pallas_call(products_kernel, out_shape=(part, part, jax.ShapeDtypeStru...  3.03 us
    pallas_call x1, Pallas kernels, gram(): pl.pallas_call(lambda *refs: gram_kernel(tuple(held), *refs), out_shape=(...  1.3 us
    slice x1, local copies, waits for them, and re-layouts, per_device(): lead, _ = lax.optimization_barrier((trailing[:n], held[1]))  0.97 us
  transfers between devices with their start and end apart: 14, of which 6 were waited for; matrix products, arithmetic and copies ran while one was open for 2% of the time, Pallas kernels for 29%

profile of v4, /device:TPU:0, one launch (start us, length us, event | category | flops | bytes accessed | tf_op | source)
XLA Modules:
  0.0 48.0 jit_solution(14621425290586990743)
XLA Ops:
  0.6 0.5 %collective-permute-start = (f32[32,2048]{1,0:T(8,128)}, f32[32,2048]{1,0:T(8,128)S(1)}, u32[]{:S(2)}, u32[]{:S(2)}) collective-permute-start(f32[32,2048]{1,0:T(8,128)} %bitcast.4), channel_id=1, source_target_pairs={{0,1},{1,0},{2,3},{3,2},{4,5},{5,4},{6,7},{7,6},{8,9},{9,8},{10,11... | collective-permute-start | bytes 786440 | tf_op jit(solution)/shard_map/ppermute | solution.py:245
  1.1 2.6 %collective-permute-start.1 = (f32[32,2048]{1,0:T(8,128)}, f32[32,2048]{1,0:T(8,128)S(1)}, u32[]{:S(2)}, u32[]{:S(2)}) collective-permute-start(f32[32,2048]{1,0:T(8,128)} %bitcast.5), channel_id=1, source_target_pairs={{0,2},{1,3},{2,0},{3,1},{4,6},{5,7},{6,4},{7,5},{8,10},{9,11},{10,... | collective-permute-start | bytes 786440 | tf_op jit(solution)/shard_map/ppermute | solution.py:245
  3.7 1.0 %slice.10 = f32[128,512]{1,0:T(8,128)S(1)} slice(f32[2048,512]{1,0:T(8,128)} %trailing.3), slice={[0:128], [0:512]} | slice | bytes 524288 | tf_op jit(solution)/shard_map/slice | solution.py:502
  4.7 1.6 %collective-permute-start.4 = (f32[128,256]{1,0:T(8,128)S(1)}, f32[128,256]{1,0:T(8,128)S(1)}, u32[]{:S(2)}, u32[]{:S(2)}) collective-permute-start(f32[128,256]{1,0:T(8,128)S(1)} %get-tuple-element.40), channel_id=1, source_target_pairs={{0,4},{4,0},{8,12},{12,8},{16,20},{20,16},{24,28},{28,24},{1,5},{5... | collective-permute-start | bytes 393224 | tf_op jit(solution)/shard_map/ppermute | solution.py:245
  6.3 0.9 %copy-done = f32[2048,32]{0,1:T(8,128)S(1)} copy-done((f32[2048,32]{0,1:T(8,128)S(1)}, f32[2048,32]{0,1:T(8,128)}, u32[]{:S(2)}) %copy-start) | copy-done | bytes 262168
  7.3 3.5 %collective-permute-done.1.refs_2_ = f32[32,2048]{1,0:T(8,128)S(1)} collective-permute-done((f32[32,2048]{1,0:T(8,128)}, f32[32,2048]{1,0:T(8,128)S(1)}, u32[]{:S(2)}, u32[]{:S(2)}) %collective-permute-start.1) | collective-permute-done | bytes 262176 | tf_op jit(solution)/shard_map/ppermute | solution.py:245
  10.8 1.9 %collective-permute-start.5 = (f32[128,256]{1,0:T(8,128)S(1)}, f32[128,256]{1,0:T(8,128)S(1)}, u32[]{:S(2)}, u32[]{:S(2)}) collective-permute-start(f32[128,256]{1,0:T(8,128)S(1)} %broadcast_select_fusion.1), channel_id=1, source_target_pairs={{0,8},{4,12},{8,0},{12,4},{16,24},{20,28},{24,16},{28,20},{1,9},{5... | collective-permute-start | bytes 393224 | tf_op jit(solution)/shard_map/ppermute | solution.py:245
  12.8 1.3 %gram.1 = (f32[128,2048]{1,0:T(8,128)S(1)}, f32[128,128]{1,0:T(8,128)S(1)}) custom-call(s32[2]{0:T(128)S(1)} %pad_add_fusion.refs_0_.where_ref, f32[32,2048]{1,0:T(8,128)S(1)} %nearby.1.refs_1_, f32[32,2048]{1,0:T(8,128)S(1)} %collective-permute-done.1.refs_2_, f32[32,2048]{1,0:T(8,128)S(1)} %collective-permute-done.refs_3_, ...), custom_call_target="tpu_custom_call" | custom-call | flops 1 | bytes 1 | tf_op jit(solution)/shard_map/gram/pallas_call | solution.py:320
  14.1 1.4 %collective-permute-start.6 = (f32[128,128]{1,0:T(8,128)S(1)}, f32[128,128]{1,0:T(8,128)S(1)}, u32[]{:S(2)}, u32[]{:S(2)}) collective-permute-start(f32[128,128]{1,0:T(8,128)S(1)} %get-tuple-element.42), channel_id=1, source_target_pairs={{0,8},{4,12},{8,0},{12,4},{16,24},{20,28},{24,16},{28,20},{1,9},{5... | collective-permute-start | bytes 196616 | tf_op jit(solution)/shard_map/ppermute | solution.py:245
  15.6 3.0 %products.1 = (f32[128,256]{1,0:T(8,128)S(1)}, f32[128,256]{1,0:T(8,128)S(1)}, bf16[2048,256]{1,0:T(8,128)(2,1)S(1)}) custom-call(s32[2]{0:T(128)S(1)} %pad_add_fusion.refs_0_.where_ref, f32[128,2048]{1,0:T(8,128)S(1)} %get-tuple-element.35.panel_t, f32[2048,512]{1,0:T(8,128)} %trailing.3), custom_call_target="tpu_custom_call" | custom-call | bytes 11000000 | tf_op jit(solution)/shard_map/products/pallas_call | solution.py:363
  18.6 1.6 %collective-permute-start.3 = (f32[128,256]{1,0:T(8,128)S(1)}, f32[128,256]{1,0:T(8,128)S(1)}, u32[]{:S(2)}, u32[]{:S(2)}) collective-permute-start(f32[128,256]{1,0:T(8,128)S(1)} %get-tuple-element.38), channel_id=1, source_target_pairs={{0,4},{4,0},{8,12},{12,8},{16,20},{20,16},{24,28},{28,24},{1,5},{5... | collective-permute-start | bytes 393224 | tf_op jit(solution)/shard_map/ppermute | solution.py:245
  20.3 2.7 %collective-permute-start.7 = (f32[128,128]{1,0:T(8,128)S(1)}, f32[128,128]{1,0:T(8,128)S(1)}, u32[]{:S(2)}, u32[]{:S(2)}) collective-permute-start(f32[128,128]{1,0:T(8,128)S(1)} %add.16), channel_id=1, source_target_pairs={{0,16},{4,20},{8,24},{12,28},{16,0},{20,4},{24,8},{28,12},{1,17},{... | collective-permute-start | bytes 196616 | tf_op jit(solution)/shard_map/ppermute | solution.py:245
  22.9 3.3 %collective-permute-done.7 = f32[128,128]{1,0:T(8,128)S(1)} collective-permute-done((f32[128,128]{1,0:T(8,128)S(1)}, f32[128,128]{1,0:T(8,128)S(1)}, u32[]{:S(2)}, u32[]{:S(2)}) %collective-permute-start.7) | collective-permute-done | bytes 65568 | tf_op jit(solution)/shard_map/ppermute | solution.py:245
  26.4 0.7 %collective-permute-start.8 = (f32[128,128]{1,0:T(8,128)S(1)}, f32[128,128]{1,0:T(8,128)S(1)}, u32[]{:S(2)}, u32[]{:S(2)}) collective-permute-start(f32[128,128]{1,0:T(8,128)S(1)} %add.17), channel_id=1, source_target_pairs={{0,4},{4,0},{8,12},{12,8},{16,20},{20,16},{24,28},{28,24},{1,5},{5... | collective-permute-start | bytes 196616 | tf_op jit(solution)/shard_map/ppermute | solution.py:245
  27.1 2.5 %collective-permute-start.12 = (f32[128,256]{1,0:T(8,128)S(1)}, f32[128,256]{1,0:T(8,128)S(1)}, u32[]{:S(2)}, u32[]{:S(2)}) collective-permute-start(f32[128,256]{1,0:T(8,128)S(1)} %broadcast_select_fusion.2), channel_id=1, source_target_pairs={{0,16},{4,20},{8,24},{12,28},{16,0},{20,4},{24,8},{28,12},{1,17},{... | collective-permute-start | bytes 393224 | tf_op jit(solution)/shard_map/ppermute | solution.py:245
  29.6 1.1 %collective-permute-done.8 = f32[128,128]{1,0:T(8,128)S(1)} collective-permute-done((f32[128,128]{1,0:T(8,128)S(1)}, f32[128,128]{1,0:T(8,128)S(1)}, u32[]{:S(2)}, u32[]{:S(2)}) %collective-permute-start.8) | collective-permute-done | bytes 65568 | tf_op jit(solution)/shard_map/ppermute | solution.py:245
  30.7 2.4 %collective-permute-done.10 = f32[128,256]{1,0:T(8,128)S(1)} collective-permute-done((f32[128,256]{1,0:T(8,128)S(1)}, f32[128,256]{1,0:T(8,128)S(1)}, u32[]{:S(2)}, u32[]{:S(2)}) %collective-permute-start.10) | collective-permute-done | bytes 131104 | tf_op jit(solution)/shard_map/ppermute | solution.py:245
  33.5 6.3 %factor.1 = (f32[128,128]{1,0:T(8,128)}, f32[128,256]{1,0:T(8,128)S(1)}, f32[128,128]{1,0:T(8,128)S(1)}, f32[128,128]{1,0:T(8,128)S(1)}, f32[2048,512]{1,0:T(8,128)S(1)}) custom-call(s32[1]{0:T(128)S(6)} %and.14.odd, f32[128,128]{1,0:T(8,128)S(1)} %add.18.mine, f32[128,128]{1,0:T(8,128)S(1)} %collective-permute-done.9.theirs, f32[2048,512]{1,0:T(8,128)} %trailing.3), custom_call_target="tpu_custom_call" | custom-call | bytes 22000000 | tf_op jit(solution)/shard_map/factor/pallas_call | solution.py:227
  39.9 0.6 %collective-permute-done.11.theirs = f32[128,256]{1,0:T(8,128)S(1)} collective-permute-done((f32[128,256]{1,0:T(8,128)S(1)}, f32[128,256]{1,0:T(8,128)S(1)}, u32[]{:S(2)}, u32[]{:S(2)}) %collective-permute-start.11) | collective-permute-done | bytes 131104 | tf_op jit(solution)/shard_map/ppermute | solution.py:245
  40.4 0.3 mix.1.refs_3_
  40.7 0.9 %collective-permute-start.13 = (f32[128,256]{1,0:T(8,128)S(1)}, f32[128,256]{1,0:T(8,128)S(1)}, u32[]{:S(2)}, u32[]{:S(2)}) collective-permute-start(f32[128,256]{1,0:T(8,128)S(1)} %mix.1.refs_3_), channel_id=1, source_target_pairs={{0,4},{4,0},{8,12},{12,8},{16,20},{20,16},{24,28},{28,24},{1,5},{5... | collective-permute-start | bytes 393224 | tf_op jit(solution)/shard_map/ppermute | solution.py:245
  41.6 3.0 %update.1 = (f32[2048,512]{1,0:T(8,128)}, f32[32,2048]{1,0:T(8,128)}, bf16[128,256]{1,0:T(8,128)(2,1)S(1)}) custom-call(s32[2]{0:T(128)S(1)} %pad_add_fusion.refs_0_.where_ref, bf16[2048,256]{1,0:T(8,128)(2,1)S(1)} %get-tuple-element.36.refs_1_, f32[2048,512]{1,0:T(8,128)S(1)} %get-tuple-element.49.refs_2_, f32[128,256]{1,0:T(8,128)S(1)} %mix.1.refs_3_, ...), custom_call_target="tpu_custom_call" | custom-call | flops 1 | bytes 1 | tf_op jit(solution)/shard_map/update/pallas_call | solution.py:428
  44.7 1.1 %collective-permute-done.13.refs_3_ = f32[128,256]{1,0:T(8,128)S(1)} collective-permute-done((f32[128,256]{1,0:T(8,128)S(1)}, f32[128,256]{1,0:T(8,128)S(1)}, u32[]{:S(2)}, u32[]{:S(2)}) %collective-permute-start.13) | collective-permute-done | bytes 131104 | tf_op jit(solution)/shard_map/ppermute | solution.py:245
  45.8 2.3 %update_rest.1 = f32[2048,512]{1,0:T(8,128)} custom-call(s32[2]{0:T(128)S(1)} %pad_add_fusion.refs_0_.where_ref, bf16[2048,256]{1,0:T(8,128)(2,1)S(1)} %get-tuple-element.36.refs_1_, f32[2048,512]{1,0:T(8,128)S(1)} %get-tuple-element.49.refs_2_, f32[128,256]{1,0:T(8,128)S(1)} %collective-permute-done.13.refs_3_, ...), custom_call_target="tpu_custom_call", output_to_operand_aliasing={{}: (5, {})} | custom-call | flops 1 | bytes 1 | tf_op jit(solution)/shard_map/update_rest/pallas_call | solution.py:428
  (24 shorter events, 0.7 us)
Async XLA Ops:
  0.6 4.1 %collective-permute-start = (f32[32,2048]{1,0:T(8,128)}, f32[32,2048]{1,0:T(8,128)S(1)}, u32[]{:S(2)}, u32[]{:S(2)}) collective-permute-start(f32[32,2048]{1,0:T(8,128)} %bitcast.4), channel_id=1, source_target_pairs={{0,1},{1,0},{2,3},{3,2},{4,5},{5,4},{6,7},{7,6},{8,9},{9,8},{10,11... | collective-permute-start | bytes 786440 | tf_op jit(solution)/shard_map/ppermute | solution.py:245
  1.1 9.7 %collective-permute-start.1 = (f32[32,2048]{1,0:T(8,128)}, f32[32,2048]{1,0:T(8,128)S(1)}, u32[]{:S(2)}, u32[]{:S(2)}) collective-permute-start(f32[32,2048]{1,0:T(8,128)} %bitcast.5), channel_id=1, source_target_pairs={{0,2},{1,3},{2,0},{3,1},{4,6},{5,7},{6,4},{7,5},{8,10},{9,11},{10,... | collective-permute-start | bytes 786440 | tf_op jit(solution)/shard_map/ppermute | solution.py:245
  4.7 6.1 %collective-permute-start.4 = (f32[128,256]{1,0:T(8,128)S(1)}, f32[128,256]{1,0:T(8,128)S(1)}, u32[]{:S(2)}, u32[]{:S(2)}) collective-permute-start(f32[128,256]{1,0:T(8,128)S(1)} %get-tuple-element.40), channel_id=1, source_target_pairs={{0,4},{4,0},{8,12},{12,8},{16,20},{20,16},{24,28},{28,24},{1,5},{5... | collective-permute-start | bytes 393224 | tf_op jit(solution)/shard_map/ppermute | solution.py:245
  6.3 0.9 %copy-start = (f32[2048,32]{0,1:T(8,128)S(1)}, f32[2048,32]{0,1:T(8,128)}, u32[]{:S(2)}) copy-start(f32[2048,32]{0,1:T(8,128)} %param.2) | copy-start | bytes 786436
  10.8 2.0 %collective-permute-start.2 = (f32[32,2048]{1,0:T(8,128)S(1)}, f32[32,2048]{1,0:T(8,128)S(1)}, u32[]{:S(2)}, u32[]{:S(2)}) collective-permute-start(f32[32,2048]{1,0:T(8,128)S(1)} %collective-permute-done.1.refs_2_), channel_id=1, source_target_pairs={{0,1},{1,0},{2,3},{3,2},{4,5},{5,4},{6,7},{7,6},{8,9},{9,8},{10,11... | collective-permute-start | bytes 786440 | tf_op jit(solution)/shard_map/ppermute | solution.py:245
  10.8 9.4 %collective-permute-start.5 = (f32[128,256]{1,0:T(8,128)S(1)}, f32[128,256]{1,0:T(8,128)S(1)}, u32[]{:S(2)}, u32[]{:S(2)}) collective-permute-start(f32[128,256]{1,0:T(8,128)S(1)} %broadcast_select_fusion.1), channel_id=1, source_target_pairs={{0,8},{4,12},{8,0},{12,4},{16,24},{20,28},{24,16},{28,20},{1,9},{5... | collective-permute-start | bytes 393224 | tf_op jit(solution)/shard_map/ppermute | solution.py:245
  14.1 6.1 %collective-permute-start.6 = (f32[128,128]{1,0:T(8,128)S(1)}, f32[128,128]{1,0:T(8,128)S(1)}, u32[]{:S(2)}, u32[]{:S(2)}) collective-permute-start(f32[128,128]{1,0:T(8,128)S(1)} %get-tuple-element.42), channel_id=1, source_target_pairs={{0,8},{4,12},{8,0},{12,4},{16,24},{20,28},{24,16},{28,20},{1,9},{5... | collective-permute-start | bytes 196616 | tf_op jit(solution)/shard_map/ppermute | solution.py:245
  18.6 7.6 %collective-permute-start.3 = (f32[128,256]{1,0:T(8,128)S(1)}, f32[128,256]{1,0:T(8,128)S(1)}, u32[]{:S(2)}, u32[]{:S(2)}) collective-permute-start(f32[128,256]{1,0:T(8,128)S(1)} %get-tuple-element.38), channel_id=1, source_target_pairs={{0,4},{4,0},{8,12},{12,8},{16,20},{20,16},{24,28},{28,24},{1,5},{5... | collective-permute-start | bytes 393224 | tf_op jit(solution)/shard_map/ppermute | solution.py:245
  20.3 5.9 %collective-permute-start.7 = (f32[128,128]{1,0:T(8,128)S(1)}, f32[128,128]{1,0:T(8,128)S(1)}, u32[]{:S(2)}, u32[]{:S(2)}) collective-permute-start(f32[128,128]{1,0:T(8,128)S(1)} %add.16), channel_id=1, source_target_pairs={{0,16},{4,20},{8,24},{12,28},{16,0},{20,4},{24,8},{28,12},{1,17},{... | collective-permute-start | bytes 196616 | tf_op jit(solution)/shard_map/ppermute | solution.py:245
  26.2 7.0 %collective-permute-start.10 = (f32[128,256]{1,0:T(8,128)S(1)}, f32[128,256]{1,0:T(8,128)S(1)}, u32[]{:S(2)}, u32[]{:S(2)}) collective-permute-start(f32[128,256]{1,0:T(8,128)S(1)} %add.15), channel_id=1, source_target_pairs={{0,8},{4,12},{8,0},{12,4},{16,24},{20,28},{24,16},{28,20},{1,9},{5... | collective-permute-start | bytes 393224 | tf_op jit(solution)/shard_map/ppermute | solution.py:245
  26.4 4.3 %collective-permute-start.8 = (f32[128,128]{1,0:T(8,128)S(1)}, f32[128,128]{1,0:T(8,128)S(1)}, u32[]{:S(2)}, u32[]{:S(2)}) collective-permute-start(f32[128,128]{1,0:T(8,128)S(1)} %add.17), channel_id=1, source_target_pairs={{0,4},{4,0},{8,12},{12,8},{16,20},{20,16},{24,28},{28,24},{1,5},{5... | collective-permute-start | bytes 196616 | tf_op jit(solution)/shard_map/ppermute | solution.py:245
  27.1 12.8 %collective-permute-start.12 = (f32[128,256]{1,0:T(8,128)S(1)}, f32[128,256]{1,0:T(8,128)S(1)}, u32[]{:S(2)}, u32[]{:S(2)}) collective-permute-start(f32[128,256]{1,0:T(8,128)S(1)} %broadcast_select_fusion.2), channel_id=1, source_target_pairs={{0,16},{4,20},{8,24},{12,28},{16,0},{20,4},{24,8},{28,12},{1,17},{... | collective-permute-start | bytes 393224 | tf_op jit(solution)/shard_map/ppermute | solution.py:245
  30.7 2.8 %collective-permute-start.9 = (f32[128,128]{1,0:T(8,128)S(1)}, f32[128,128]{1,0:T(8,128)S(1)}, u32[]{:S(2)}, u32[]{:S(2)}) collective-permute-start(f32[128,128]{1,0:T(8,128)S(1)} %add.18.mine), channel_id=1, source_target_pairs={{0,1},{1,0},{2,3},{3,2},{4,5},{5,4},{6,7},{7,6},{8,9},{9,8},{10,11... | collective-permute-start | bytes 196616 | tf_op jit(solution)/shard_map/ppermute | solution.py:245
  33.2 7.2 %collective-permute-start.11 = (f32[128,256]{1,0:T(8,128)S(1)}, f32[128,256]{1,0:T(8,128)S(1)}, u32[]{:S(2)}, u32[]{:S(2)}) collective-permute-start(f32[128,256]{1,0:T(8,128)S(1)} %add.19.mine), channel_id=1, source_target_pairs={{0,16},{4,20},{8,24},{12,28},{16,0},{20,4},{24,8},{28,12},{1,17},{... | collective-permute-start | bytes 393224 | tf_op jit(solution)/shard_map/ppermute | solution.py:245
  40.7 5.0 %collective-permute-start.13 = (f32[128,256]{1,0:T(8,128)S(1)}, f32[128,256]{1,0:T(8,128)S(1)}, u32[]{:S(2)}, u32[]{:S(2)}) collective-permute-start(f32[128,256]{1,0:T(8,128)S(1)} %mix.1.refs_3_), channel_id=1, source_target_pairs={{0,4},{4,0},{8,12},{12,8},{16,20},{20,16},{24,28},{28,24},{1,5},{5... | collective-permute-start | bytes 393224 | tf_op jit(solution)/shard_map/ppermute | solution.py:245

commit v5 on v4

--- a/solution.py
+++ b/solution.py
@@ -7,7 +7,7 @@
 
 SUB = 16
 GROUP = 2
-LAG = 2
+LAG = 1
 HIGHEST, HIGH = lax.Precision.HIGHEST, lax.Precision.HIGH
 MOST = 60 << 20
 MOST = 50 << 20
@@ -126,7 +126,7 @@
                 left = jnp.concatenate([jnp.where(mask, whole[t * SUB : (t + 1) * SUB], 0.0) for t in targets], axis=0)
                 change = times(left, whole)
             else:
-                targets = list(range(slabs))
+                targets = [*range(last, slabs), *range(first, last), *range(first)]
                 left = jnp.concatenate(
                     [
                         jnp.where(mask, lower[rows(t), :] if t in group(s) else whole[t * SUB : (t + 1) * SUB], 0.0)
@@ -135,8 +135,8 @@
                     axis=0,
                 )
                 change = times(left, whole)
-                below = times(left[first * SUB :], upper[...])
-                for i, t in enumerate(range(first, slabs)):
+                below = times(left[: (slabs - first) * SUB], upper[...])
+                for i, t in enumerate(targets[: slabs - first]):
                     part = below[i * SUB : (i + 1) * SUB]
                     lower[rows(t), :] = jnp.where(mask, part, jnp.where(lane < first * SUB, lower[rows(t), :], 0.0))
             for i, t in enumerate(targets):
@@ -184,8 +184,9 @@
     for k in range(slabs + LAG):
         streams, after = [], []
         if 0 <= k - 1 < slabs:
-            streams.append(cholesky_out(k - 1))
-        for name, s, ref in (("g", k, g), ("d", k - LAG, d)):
+            for step in cholesky_out(k - 1):
+                step()
+        for name, s, ref in (("d", k - LAG, d), ("g", k, g)):
             if not 0 <= s < slabs:
                 continue
             if name == "d" and s % GROUP == 0:
@@ -204,8 +205,9 @@
         for step in after:
             step()
     inv_ref[:, :n] = d[...]
-    inv_ref[:, n:] = -times(d[...], weight_ref[...])
-    pivot_ref[...] = times(d[...], lower[...])
+    last_two = times(d[...], jnp.concatenate([weight_ref[...], lower[...]], axis=1))
+    inv_ref[:, n:] = -last_two[:, :n]
+    pivot_ref[...] = last_two[:, n:]
 
 
 def fetching_factor_kernel(odd, mine, theirs, trailing, *refs):

time: 48.2 us -> 48.2 us (level)
  waiting for transfers between devices: 12 us -> 12.8 us
  Pallas kernels: 16.2 us -> 15.5 us
    ppermute x14, waiting for transfers between devices: 12 us -> 12.8 us  [swap(): lax.ppermute(x, axis, [(i, i ^ mask) for i in range(lax.axis_size(axis))])]
    pallas_call x1, Pallas kernels: 6.34 us -> 5.6 us  [factor(): pl.pallas_call(fetching_factor_kernel, out_shape=(out, jax.ShapeDtypeStru...]
  transfers between devices with their start and end apart: 14 -> 14, of which waited for: 6 -> 6; matrix products, arithmetic and copies ran while one was open for 2% -> 2% of each run, Pallas kernels for 29% -> 27%
where the time goes in v5:
time: 48.2 us; the launch traced here: 48 us
  starting transfers between devices  16.8 us (35%)
  Pallas kernels  15.5 us (32%)
  waiting for transfers between devices  12.8 us (27%)
  local copies, waits for them, and re-layouts  1.92 us (4%)
  between operations  0.79 us (2%)
    ppermute x14, starting transfers between devices, swap(): lax.ppermute(x, axis, [(i, i ^ mask) for i in range(lax.axis_size(axis))])  16.8 us
    ppermute x14, waiting for transfers between devices, swap(): lax.ppermute(x, axis, [(i, i ^ mask) for i in range(lax.axis_size(axis))])  12.8 us
    pallas_call x1, Pallas kernels, factor(): pl.pallas_call(fetching_factor_kernel, out_shape=(out, jax.ShapeDtypeStru...  5.6 us
    pallas_call x2, Pallas kernels, update_call(): pl.pallas_call(lambda *refs: update_kernel(pieces, second, *refs), out_sh...  5.26 us
    pallas_call x1, Pallas kernels, products_of(): pl.pallas_call(products_kernel, out_shape=(part, part, jax.ShapeDtypeStru...  3.03 us
    pallas_call x1, Pallas kernels, gram(): pl.pallas_call(lambda *refs: gram_kernel(tuple(held), *refs), out_shape=(...  1.3 us
    slice x1, local copies, waits for them, and re-layouts, per_device(): lead, _ = lax.optimization_barrier((trailing[:n], held[1]))  0.97 us
  transfers between devices with their start and end apart: 14, of which 6 were waited for; matrix products, arithmetic and copies ran while one was open for 2% of the time, Pallas kernels for 27%

profile of v5, /device:TPU:0, one launch (start us, length us, event | category | flops | bytes accessed | tf_op | source)
XLA Modules:
  0.0 48.0 jit_solution(4070330809749419334)
XLA Ops:
  0.6 0.5 %collective-permute-start = (f32[32,2048]{1,0:T(8,128)}, f32[32,2048]{1,0:T(8,128)S(1)}, u32[]{:S(2)}, u32[]{:S(2)}) collective-permute-start(f32[32,2048]{1,0:T(8,128)} %bitcast.4), channel_id=1, source_target_pairs={{0,1},{1,0},{2,3},{3,2},{4,5},{5,4},{6,7},{7,6},{8,9},{9,8},{10,11... | collective-permute-start | bytes 786440 | tf_op jit(solution)/shard_map/ppermute | solution.py:247
  1.1 2.6 %collective-permute-start.1 = (f32[32,2048]{1,0:T(8,128)}, f32[32,2048]{1,0:T(8,128)S(1)}, u32[]{:S(2)}, u32[]{:S(2)}) collective-permute-start(f32[32,2048]{1,0:T(8,128)} %bitcast.5), channel_id=1, source_target_pairs={{0,2},{1,3},{2,0},{3,1},{4,6},{5,7},{6,4},{7,5},{8,10},{9,11},{10,... | collective-permute-start | bytes 786440 | tf_op jit(solution)/shard_map/ppermute | solution.py:247
  3.7 1.0 %slice.10 = f32[128,512]{1,0:T(8,128)S(1)} slice(f32[2048,512]{1,0:T(8,128)} %trailing.3), slice={[0:128], [0:512]} | slice | bytes 524288 | tf_op jit(solution)/shard_map/slice | solution.py:504
  4.7 1.6 %collective-permute-start.4 = (f32[128,256]{1,0:T(8,128)S(1)}, f32[128,256]{1,0:T(8,128)S(1)}, u32[]{:S(2)}, u32[]{:S(2)}) collective-permute-start(f32[128,256]{1,0:T(8,128)S(1)} %get-tuple-element.40), channel_id=1, source_target_pairs={{0,4},{4,0},{8,12},{12,8},{16,20},{20,16},{24,28},{28,24},{1,5},{5... | collective-permute-start | bytes 393224 | tf_op jit(solution)/shard_map/ppermute | solution.py:247
  6.3 0.9 %copy-done = f32[2048,32]{0,1:T(8,128)S(1)} copy-done((f32[2048,32]{0,1:T(8,128)S(1)}, f32[2048,32]{0,1:T(8,128)}, u32[]{:S(2)}) %copy-start) | copy-done | bytes 262168
  7.3 3.5 %collective-permute-done.1.refs_2_ = f32[32,2048]{1,0:T(8,128)S(1)} collective-permute-done((f32[32,2048]{1,0:T(8,128)}, f32[32,2048]{1,0:T(8,128)S(1)}, u32[]{:S(2)}, u32[]{:S(2)}) %collective-permute-start.1) | collective-permute-done | bytes 262176 | tf_op jit(solution)/shard_map/ppermute | solution.py:247
  10.8 1.9 %collective-permute-start.5 = (f32[128,256]{1,0:T(8,128)S(1)}, f32[128,256]{1,0:T(8,128)S(1)}, u32[]{:S(2)}, u32[]{:S(2)}) collective-permute-start(f32[128,256]{1,0:T(8,128)S(1)} %broadcast_select_fusion.1), channel_id=1, source_target_pairs={{0,8},{4,12},{8,0},{12,4},{16,24},{20,28},{24,16},{28,20},{1,9},{5... | collective-permute-start | bytes 393224 | tf_op jit(solution)/shard_map/ppermute | solution.py:247
  12.8 1.3 %gram.1 = (f32[128,2048]{1,0:T(8,128)S(1)}, f32[128,128]{1,0:T(8,128)S(1)}) custom-call(s32[2]{0:T(128)S(1)} %pad_add_fusion.refs_0_.where_ref, f32[32,2048]{1,0:T(8,128)S(1)} %nearby.1.refs_1_, f32[32,2048]{1,0:T(8,128)S(1)} %collective-permute-done.1.refs_2_, f32[32,2048]{1,0:T(8,128)S(1)} %collective-permute-done.refs_3_, ...), custom_call_target="tpu_custom_call" | custom-call | flops 1 | bytes 1 | tf_op jit(solution)/shard_map/gram/pallas_call | solution.py:322
  14.1 1.4 %collective-permute-start.6 = (f32[128,128]{1,0:T(8,128)S(1)}, f32[128,128]{1,0:T(8,128)S(1)}, u32[]{:S(2)}, u32[]{:S(2)}) collective-permute-start(f32[128,128]{1,0:T(8,128)S(1)} %get-tuple-element.42), channel_id=1, source_target_pairs={{0,8},{4,12},{8,0},{12,4},{16,24},{20,28},{24,16},{28,20},{1,9},{5... | collective-permute-start | bytes 196616 | tf_op jit(solution)/shard_map/ppermute | solution.py:247
  15.6 3.0 %products.1 = (f32[128,256]{1,0:T(8,128)S(1)}, f32[128,256]{1,0:T(8,128)S(1)}, bf16[2048,256]{1,0:T(8,128)(2,1)S(1)}) custom-call(s32[2]{0:T(128)S(1)} %pad_add_fusion.refs_0_.where_ref, f32[128,2048]{1,0:T(8,128)S(1)} %get-tuple-element.35.panel_t, f32[2048,512]{1,0:T(8,128)} %trailing.3), custom_call_target="tpu_custom_call" | custom-call | bytes 11000000 | tf_op jit(solution)/shard_map/products/pallas_call | solution.py:365
  18.6 1.6 %collective-permute-start.3 = (f32[128,256]{1,0:T(8,128)S(1)}, f32[128,256]{1,0:T(8,128)S(1)}, u32[]{:S(2)}, u32[]{:S(2)}) collective-permute-start(f32[128,256]{1,0:T(8,128)S(1)} %get-tuple-element.38), channel_id=1, source_target_pairs={{0,4},{4,0},{8,12},{12,8},{16,20},{20,16},{24,28},{28,24},{1,5},{5... | collective-permute-start | bytes 393224 | tf_op jit(solution)/shard_map/ppermute | solution.py:247
  20.3 2.7 %collective-permute-start.7 = (f32[128,128]{1,0:T(8,128)S(1)}, f32[128,128]{1,0:T(8,128)S(1)}, u32[]{:S(2)}, u32[]{:S(2)}) collective-permute-start(f32[128,128]{1,0:T(8,128)S(1)} %add.16), channel_id=1, source_target_pairs={{0,16},{4,20},{8,24},{12,28},{16,0},{20,4},{24,8},{28,12},{1,17},{... | collective-permute-start | bytes 196616 | tf_op jit(solution)/shard_map/ppermute | solution.py:247
  22.9 3.3 %collective-permute-done.7 = f32[128,128]{1,0:T(8,128)S(1)} collective-permute-done((f32[128,128]{1,0:T(8,128)S(1)}, f32[128,128]{1,0:T(8,128)S(1)}, u32[]{:S(2)}, u32[]{:S(2)}) %collective-permute-start.7) | collective-permute-done | bytes 65568 | tf_op jit(solution)/shard_map/ppermute | solution.py:247
  26.4 0.7 %collective-permute-start.8 = (f32[128,128]{1,0:T(8,128)S(1)}, f32[128,128]{1,0:T(8,128)S(1)}, u32[]{:S(2)}, u32[]{:S(2)}) collective-permute-start(f32[128,128]{1,0:T(8,128)S(1)} %add.17), channel_id=1, source_target_pairs={{0,4},{4,0},{8,12},{12,8},{16,20},{20,16},{24,28},{28,24},{1,5},{5... | collective-permute-start | bytes 196616 | tf_op jit(solution)/shard_map/ppermute | solution.py:247
  27.1 2.5 %collective-permute-start.12 = (f32[128,256]{1,0:T(8,128)S(1)}, f32[128,256]{1,0:T(8,128)S(1)}, u32[]{:S(2)}, u32[]{:S(2)}) collective-permute-start(f32[128,256]{1,0:T(8,128)S(1)} %broadcast_select_fusion.2), channel_id=1, source_target_pairs={{0,16},{4,20},{8,24},{12,28},{16,0},{20,4},{24,8},{28,12},{1,17},{... | collective-permute-start | bytes 393224 | tf_op jit(solution)/shard_map/ppermute | solution.py:247
  29.6 1.1 %collective-permute-done.8 = f32[128,128]{1,0:T(8,128)S(1)} collective-permute-done((f32[128,128]{1,0:T(8,128)S(1)}, f32[128,128]{1,0:T(8,128)S(1)}, u32[]{:S(2)}, u32[]{:S(2)}) %collective-permute-start.8) | collective-permute-done | bytes 65568 | tf_op jit(solution)/shard_map/ppermute | solution.py:247
  30.7 2.4 %collective-permute-done.10 = f32[128,256]{1,0:T(8,128)S(1)} collective-permute-done((f32[128,256]{1,0:T(8,128)S(1)}, f32[128,256]{1,0:T(8,128)S(1)}, u32[]{:S(2)}, u32[]{:S(2)}) %collective-permute-start.10) | collective-permute-done | bytes 131104 | tf_op jit(solution)/shard_map/ppermute | solution.py:247
  33.5 5.6 %factor.1 = (f32[128,128]{1,0:T(8,128)}, f32[128,256]{1,0:T(8,128)S(1)}, f32[128,128]{1,0:T(8,128)S(1)}, f32[128,128]{1,0:T(8,128)S(1)}, f32[2048,512]{1,0:T(8,128)S(1)}) custom-call(s32[1]{0:T(128)S(6)} %and.14.odd, f32[128,128]{1,0:T(8,128)S(1)} %add.18.mine, f32[128,128]{1,0:T(8,128)S(1)} %collective-permute-done.9.theirs, f32[2048,512]{1,0:T(8,128)} %trailing.3), custom_call_target="tpu_custom_call" | custom-call | bytes 22000000 | tf_op jit(solution)/shard_map/factor/pallas_call | solution.py:229
  39.1 1.3 %collective-permute-done.11.theirs = f32[128,256]{1,0:T(8,128)S(1)} collective-permute-done((f32[128,256]{1,0:T(8,128)S(1)}, f32[128,256]{1,0:T(8,128)S(1)}, u32[]{:S(2)}, u32[]{:S(2)}) %collective-permute-start.11) | collective-permute-done | bytes 131104 | tf_op jit(solution)/shard_map/ppermute | solution.py:247
  40.4 0.3 mix.1.refs_3_
  40.7 0.9 %collective-permute-start.13 = (f32[128,256]{1,0:T(8,128)S(1)}, f32[128,256]{1,0:T(8,128)S(1)}, u32[]{:S(2)}, u32[]{:S(2)}) collective-permute-start(f32[128,256]{1,0:T(8,128)S(1)} %mix.1.refs_3_), channel_id=1, source_target_pairs={{0,4},{4,0},{8,12},{12,8},{16,20},{20,16},{24,28},{28,24},{1,5},{5... | collective-permute-start | bytes 393224 | tf_op jit(solution)/shard_map/ppermute | solution.py:247
  41.6 3.0 %update.1 = (f32[2048,512]{1,0:T(8,128)}, f32[32,2048]{1,0:T(8,128)}, bf16[128,256]{1,0:T(8,128)(2,1)S(1)}) custom-call(s32[2]{0:T(128)S(1)} %pad_add_fusion.refs_0_.where_ref, bf16[2048,256]{1,0:T(8,128)(2,1)S(1)} %get-tuple-element.36.refs_1_, f32[2048,512]{1,0:T(8,128)S(1)} %get-tuple-element.49.refs_2_, f32[128,256]{1,0:T(8,128)S(1)} %mix.1.refs_3_, ...), custom_call_target="tpu_custom_call" | custom-call | flops 1 | bytes 1 | tf_op jit(solution)/shard_map/update/pallas_call | solution.py:430
  44.7 1.1 %collective-permute-done.13.refs_3_ = f32[128,256]{1,0:T(8,128)S(1)} collective-permute-done((f32[128,256]{1,0:T(8,128)S(1)}, f32[128,256]{1,0:T(8,128)S(1)}, u32[]{:S(2)}, u32[]{:S(2)}) %collective-permute-start.13) | collective-permute-done | bytes 131104 | tf_op jit(solution)/shard_map/ppermute | solution.py:247
  45.8 2.3 %update_rest.1 = f32[2048,512]{1,0:T(8,128)} custom-call(s32[2]{0:T(128)S(1)} %pad_add_fusion.refs_0_.where_ref, bf16[2048,256]{1,0:T(8,128)(2,1)S(1)} %get-tuple-element.36.refs_1_, f32[2048,512]{1,0:T(8,128)S(1)} %get-tuple-element.49.refs_2_, f32[128,256]{1,0:T(8,128)S(1)} %collective-permute-done.13.refs_3_, ...), custom_call_target="tpu_custom_call", output_to_operand_aliasing={{}: (5, {})} | custom-call | flops 1 | bytes 1 | tf_op jit(solution)/shard_map/update_rest/pallas_call | solution.py:430
  (24 shorter events, 0.7 us)
Async XLA Ops:
  0.6 4.1 %collective-permute-start = (f32[32,2048]{1,0:T(8,128)}, f32[32,2048]{1,0:T(8,128)S(1)}, u32[]{:S(2)}, u32[]{:S(2)}) collective-permute-start(f32[32,2048]{1,0:T(8,128)} %bitcast.4), channel_id=1, source_target_pairs={{0,1},{1,0},{2,3},{3,2},{4,5},{5,4},{6,7},{7,6},{8,9},{9,8},{10,11... | collective-permute-start | bytes 786440 | tf_op jit(solution)/shard_map/ppermute | solution.py:247
  1.1 9.7 %collective-permute-start.1 = (f32[32,2048]{1,0:T(8,128)}, f32[32,2048]{1,0:T(8,128)S(1)}, u32[]{:S(2)}, u32[]{:S(2)}) collective-permute-start(f32[32,2048]{1,0:T(8,128)} %bitcast.5), channel_id=1, source_target_pairs={{0,2},{1,3},{2,0},{3,1},{4,6},{5,7},{6,4},{7,5},{8,10},{9,11},{10,... | collective-permute-start | bytes 786440 | tf_op jit(solution)/shard_map/ppermute | solution.py:247
  4.7 6.1 %collective-permute-start.4 = (f32[128,256]{1,0:T(8,128)S(1)}, f32[128,256]{1,0:T(8,128)S(1)}, u32[]{:S(2)}, u32[]{:S(2)}) collective-permute-start(f32[128,256]{1,0:T(8,128)S(1)} %get-tuple-element.40), channel_id=1, source_target_pairs={{0,4},{4,0},{8,12},{12,8},{16,20},{20,16},{24,28},{28,24},{1,5},{5... | collective-permute-start | bytes 393224 | tf_op jit(solution)/shard_map/ppermute | solution.py:247
  6.3 0.9 %copy-start = (f32[2048,32]{0,1:T(8,128)S(1)}, f32[2048,32]{0,1:T(8,128)}, u32[]{:S(2)}) copy-start(f32[2048,32]{0,1:T(8,128)} %param.2) | copy-start | bytes 786436
  10.8 2.0 %collective-permute-start.2 = (f32[32,2048]{1,0:T(8,128)S(1)}, f32[32,2048]{1,0:T(8,128)S(1)}, u32[]{:S(2)}, u32[]{:S(2)}) collective-permute-start(f32[32,2048]{1,0:T(8,128)S(1)} %collective-permute-done.1.refs_2_), channel_id=1, source_target_pairs={{0,1},{1,0},{2,3},{3,2},{4,5},{5,4},{6,7},{7,6},{8,9},{9,8},{10,11... | collective-permute-start | bytes 786440 | tf_op jit(solution)/shard_map/ppermute | solution.py:247
  10.8 9.4 %collective-permute-start.5 = (f32[128,256]{1,0:T(8,128)S(1)}, f32[128,256]{1,0:T(8,128)S(1)}, u32[]{:S(2)}, u32[]{:S(2)}) collective-permute-start(f32[128,256]{1,0:T(8,128)S(1)} %broadcast_select_fusion.1), channel_id=1, source_target_pairs={{0,8},{4,12},{8,0},{12,4},{16,24},{20,28},{24,16},{28,20},{1,9},{5... | collective-permute-start | bytes 393224 | tf_op jit(solution)/shard_map/ppermute | solution.py:247
  14.1 6.1 %collective-permute-start.6 = (f32[128,128]{1,0:T(8,128)S(1)}, f32[128,128]{1,0:T(8,128)S(1)}, u32[]{:S(2)}, u32[]{:S(2)}) collective-permute-start(f32[128,128]{1,0:T(8,128)S(1)} %get-tuple-element.42), channel_id=1, source_target_pairs={{0,8},{4,12},{8,0},{12,4},{16,24},{20,28},{24,16},{28,20},{1,9},{5... | collective-permute-start | bytes 196616 | tf_op jit(solution)/shard_map/ppermute | solution.py:247
  18.6 7.6 %collective-permute-start.3 = (f32[128,256]{1,0:T(8,128)S(1)}, f32[128,256]{1,0:T(8,128)S(1)}, u32[]{:S(2)}, u32[]{:S(2)}) collective-permute-start(f32[128,256]{1,0:T(8,128)S(1)} %get-tuple-element.38), channel_id=1, source_target_pairs={{0,4},{4,0},{8,12},{12,8},{16,20},{20,16},{24,28},{28,24},{1,5},{5... | collective-permute-start | bytes 393224 | tf_op jit(solution)/shard_map/ppermute | solution.py:247
  20.3 5.9 %collective-permute-start.7 = (f32[128,128]{1,0:T(8,128)S(1)}, f32[128,128]{1,0:T(8,128)S(1)}, u32[]{:S(2)}, u32[]{:S(2)}) collective-permute-start(f32[128,128]{1,0:T(8,128)S(1)} %add.16), channel_id=1, source_target_pairs={{0,16},{4,20},{8,24},{12,28},{16,0},{20,4},{24,8},{28,12},{1,17},{... | collective-permute-start | bytes 196616 | tf_op jit(solution)/shard_map/ppermute | solution.py:247
  26.2 7.0 %collective-permute-start.10 = (f32[128,256]{1,0:T(8,128)S(1)}, f32[128,256]{1,0:T(8,128)S(1)}, u32[]{:S(2)}, u32[]{:S(2)}) collective-permute-start(f32[128,256]{1,0:T(8,128)S(1)} %add.15), channel_id=1, source_target_pairs={{0,8},{4,12},{8,0},{12,4},{16,24},{20,28},{24,16},{28,20},{1,9},{5... | collective-permute-start | bytes 393224 | tf_op jit(solution)/shard_map/ppermute | solution.py:247
  26.4 4.3 %collective-permute-start.8 = (f32[128,128]{1,0:T(8,128)S(1)}, f32[128,128]{1,0:T(8,128)S(1)}, u32[]{:S(2)}, u32[]{:S(2)}) collective-permute-start(f32[128,128]{1,0:T(8,128)S(1)} %add.17), channel_id=1, source_target_pairs={{0,4},{4,0},{8,12},{12,8},{16,20},{20,16},{24,28},{28,24},{1,5},{5... | collective-permute-start | bytes 196616 | tf_op jit(solution)/shard_map/ppermute | solution.py:247
  27.1 12.0 %collective-permute-start.12 = (f32[128,256]{1,0:T(8,128)S(1)}, f32[128,256]{1,0:T(8,128)S(1)}, u32[]{:S(2)}, u32[]{:S(2)}) collective-permute-start(f32[128,256]{1,0:T(8,128)S(1)} %broadcast_select_fusion.2), channel_id=1, source_target_pairs={{0,16},{4,20},{8,24},{12,28},{16,0},{20,4},{24,8},{28,12},{1,17},{... | collective-permute-start | bytes 393224 | tf_op jit(solution)/shard_map/ppermute | solution.py:247
  30.7 2.8 %collective-permute-start.9 = (f32[128,128]{1,0:T(8,128)S(1)}, f32[128,128]{1,0:T(8,128)S(1)}, u32[]{:S(2)}, u32[]{:S(2)}) collective-permute-start(f32[128,128]{1,0:T(8,128)S(1)} %add.18.mine), channel_id=1, source_target_pairs={{0,1},{1,0},{2,3},{3,2},{4,5},{5,4},{6,7},{7,6},{8,9},{9,8},{10,11... | collective-permute-start | bytes 196616 | tf_op jit(solution)/shard_map/ppermute | solution.py:247
  33.2 7.2 %collective-permute-start.11 = (f32[128,256]{1,0:T(8,128)S(1)}, f32[128,256]{1,0:T(8,128)S(1)}, u32[]{:S(2)}, u32[]{:S(2)}) collective-permute-start(f32[128,256]{1,0:T(8,128)S(1)} %add.19.mine), channel_id=1, source_target_pairs={{0,16},{4,20},{8,24},{12,28},{16,0},{20,4},{24,8},{28,12},{1,17},{... | collective-permute-start | bytes 393224 | tf_op jit(solution)/shard_map/ppermute | solution.py:247
  40.7 5.0 %collective-permute-start.13 = (f32[128,256]{1,0:T(8,128)S(1)}, f32[128,256]{1,0:T(8,128)S(1)}, u32[]{:S(2)}, u32[]{:S(2)}) collective-permute-start(f32[128,256]{1,0:T(8,128)S(1)} %mix.1.refs_3_), channel_id=1, source_target_pairs={{0,4},{4,0},{8,12},{12,8},{16,20},{20,16},{24,28},{28,24},{1,5},{5... | collective-permute-start | bytes 393224 | tf_op jit(solution)/shard_map/ppermute | solution.py:247

commit v6 on v5

--- a/solution.py
+++ b/solution.py
@@ -499,6 +499,7 @@
         held.update({m | bit: swap(piece, "col", bit) for m, piece in list(held.items()) if m | bit not in held})
     n = own.shape[0] * len(held)
     bits = bits_of("row")
+    mirrored = sum(bits[1:])
     odd, half = row & bits[0] != 0, trailing.shape[1] // 2
 
     lead, _ = lax.optimization_barrier((trailing[:n], held[1]))
@@ -514,7 +515,7 @@
     for bit in bits[1:-1]:
         mine = mine + lax.optimization_barrier((swap(mine, "row", bit), keep))[0]
     lead, mine = lax.optimization_barrier((lead, mine))
-    got_z = swap(mine, "row", bits[-1])
+    got_z = swap(mine, "row", mirrored)
     mine = mine + got_z
     sums, lead, mine = lax.optimization_barrier((keep + got, lead, mine))
     lead_got = swap(lead, "row", bits[-1])
@@ -522,7 +523,7 @@
     for bit in bits[1:-1]:
         sums = sums + swap(sums, "row", bit)
     theirs = swap(mine, "col", 1)
-    last = swap(sums, "row", bits[-1])
+    last = swap(sums, "row", mirrored)
     theirs, sums = lax.optimization_barrier((theirs, sums))
     lead = jnp.where(row & bits[-1] != 0, lead_got, lead)
     odd_col = col.astype(jnp.int32).reshape(1) & 1

time: 48.2 us -> 48.1 us (level)
  waiting for transfers between devices: 12.8 us -> 10.7 us
  starting transfers between devices: 16.8 us -> 18.8 us
    ppermute x14, waiting for transfers between devices: 12.8 us -> 10.7 us  [swap(): lax.ppermute(x, axis, [(i, i ^ mask) for i in range(lax.axis_size(axis))])]
    ppermute x14, starting transfers between devices: 16.8 us -> 18.8 us  [swap(): lax.ppermute(x, axis, [(i, i ^ mask) for i in range(lax.axis_size(axis))])]
where the time goes in v6:
time: 48.1 us; the launch traced here: 47.9 us
  starting transfers between devices  18.8 us (39%)
  Pallas kernels  15.5 us (32%)
  waiting for transfers between devices  10.7 us (22%)
  local copies, waits for them, and re-layouts  1.92 us (4%)
  between operations  0.8 us (2%)
    ppermute x14, starting transfers between devices, swap(): lax.ppermute(x, axis, [(i, i ^ mask) for i in range(lax.axis_size(axis))])  18.8 us
    ppermute x14, waiting for transfers between devices, swap(): lax.ppermute(x, axis, [(i, i ^ mask) for i in range(lax.axis_size(axis))])  10.7 us
    pallas_call x1, Pallas kernels, factor(): pl.pallas_call(fetching_factor_kernel, out_shape=(out, jax.ShapeDtypeStru...  5.6 us
    pallas_call x2, Pallas kernels, update_call(): pl.pallas_call(lambda *refs: update_kernel(pieces, second, *refs), out_sh...  5.26 us
    pallas_call x1, Pallas kernels, products_of(): pl.pallas_call(products_kernel, out_shape=(part, part, jax.ShapeDtypeStru...  3.03 us
    pallas_call x1, Pallas kernels, gram(): pl.pallas_call(lambda *refs: gram_kernel(tuple(held), *refs), out_shape=(...  1.3 us
    slice x1, local copies, waits for them, and re-layouts, per_device(): lead, _ = lax.optimization_barrier((trailing[:n], held[1]))  0.97 us
  transfers between devices with their start and end apart: 14, of which 6 were waited for; matrix products, arithmetic and copies ran while one was open for 2% of the time, Pallas kernels for 27%

profile of v6, /device:TPU:0, one launch (start us, length us, event | category | flops | bytes accessed | tf_op | source)
XLA Modules:
  0.0 47.9 jit_solution(4260027939065608867)
XLA Ops:
  0.6 0.5 %collective-permute-start = (f32[32,2048]{1,0:T(8,128)}, f32[32,2048]{1,0:T(8,128)S(1)}, u32[]{:S(2)}, u32[]{:S(2)}) collective-permute-start(f32[32,2048]{1,0:T(8,128)} %bitcast.4), channel_id=1, source_target_pairs={{0,1},{1,0},{2,3},{3,2},{4,5},{5,4},{6,7},{7,6},{8,9},{9,8},{10,11... | collective-permute-start | bytes 786440 | tf_op jit(solution)/shard_map/ppermute | solution.py:247
  1.1 2.6 %collective-permute-start.1 = (f32[32,2048]{1,0:T(8,128)}, f32[32,2048]{1,0:T(8,128)S(1)}, u32[]{:S(2)}, u32[]{:S(2)}) collective-permute-start(f32[32,2048]{1,0:T(8,128)} %bitcast.5), channel_id=1, source_target_pairs={{0,2},{1,3},{2,0},{3,1},{4,6},{5,7},{6,4},{7,5},{8,10},{9,11},{10,... | collective-permute-start | bytes 786440 | tf_op jit(solution)/shard_map/ppermute | solution.py:247
  3.7 1.0 %slice.10 = f32[128,512]{1,0:T(8,128)S(1)} slice(f32[2048,512]{1,0:T(8,128)} %trailing.3), slice={[0:128], [0:512]} | slice | bytes 524288 | tf_op jit(solution)/shard_map/slice | solution.py:505
  4.7 1.6 %collective-permute-start.4 = (f32[128,256]{1,0:T(8,128)S(1)}, f32[128,256]{1,0:T(8,128)S(1)}, u32[]{:S(2)}, u32[]{:S(2)}) collective-permute-start(f32[128,256]{1,0:T(8,128)S(1)} %get-tuple-element.40), channel_id=1, source_target_pairs={{0,4},{4,0},{8,12},{12,8},{16,20},{20,16},{24,28},{28,24},{1,5},{5... | collective-permute-start | bytes 393224 | tf_op jit(solution)/shard_map/ppermute | solution.py:247
  6.3 0.9 %copy-done = f32[2048,32]{0,1:T(8,128)S(1)} copy-done((f32[2048,32]{0,1:T(8,128)S(1)}, f32[2048,32]{0,1:T(8,128)}, u32[]{:S(2)}) %copy-start) | copy-done | bytes 262168
  7.3 3.5 %collective-permute-done.1.refs_2_ = f32[32,2048]{1,0:T(8,128)S(1)} collective-permute-done((f32[32,2048]{1,0:T(8,128)}, f32[32,2048]{1,0:T(8,128)S(1)}, u32[]{:S(2)}, u32[]{:S(2)}) %collective-permute-start.1) | collective-permute-done | bytes 262176 | tf_op jit(solution)/shard_map/ppermute | solution.py:247
  10.8 1.9 %collective-permute-start.5 = (f32[128,256]{1,0:T(8,128)S(1)}, f32[128,256]{1,0:T(8,128)S(1)}, u32[]{:S(2)}, u32[]{:S(2)}) collective-permute-start(f32[128,256]{1,0:T(8,128)S(1)} %broadcast_select_fusion.1), channel_id=1, source_target_pairs={{0,8},{4,12},{8,0},{12,4},{16,24},{20,28},{24,16},{28,20},{1,9},{5... | collective-permute-start | bytes 393224 | tf_op jit(solution)/shard_map/ppermute | solution.py:247
  12.8 1.3 %gram.1 = (f32[128,2048]{1,0:T(8,128)S(1)}, f32[128,128]{1,0:T(8,128)S(1)}) custom-call(s32[2]{0:T(128)S(1)} %pad_add_fusion.refs_0_.where_ref, f32[32,2048]{1,0:T(8,128)S(1)} %nearby.1.refs_1_, f32[32,2048]{1,0:T(8,128)S(1)} %collective-permute-done.1.refs_2_, f32[32,2048]{1,0:T(8,128)S(1)} %collective-permute-done.refs_3_, ...), custom_call_target="tpu_custom_call" | custom-call | flops 1 | bytes 1 | tf_op jit(solution)/shard_map/gram/pallas_call | solution.py:322
  14.1 1.4 %collective-permute-start.6 = (f32[128,128]{1,0:T(8,128)S(1)}, f32[128,128]{1,0:T(8,128)S(1)}, u32[]{:S(2)}, u32[]{:S(2)}) collective-permute-start(f32[128,128]{1,0:T(8,128)S(1)} %get-tuple-element.42), channel_id=1, source_target_pairs={{0,8},{4,12},{8,0},{12,4},{16,24},{20,28},{24,16},{28,20},{1,9},{5... | collective-permute-start | bytes 196616 | tf_op jit(solution)/shard_map/ppermute | solution.py:247
  15.6 3.0 %products.1 = (f32[128,256]{1,0:T(8,128)S(1)}, f32[128,256]{1,0:T(8,128)S(1)}, bf16[2048,256]{1,0:T(8,128)(2,1)S(1)}) custom-call(s32[2]{0:T(128)S(1)} %pad_add_fusion.refs_0_.where_ref, f32[128,2048]{1,0:T(8,128)S(1)} %get-tuple-element.35.panel_t, f32[2048,512]{1,0:T(8,128)} %trailing.3), custom_call_target="tpu_custom_call" | custom-call | bytes 11000000 | tf_op jit(solution)/shard_map/products/pallas_call | solution.py:365
  18.6 1.6 %collective-permute-start.3 = (f32[128,256]{1,0:T(8,128)S(1)}, f32[128,256]{1,0:T(8,128)S(1)}, u32[]{:S(2)}, u32[]{:S(2)}) collective-permute-start(f32[128,256]{1,0:T(8,128)S(1)} %get-tuple-element.38), channel_id=1, source_target_pairs={{0,4},{4,0},{8,12},{12,8},{16,20},{20,16},{24,28},{28,24},{1,5},{5... | collective-permute-start | bytes 393224 | tf_op jit(solution)/shard_map/ppermute | solution.py:247
  20.3 2.8 %collective-permute-start.7 = (f32[128,128]{1,0:T(8,128)S(1)}, f32[128,128]{1,0:T(8,128)S(1)}, u32[]{:S(2)}, u32[]{:S(2)}) collective-permute-start(f32[128,128]{1,0:T(8,128)S(1)} %add.16), channel_id=1, source_target_pairs={{0,24},{4,28},{8,16},{12,20},{16,8},{20,12},{24,0},{28,4},{1,25},{... | collective-permute-start | bytes 196616 | tf_op jit(solution)/shard_map/ppermute | solution.py:247
  23.0 3.4 %collective-permute-done.7 = f32[128,128]{1,0:T(8,128)S(1)} collective-permute-done((f32[128,128]{1,0:T(8,128)S(1)}, f32[128,128]{1,0:T(8,128)S(1)}, u32[]{:S(2)}, u32[]{:S(2)}) %collective-permute-start.7) | collective-permute-done | bytes 65568 | tf_op jit(solution)/shard_map/ppermute | solution.py:247
  26.5 0.6 %collective-permute-start.8 = (f32[128,128]{1,0:T(8,128)S(1)}, f32[128,128]{1,0:T(8,128)S(1)}, u32[]{:S(2)}, u32[]{:S(2)}) collective-permute-start(f32[128,128]{1,0:T(8,128)S(1)} %add.17), channel_id=1, source_target_pairs={{0,4},{4,0},{8,12},{12,8},{16,20},{20,16},{24,28},{28,24},{1,5},{5... | collective-permute-start | bytes 196616 | tf_op jit(solution)/shard_map/ppermute | solution.py:247
  27.1 3.7 %collective-permute-start.12 = (f32[128,256]{1,0:T(8,128)S(1)}, f32[128,256]{1,0:T(8,128)S(1)}, u32[]{:S(2)}, u32[]{:S(2)}) collective-permute-start(f32[128,256]{1,0:T(8,128)S(1)} %broadcast_select_fusion.2), channel_id=1, source_target_pairs={{0,16},{4,20},{8,24},{12,28},{16,0},{20,4},{24,8},{28,12},{1,17},{... | collective-permute-start | bytes 393224 | tf_op jit(solution)/shard_map/ppermute | solution.py:247
  30.9 2.4 %collective-permute-done.10 = f32[128,256]{1,0:T(8,128)S(1)} collective-permute-done((f32[128,256]{1,0:T(8,128)S(1)}, f32[128,256]{1,0:T(8,128)S(1)}, u32[]{:S(2)}, u32[]{:S(2)}) %collective-permute-start.10) | collective-permute-done | bytes 131104 | tf_op jit(solution)/shard_map/ppermute | solution.py:247
  33.4 1.2 %collective-permute-start.11 = (f32[128,256]{1,0:T(8,128)S(1)}, f32[128,256]{1,0:T(8,128)S(1)}, u32[]{:S(2)}, u32[]{:S(2)}) collective-permute-start(f32[128,256]{1,0:T(8,128)S(1)} %add.19.mine), channel_id=1, source_target_pairs={{0,24},{4,28},{8,16},{12,20},{16,8},{20,12},{24,0},{28,4},{1,25},{... | collective-permute-start | bytes 393224 | tf_op jit(solution)/shard_map/ppermute | solution.py:247
  34.6 5.6 %factor.1 = (f32[128,128]{1,0:T(8,128)}, f32[128,256]{1,0:T(8,128)S(1)}, f32[128,128]{1,0:T(8,128)S(1)}, f32[128,128]{1,0:T(8,128)S(1)}, f32[2048,512]{1,0:T(8,128)S(1)}) custom-call(s32[1]{0:T(128)S(6)} %and.14.odd, f32[128,128]{1,0:T(8,128)S(1)} %add.18.mine, f32[128,128]{1,0:T(8,128)S(1)} %collective-permute-done.9.theirs, f32[2048,512]{1,0:T(8,128)} %trailing.3), custom_call_target="tpu_custom_call" | custom-call | bytes 22000000 | tf_op jit(solution)/shard_map/factor/pallas_call | solution.py:229
  40.2 0.1 collective-permute-done.11.theirs
  40.3 0.3 mix.1.refs_3_
  40.6 0.9 %collective-permute-start.13 = (f32[128,256]{1,0:T(8,128)S(1)}, f32[128,256]{1,0:T(8,128)S(1)}, u32[]{:S(2)}, u32[]{:S(2)}) collective-permute-start(f32[128,256]{1,0:T(8,128)S(1)} %mix.1.refs_3_), channel_id=1, source_target_pairs={{0,4},{4,0},{8,12},{12,8},{16,20},{20,16},{24,28},{28,24},{1,5},{5... | collective-permute-start | bytes 393224 | tf_op jit(solution)/shard_map/ppermute | solution.py:247
  41.4 3.0 %update.1 = (f32[2048,512]{1,0:T(8,128)}, f32[32,2048]{1,0:T(8,128)}, bf16[128,256]{1,0:T(8,128)(2,1)S(1)}) custom-call(s32[2]{0:T(128)S(1)} %pad_add_fusion.refs_0_.where_ref, bf16[2048,256]{1,0:T(8,128)(2,1)S(1)} %get-tuple-element.36.refs_1_, f32[2048,512]{1,0:T(8,128)S(1)} %get-tuple-element.49.refs_2_, f32[128,256]{1,0:T(8,128)S(1)} %mix.1.refs_3_, ...), custom_call_target="tpu_custom_call" | custom-call | flops 1 | bytes 1 | tf_op jit(solution)/shard_map/update/pallas_call | solution.py:430
  44.4 1.2 %collective-permute-done.13.refs_3_ = f32[128,256]{1,0:T(8,128)S(1)} collective-permute-done((f32[128,256]{1,0:T(8,128)S(1)}, f32[128,256]{1,0:T(8,128)S(1)}, u32[]{:S(2)}, u32[]{:S(2)}) %collective-permute-start.13) | collective-permute-done | bytes 131104 | tf_op jit(solution)/shard_map/ppermute | solution.py:247
  45.6 2.3 %update_rest.1 = f32[2048,512]{1,0:T(8,128)} custom-call(s32[2]{0:T(128)S(1)} %pad_add_fusion.refs_0_.where_ref, bf16[2048,256]{1,0:T(8,128)(2,1)S(1)} %get-tuple-element.36.refs_1_, f32[2048,512]{1,0:T(8,128)S(1)} %get-tuple-element.49.refs_2_, f32[128,256]{1,0:T(8,128)S(1)} %collective-permute-done.13.refs_3_, ...), custom_call_target="tpu_custom_call", output_to_operand_aliasing={{}: (5, {})} | custom-call | flops 1 | bytes 1 | tf_op jit(solution)/shard_map/update_rest/pallas_call | solution.py:430
  (24 shorter events, 0.5 us)
Async XLA Ops:
  0.6 4.1 %collective-permute-start = (f32[32,2048]{1,0:T(8,128)}, f32[32,2048]{1,0:T(8,128)S(1)}, u32[]{:S(2)}, u32[]{:S(2)}) collective-permute-start(f32[32,2048]{1,0:T(8,128)} %bitcast.4), channel_id=1, source_target_pairs={{0,1},{1,0},{2,3},{3,2},{4,5},{5,4},{6,7},{7,6},{8,9},{9,8},{10,11... | collective-permute-start | bytes 786440 | tf_op jit(solution)/shard_map/ppermute | solution.py:247
  1.1 9.7 %collective-permute-start.1 = (f32[32,2048]{1,0:T(8,128)}, f32[32,2048]{1,0:T(8,128)S(1)}, u32[]{:S(2)}, u32[]{:S(2)}) collective-permute-start(f32[32,2048]{1,0:T(8,128)} %bitcast.5), channel_id=1, source_target_pairs={{0,2},{1,3},{2,0},{3,1},{4,6},{5,7},{6,4},{7,5},{8,10},{9,11},{10,... | collective-permute-start | bytes 786440 | tf_op jit(solution)/shard_map/ppermute | solution.py:247
  4.7 6.1 %collective-permute-start.4 = (f32[128,256]{1,0:T(8,128)S(1)}, f32[128,256]{1,0:T(8,128)S(1)}, u32[]{:S(2)}, u32[]{:S(2)}) collective-permute-start(f32[128,256]{1,0:T(8,128)S(1)} %get-tuple-element.40), channel_id=1, source_target_pairs={{0,4},{4,0},{8,12},{12,8},{16,20},{20,16},{24,28},{28,24},{1,5},{5... | collective-permute-start | bytes 393224 | tf_op jit(solution)/shard_map/ppermute | solution.py:247
  6.3 0.9 %copy-start = (f32[2048,32]{0,1:T(8,128)S(1)}, f32[2048,32]{0,1:T(8,128)}, u32[]{:S(2)}) copy-start(f32[2048,32]{0,1:T(8,128)} %param.2) | copy-start | bytes 786436
  10.8 2.0 %collective-permute-start.2 = (f32[32,2048]{1,0:T(8,128)S(1)}, f32[32,2048]{1,0:T(8,128)S(1)}, u32[]{:S(2)}, u32[]{:S(2)}) collective-permute-start(f32[32,2048]{1,0:T(8,128)S(1)} %collective-permute-done.1.refs_2_), channel_id=1, source_target_pairs={{0,1},{1,0},{2,3},{3,2},{4,5},{5,4},{6,7},{7,6},{8,9},{9,8},{10,11... | collective-permute-start | bytes 786440 | tf_op jit(solution)/shard_map/ppermute | solution.py:247
  10.8 9.4 %collective-permute-start.5 = (f32[128,256]{1,0:T(8,128)S(1)}, f32[128,256]{1,0:T(8,128)S(1)}, u32[]{:S(2)}, u32[]{:S(2)}) collective-permute-start(f32[128,256]{1,0:T(8,128)S(1)} %broadcast_select_fusion.1), channel_id=1, source_target_pairs={{0,8},{4,12},{8,0},{12,4},{16,24},{20,28},{24,16},{28,20},{1,9},{5... | collective-permute-start | bytes 393224 | tf_op jit(solution)/shard_map/ppermute | solution.py:247
  14.1 6.1 %collective-permute-start.6 = (f32[128,128]{1,0:T(8,128)S(1)}, f32[128,128]{1,0:T(8,128)S(1)}, u32[]{:S(2)}, u32[]{:S(2)}) collective-permute-start(f32[128,128]{1,0:T(8,128)S(1)} %get-tuple-element.42), channel_id=1, source_target_pairs={{0,8},{4,12},{8,0},{12,4},{16,24},{20,28},{24,16},{28,20},{1,9},{5... | collective-permute-start | bytes 196616 | tf_op jit(solution)/shard_map/ppermute | solution.py:247
  18.6 7.8 %collective-permute-start.3 = (f32[128,256]{1,0:T(8,128)S(1)}, f32[128,256]{1,0:T(8,128)S(1)}, u32[]{:S(2)}, u32[]{:S(2)}) collective-permute-start(f32[128,256]{1,0:T(8,128)S(1)} %get-tuple-element.38), channel_id=1, source_target_pairs={{0,4},{4,0},{8,12},{12,8},{16,20},{20,16},{24,28},{28,24},{1,5},{5... | collective-permute-start | bytes 393224 | tf_op jit(solution)/shard_map/ppermute | solution.py:247
  20.3 6.1 %collective-permute-start.7 = (f32[128,128]{1,0:T(8,128)S(1)}, f32[128,128]{1,0:T(8,128)S(1)}, u32[]{:S(2)}, u32[]{:S(2)}) collective-permute-start(f32[128,128]{1,0:T(8,128)S(1)} %add.16), channel_id=1, source_target_pairs={{0,24},{4,28},{8,16},{12,20},{16,8},{20,12},{24,0},{28,4},{1,25},{... | collective-permute-start | bytes 196616 | tf_op jit(solution)/shard_map/ppermute | solution.py:247
  26.4 6.9 %collective-permute-start.10 = (f32[128,256]{1,0:T(8,128)S(1)}, f32[128,256]{1,0:T(8,128)S(1)}, u32[]{:S(2)}, u32[]{:S(2)}) collective-permute-start(f32[128,256]{1,0:T(8,128)S(1)} %add.15), channel_id=1, source_target_pairs={{0,8},{4,12},{8,0},{12,4},{16,24},{20,28},{24,16},{28,20},{1,9},{5... | collective-permute-start | bytes 393224 | tf_op jit(solution)/shard_map/ppermute | solution.py:247
  26.5 4.3 %collective-permute-start.8 = (f32[128,128]{1,0:T(8,128)S(1)}, f32[128,128]{1,0:T(8,128)S(1)}, u32[]{:S(2)}, u32[]{:S(2)}) collective-permute-start(f32[128,128]{1,0:T(8,128)S(1)} %add.17), channel_id=1, source_target_pairs={{0,4},{4,0},{8,12},{12,8},{16,20},{20,16},{24,28},{28,24},{1,5},{5... | collective-permute-start | bytes 196616 | tf_op jit(solution)/shard_map/ppermute | solution.py:247
  27.1 13.1 %collective-permute-start.12 = (f32[128,256]{1,0:T(8,128)S(1)}, f32[128,256]{1,0:T(8,128)S(1)}, u32[]{:S(2)}, u32[]{:S(2)}) collective-permute-start(f32[128,256]{1,0:T(8,128)S(1)} %broadcast_select_fusion.2), channel_id=1, source_target_pairs={{0,16},{4,20},{8,24},{12,28},{16,0},{20,4},{24,8},{28,12},{1,17},{... | collective-permute-start | bytes 393224 | tf_op jit(solution)/shard_map/ppermute | solution.py:247
  30.9 3.7 %collective-permute-start.9 = (f32[128,128]{1,0:T(8,128)S(1)}, f32[128,128]{1,0:T(8,128)S(1)}, u32[]{:S(2)}, u32[]{:S(2)}) collective-permute-start(f32[128,128]{1,0:T(8,128)S(1)} %add.18.mine), channel_id=1, source_target_pairs={{0,1},{1,0},{2,3},{3,2},{4,5},{5,4},{6,7},{7,6},{8,9},{9,8},{10,11... | collective-permute-start | bytes 196616 | tf_op jit(solution)/shard_map/ppermute | solution.py:247
  33.4 6.9 %collective-permute-start.11 = (f32[128,256]{1,0:T(8,128)S(1)}, f32[128,256]{1,0:T(8,128)S(1)}, u32[]{:S(2)}, u32[]{:S(2)}) collective-permute-start(f32[128,256]{1,0:T(8,128)S(1)} %add.19.mine), channel_id=1, source_target_pairs={{0,24},{4,28},{8,16},{12,20},{16,8},{20,12},{24,0},{28,4},{1,25},{... | collective-permute-start | bytes 393224 | tf_op jit(solution)/shard_map/ppermute | solution.py:247
  40.6 5.0 %collective-permute-start.13 = (f32[128,256]{1,0:T(8,128)S(1)}, f32[128,256]{1,0:T(8,128)S(1)}, u32[]{:S(2)}, u32[]{:S(2)}) collective-permute-start(f32[128,256]{1,0:T(8,128)S(1)} %mix.1.refs_3_), channel_id=1, source_target_pairs={{0,4},{4,0},{8,12},{12,8},{16,20},{20,16},{24,28},{28,24},{1,5},{5... | collective-permute-start | bytes 393224 | tf_op jit(solution)/shard_map/ppermute | solution.py:247
